TPU v7x, 512 devices: a whole 4x8x8 slice. The times are simulated.
512 devices in a mesh: exp: 8 (over x, y_hi), tp: 64 (over y_lo, z, core).
Axes of the slice: x: 4, y: 8 (y_hi: 2, y_lo: 4; y = y_hi * 4 + y_lo), z: 8, core: 2. Of those that a mesh axis runs over, the one named last changes fastest.
Arguments:
- hidden_state: bfloat16 [1024, 6144], P('exp', 'tp')
- norm_gain: bfloat16 [6144], P('tp'), may hold values from 0.099609375 to 1.8984375
- routes: int32 [1024, 2], P('exp'), may hold values from 0 to 7, all different within a row; in each aligned block of 128 rows (0 to 127, 128 to 255, ...) at most 64 rows name the same one
- gates: float32 [1024, 2], P('exp'), may hold values from 0.2 to 1
- w_gate: bfloat16 [8, 6144, 8192], P('exp', None, 'tp'), may hold values from -0.078125 to 0.078125
- w_up: bfloat16 [8, 6144, 8192], P('exp', None, 'tp'), may hold values from -0.078125 to 0.078125
- w_down: bfloat16 [8, 8192, 6144], P('exp', None, 'tp'), may hold values from -0.0625 to 0.0625
Outputs:
- mixed: bfloat16 [1024, 6144], P('exp', 'tp')
Inputs may be any that keep to these rules, and one draw needn't show every extreme that they name: `routes`: the two experts of a row differ. Among the rows of one index of exp, no expert is named by more than 64 rows, a bound that some block reaches.
All inputs are finite; a program needn't handle non-finite values.
Results may differ from a plain program's by a relative error of at most 0.0071.
Values may be sent and summed in bfloat16 or wider, within the bound.
No kernel may reach another device: no remote copies, remote signals or barrier semaphores. Data moves between devices by JAX's collectives and lax.ppermute only.
A program may use at most 64 MiB of HBM per device.

v0:
```python
import jax
import jax.numpy as jnp
from jax import lax
from jax.sharding import PartitionSpec as P

D = 6144


def pair_targets(routes, experts, capacity):
    flat_routes = routes.reshape(-1)
    onehot = (flat_routes[:, None] == jnp.arange(experts, dtype=jnp.int32)[None, :]).astype(
        jnp.int32
    )
    before = jnp.cumsum(onehot, axis=0) - onehot
    slots = jnp.sum(before * onehot, axis=1)
    return (flat_routes * capacity + slots).reshape(routes.shape)


def place_rows(targets, rows_in, total_slots):
    slot_ids = jnp.arange(total_slots, dtype=jnp.int32)
    placer = jnp.any(slot_ids[:, None, None] == targets[None, :, :], axis=2).astype(jnp.bfloat16)
    return jnp.dot(placer, rows_in, preferred_element_type=jnp.float32).astype(jnp.bfloat16)


def per_device(hidden_state, norm_gain, routes, gates, w_gate, w_up, w_down):
    experts = lax.axis_size("exp")
    row_count = hidden_state.shape[0]
    capacity = min(row_count, 4 * row_count // experts)
    total_slots = experts * capacity
    targets = pair_targets(routes, experts, capacity)
    gate_rows = w_gate[0]
    up_rows = w_up[0]
    down_rows = w_down[0]
    gain_local = norm_gain.astype(jnp.float32)[None, :]
    values = hidden_state.astype(jnp.float32)
    squares = lax.psum(jnp.sum(values * values, axis=1), "tp")
    inv_rms = lax.rsqrt(squares / D + 1e-05)
    normed = (values * inv_rms[:, None] * gain_local).astype(jnp.bfloat16)
    outgoing = place_rows(targets, normed, total_slots).reshape(experts, capacity, normed.shape[1])
    incoming = lax.all_to_all(outgoing, "exp", split_axis=0, concat_axis=0, tiled=True)
    incoming = incoming.reshape(total_slots, normed.shape[1])
    piece = lax.all_gather(incoming, "tp", axis=1, tiled=True)
    gate = jnp.dot(piece, gate_rows, preferred_element_type=jnp.float32)
    up = jnp.dot(piece, up_rows, preferred_element_type=jnp.float32)
    act = (jax.nn.silu(gate) * up).astype(jnp.bfloat16)
    expert_out = jnp.dot(
        lax.all_gather(act, "tp", axis=1, tiled=True), down_rows, preferred_element_type=jnp.float32
    ).astype(jnp.bfloat16)
    expert_out = expert_out.reshape(experts, capacity, down_rows.shape[1])
    back = lax.all_to_all(expert_out, "exp", split_axis=0, concat_axis=0, tiled=True)
    back = back.reshape(total_slots, down_rows.shape[1])
    picked = back[targets].astype(jnp.float32)
    mixed = jnp.sum(gates[:, :, None] * picked, axis=1)
    return mixed.astype(jnp.bfloat16)


def solution(mesh):
    in_specs = (
        P("exp", "tp"),
        P("tp"),
        P("exp", None),
        P("exp", None),
        P("exp", None, "tp"),
        P("exp", None, "tp"),
        P("exp", None, "tp"),
    )
    out_specs = P("exp", "tp")
    return jax.shard_map(
        per_device, mesh=mesh, in_specs=in_specs, out_specs=out_specs, check_vma=False
    )
```

profile of v0, /device:TPU:1, one launch (start us, length us, event | category | flops | bytes accessed | tf_op | source)
XLA Modules:
  0.0 464.7 jit_solution(16885456730432442961)
XLA Ops:
  6.5 0.9 copy.38
  7.6 0.1 eq.39
  7.7 0.6 reduce-window.6
  8.3 0.2 slice_reduce_fusion
  8.7 0.1 reduce_sum.30
  8.9 0.7 compare_select_fusion
  9.7 0.8 fusion.17
  10.4 140.8 %psum.7 = f32[128]{0:T(128)S(1)} all-reduce(f32[128]{0:T(128)S(1)} %fusion.17), channel_id=1, replica_groups=mesh['exp'=8,'tp'=64] {'tp'}, use_global_device_ids=true, to_apply=%region_5.6 | all-reduce | flops 128 | bytes 1024 | tf_op jit(solution)/shard_map/psum | solution.py:36
  151.3 0.7 convert_element_type.35
  151.9 0.9 convolution_convert_fusion
  153.0 15.8 %all_to_all.10 = bf16[8,64,96]{2,1,0:T(8,128)(2,1)S(1)} all-to-all(bf16[8,64,96]{2,1,0:T(8,128)(2,1)S(1)} %bitcast.34), channel_id=1, replica_groups=mesh['exp'=8,'tp'=64] {'exp'}, dimensions={0} | all-to-all | bytes 196608 | tf_op jit(solution)/shard_map/all_to_all | solution.py:40
  168.9 0.7 copy.42
  169.7 117.9 %all-gather.3.cloned.1.call-done = bf16[512,6144]{0,1:T(8,128)(2,1)} async-done(((bf16[512,96]{0,1:T(8,128)(2,1)}), bf16[512,6144]{0,1:T(8,128)(2,1)}) %all-gather.3.cloned.1.call-update) | async-done | bytes 6291472 | tf_op jit(solution)/shard_map/all_gather | solution.py:42
  287.6 4.8 %fusion.4 = f32[512,128]{1,0:T(8,128)S(1)} fusion(bf16[512,6144]{0,1:T(8,128)(2,1)} %all-gather.3.cloned.1.call-done, bf16[1,6144,128]{2,1,0:T(8,128)(2,1)S(1)} %copy-done), kind=kOutput, calls=%fused_computation.5 | convolution fusion | flops 805306368 | bytes 8126464 | tf_op jit(solution)/shard_map/dot_general | solution.py:43
  292.4 4.1 fusion.9
  296.5 135.3 %all-gather.5.cloned.1.call-done = bf16[512,8192]{1,0:T(8,128)(2,1)} async-done(((bf16[512,128]{1,0:T(8,128)(2,1)}), bf16[512,8192]{1,0:T(8,128)(2,1)}) %all-gather.5.cloned.1.call-update) | async-done | bytes 8388624 | tf_op jit(solution)/shard_map/all_gather | solution.py:47
  431.7 6.1 %fusion.12 = bf16[512,96]{0,1:T(8,128)(2,1)S(1)} fusion(bf16[512,8192]{1,0:T(8,128)(2,1)} %all-gather.5.cloned.1.call-done, bf16[1,8192,96]{1,2,0:T(8,128)(2,1)S(1)} %copy-done.1), kind=kOutput, calls=%fused_computation.9 | convolution fusion | flops 805355520 | bytes 10059776 | tf_op jit(solution)/shard_map/dot_general | solution.py:46
  437.9 0.7 copy.43
  438.6 7.9 %all-to-all-start.1 = ((bf16[8,64,96]{2,1,0:T(8,128)(2,1)}), bf16[8,64,96]{2,1,0:T(8,128)(2,1)S(1)}, u32[]{:S(2)}, u32[]{:S(2)}) async-start(bf16[8,64,96]{2,1,0:T(8,128)(2,1)} %bitcast.7), calls=%async_computation.1 | async-start | bytes 262144 | tf_op jit(solution)/shard_map/all_to_all | solution.py:50
  446.6 0.1 reshape.48
  446.9 9.2 %all-to-all-done.1 = bf16[8,64,96]{2,1,0:T(8,128)(2,1)S(1)} async-done(((bf16[8,64,96]{2,1,0:T(8,128)(2,1)}), bf16[8,64,96]{2,1,0:T(8,128)(2,1)S(1)}, u32[]{:S(2)}, u32[]{:S(2)}) %all-to-all-start.1) | async-done | bytes 98336 | tf_op jit(solution)/shard_map/all_to_all | solution.py:50
  456.1 0.9 gather_fusion
  456.9 0.3 fusion.16
  457.2 0.7 copy.45
  (24 shorter events, 0.9 us)
Async XLA Ops:
  6.5 281.0 %copy-start = (bf16[1,6144,128]{2,1,0:T(8,128)(2,1)S(1)}, bf16[1,6144,128]{2,1,0:T(8,128)(2,1)}, u32[]{:S(2)}) copy-start(bf16[1,6144,128]{2,1,0:T(8,128)(2,1)} %param.11) | copy-start | bytes 4718596
  6.5 281.0 %all-gather.3.cloned.1.call-start = ((), (), s32[]{:S(2)}) async-start(), calls=%async_computation.2 | async-start | bytes 6389760 | tf_op jit(solution)/shard_map/all_gather | solution.py:42
  169.6 262.1 %all-gather.5.cloned.1.call-start = ((), (), s32[]{:S(2)}) async-start(), calls=%async_computation.3 | async-start | bytes 8519680 | tf_op jit(solution)/shard_map/all_gather | solution.py:47
  287.6 4.8 %copy-start.3 = (bf16[512,6144]{0,1:T(8,128)(2,1)S(1)}, bf16[512,6144]{0,1:T(8,128)(2,1)}, u32[]{:S(2)}) copy-start(bf16[512,6144]{0,1:T(8,128)(2,1)} %all-gather.3.cloned.1.call-done) | copy-start | bytes 18874372
  292.4 139.4 %copy-start.1 = (bf16[1,8192,96]{1,2,0:T(8,128)(2,1)S(1)}, bf16[1,8192,96]{1,2,0:T(8,128)(2,1)}, u32[]{:S(2)}) copy-start(bf16[1,8192,96]{1,2,0:T(8,128)(2,1)} %param.13) | copy-start | bytes 4718596
  296.4 150.3 %copy-start.2 = (f32[128,2]{0,1:T(2,128)S(1)}, f32[128,2]{0,1:T(2,128)}, u32[]{:S(2)}) copy-start(f32[128,2]{0,1:T(2,128)} %param.10) | copy-start | bytes 3076
  438.6 17.5 %all-to-all-start.1 = ((bf16[8,64,96]{2,1,0:T(8,128)(2,1)}), bf16[8,64,96]{2,1,0:T(8,128)(2,1)S(1)}, u32[]{:S(2)}, u32[]{:S(2)}) async-start(bf16[8,64,96]{2,1,0:T(8,128)(2,1)} %bitcast.7), calls=%async_computation.1 | async-start | bytes 262144 | tf_op jit(solution)/shard_map/all_to_all | solution.py:50
Sparse Core Ops, SparseCore 0:
  169.7 117.8 all-gather.2
  296.6 135.1 all-gather.4
where the time goes:
time: 466 us; the launch traced here: 465 us
  waiting for transfers between devices  262 us (56%)
  blocking collectives  157 us (34%)
  matrix products  15.9 us (3%)
  between operations  13.5 us (3%)
  starting transfers between devices  7.95 us (2%)
  local copies, waits for them, and re-layouts  5.15 us (1%)
    psum x1, blocking collectives, per_device(): squares = lax.psum(jnp.sum(values * values, axis=1), 'tp')  141 us
    all_gather x1, waiting for transfers between devices, per_device(): lax.all_gather(act, 'tp', axis=1, tiled=True)  135 us
    all_gather x1, waiting for transfers between devices, per_device(): piece = lax.all_gather(incoming, 'tp', axis=1, tiled=True)  118 us
    all_to_all x1, blocking collectives, per_device(): lax.all_to_all(outgoing, 'exp', split_axis=0, concat_axis=0, tiled=True)  15.8 us
  transfers between devices with their start and end apart: 3, of which 3 were waited for; matrix products, arithmetic and copies ran while one was open for 0% of the time, Pallas kernels for 0%

commit v1 on v0

v1 whole, which is shorter than its diff:
```python
import jax
import jax.numpy as jnp
from jax import lax
from jax.sharding import Mesh, PartitionSpec as P

D = 6144
EXPERTS = 8
NX, NYH, NYL, NZ, NC = 4, 2, 4, 8, 2
NZC = NZ * NC
ROW_DEV = 128
CAP = 64
EXTRA = 16
BF = jnp.bfloat16
F32 = jnp.float32


def three_parts(value):
    hi = value.astype(BF)
    rest = value - hi.astype(F32)
    mid = rest.astype(BF)
    lo = (rest - mid.astype(F32)).astype(BF)
    return [hi, mid, lo]


def from_parts(parts):
    parts = parts.astype(F32)
    return parts[0] + parts[1] + parts[2]


def slot_targets(route_rows, half):
    experts = jnp.arange(EXPERTS, dtype=jnp.int32)
    named = route_rows[:, :, None, :] == experts[None, None, :, None]
    mask = (named[0] | named[1]).astype(BF)
    earlier = lax.broadcasted_iota(jnp.int32, (ROW_DEV, ROW_DEV), 0) < lax.broadcasted_iota(
        jnp.int32, (ROW_DEV, ROW_DEV), 1
    )
    before = jnp.dot(
        mask.reshape(NYH * EXPERTS, ROW_DEV), earlier.astype(BF), preferred_element_type=F32
    ).reshape(1, NYH, EXPERTS, ROW_DEV)
    rank = jnp.sum(jnp.where(named, before, 0.0), axis=2).astype(jnp.int32)
    block = jnp.arange(NYH, dtype=jnp.int32)[None, :, None]
    target = (route_rows // 2) * (NYH * CAP) + block * CAP + rank
    return jnp.where(route_rows % 2 == half, target, -1).reshape(2, NYH * ROW_DEV)


def per_device(hidden_state, norm_gain, routes, gates, w_gate, w_up, w_down):
    half = lax.axis_index("yh")
    quarter = lax.axis_index("yl")

    values = hidden_state.astype(F32)
    scaled = (values * norm_gain.astype(F32)[None, :]).astype(BF).T
    extras = three_parts(jnp.sum(values * values, axis=1))
    extras += [routes[:, 0].astype(BF), routes[:, 1].astype(BF)]
    extras += three_parts(gates[:, 0]) + three_parts(gates[:, 1])
    extras += [jnp.zeros((ROW_DEV,), BF)] * (EXTRA - len(extras))
    payload = jnp.concatenate([scaled, jnp.stack(extras)], axis=0)

    with jax.named_scope("rows_over_y"):
        held = lax.all_gather(payload, ("yh", "yl"), axis=0, tiled=False)
    feats = held.shape[1] - EXTRA
    held = held.reshape(NYH, NYL, feats + EXTRA, ROW_DEV)
    info = held[:, 0, feats:, :]
    squares = jnp.sum(
        held[:, :, feats, :].astype(F32)
        + held[:, :, feats + 1, :].astype(F32)
        + held[:, :, feats + 2, :].astype(F32),
        axis=1,
    ).reshape(NYH * ROW_DEV)
    route_rows = info[:, 3:5, :].astype(jnp.int32).transpose(1, 0, 2)
    gate0 = from_parts(info[:, 5:8, :].transpose(1, 0, 2)).reshape(1, NYH * ROW_DEV)
    gate1 = from_parts(info[:, 8:11, :].transpose(1, 0, 2)).reshape(1, NYH * ROW_DEV)
    targets = slot_targets(route_rows, half)
    slot_ids = lax.broadcasted_iota(jnp.int32, (NX * NYH * CAP, NYH * ROW_DEV), 0)
    place0 = (slot_ids == targets[0][None, :]).astype(BF)
    place1 = (slot_ids == targets[1][None, :]).astype(BF)

    rows = held[:, :, :feats, :].transpose(1, 2, 0, 3).reshape(NYL * feats, NYH * ROW_DEV)
    square_rows = jnp.stack(three_parts(squares) + [jnp.zeros_like(squares, BF)] * (EXTRA - 3))
    rows = jnp.concatenate([rows, square_rows], axis=0)
    depth = rows.shape[0]
    outgoing = lax.dot_general(
        rows, place0 + place1, (((1,), (1,)), ((), ())), preferred_element_type=F32
    ).astype(BF)
    outgoing = outgoing.reshape(depth, NX, NYH * CAP).transpose(1, 0, 2)
    with jax.named_scope("rows_over_x"):
        incoming = lax.all_to_all(outgoing, "x", split_axis=0, concat_axis=0, tiled=True)
    slots = NX * NYH * CAP
    incoming = incoming.transpose(1, 0, 2).reshape(depth, slots)

    incoming, down, gate_cols, up_cols = lax.optimization_barrier(
        (incoming, w_down[0], w_gate[0], w_up[0])
    )
    with jax.named_scope("features_over_zc"):
        features = lax.all_gather(incoming, ("z", "c"), axis=0, tiled=True)
    units = down.shape[0] // NYL
    down_t = down.T.reshape(feats, NYL, units).transpose(1, 0, 2)
    pieces = [lax.dynamic_index_in_dim(down_t, quarter, 0, keepdims=False)]
    for m in range(1, NYL):
        piece = lax.dynamic_index_in_dim(down_t, quarter ^ m, 0, keepdims=False)
        with jax.named_scope("down_over_y"):
            pieces.append(lax.ppermute(piece, "yl", [(i, i ^ m) for i in range(NYL)]))
    pieces = jnp.stack(pieces)
    down_part = jnp.concatenate(
        [lax.dynamic_index_in_dim(pieces, quarter ^ j, 0, keepdims=False) for j in range(NYL)], axis=0
    )

    def reordered(cols):
        cols = cols.reshape(NYL, NZC, feats, cols.shape[1]).transpose(1, 0, 2, 3)
        cols = cols.reshape(NZC, NYL * feats, cols.shape[3])
        return jnp.pad(cols, ((0, 0), (0, EXTRA), (0, 0)))

    both = jnp.concatenate([reordered(gate_cols), reordered(up_cols)], axis=2)
    both = both.reshape(NZC * depth, both.shape[2])
    squares = features.reshape(NZC, depth, slots)[:, NYL * feats : NYL * feats + 3, :]
    inv_rms = lax.rsqrt(jnp.sum(squares.astype(F32), axis=(0, 1)) / D + 1e-05)[None, :]
    hidden = lax.dot_general(both, features, (((0,), (0,)), ((), ())), preferred_element_type=F32)
    own = hidden.shape[0] // 2
    act = (jax.nn.silu(hidden[:own] * inv_rms) * (hidden[own:] * inv_rms)).astype(BF)

    with jax.named_scope("units_over_zc"):
        acts = lax.all_gather(act, ("z", "c"), axis=0, tiled=True)
    out = jnp.dot(down_part, acts, preferred_element_type=F32).astype(BF)
    out = out.reshape(NYL * feats, NX, NYH * CAP).transpose(1, 0, 2)
    with jax.named_scope("out_over_x"):
        back = lax.all_to_all(out, "x", split_axis=0, concat_axis=0, tiled=True)
    back = back.transpose(1, 0, 2).reshape(NYL * feats, slots)
    mixed = gate0 * jnp.dot(back, place0, preferred_element_type=F32) + gate1 * jnp.dot(
        back, place1, preferred_element_type=F32
    )
    mixed = mixed.reshape(NYL, feats, NYH, ROW_DEV).transpose(2, 0, 1, 3)
    mixed = mixed.reshape(NYH * NYL, feats, ROW_DEV).astype(BF)
    with jax.named_scope("out_over_y"):
        parts = lax.all_to_all(mixed, ("yh", "yl"), split_axis=0, concat_axis=0, tiled=True)
    return jnp.sum(parts.astype(F32), axis=0).T.astype(BF)


def solution(mesh):
    fine = Mesh(mesh.devices.reshape(NX, NYH, NYL, NZ, NC), ("x", "yh", "yl", "z", "c"))
    exp, tp = ("x", "yh"), ("yl", "z", "c")
    in_specs = (
        P(exp, tp),
        P(tp),
        P(exp, None),
        P(exp, None),
        P(exp, None, tp),
        P(exp, None, tp),
        P(exp, None, tp),
    )
    return jax.shard_map(
        per_device, mesh=fine, in_specs=in_specs, out_specs=P(exp, tp), check_vma=False
    )
```

time: 466 us -> 194 us (0.42)
  waiting for transfers between devices: 262 us -> 93.7 us
  blocking collectives: 157 us -> 45.4 us
  matrix products: 15.9 us -> 8.42 us
  local copies, waits for them, and re-layouts: 5.15 us -> 11.5 us
  starting transfers between devices: 7.95 us -> 13.3 us
    all_gather x2, waiting for transfers between devices: 253 us -> 58.7 us  [the longest x1 58.7 us: per_device(): features = lax.all_gather(incoming, ('z', 'c'), axis=0, tiled=True)]
    psum x1 -> x0, blocking collectives: 141 us -> none  [per_device(): squares = lax.psum(jnp.sum(values * values, axis=1), 'tp')]
    ppermute x0 -> x3, waiting for transfers between devices: none -> 28.5 us  [per_device(): pieces.append(lax.ppermute(piece, 'yl', [(i, i ^ m) for i in range(NYL)]))]
    all_gather x0 -> x1, blocking collectives: none -> 20.8 us  [per_device(): held = lax.all_gather(payload, ('yh', 'yl'), axis=0, tiled=False)]
    ppermute x0 -> x3, starting transfers between devices: none -> 9.27 us  [per_device(): pieces.append(lax.ppermute(piece, 'yl', [(i, i ^ m) for i in range(NYL)]))]
    all_to_all x1 -> x2, blocking collectives: 15.8 us -> 24.6 us  [the longest x1 14.1 us: per_device(): lax.all_to_all(mixed, ('yh', 'yl'), split_axis=0, concat_axis=0, tiled=True)]
    dot_general x4 -> x6, matrix products: 15.9 us -> 8.42 us  [the longest x1 4.73 us: per_device(): lax.dot_general(both, features, (((0,), (0,)), ((), ())), preferred_eleme...]
  transfers between devices with their start and end apart: 3 -> 6, of which waited for: 3 -> 4; matrix products, arithmetic and copies ran while one was open for 0% -> 4% of each run, Pallas kernels for 0% -> 0%
where the time goes in v1:
time: 194 us; the launch traced here: 192 us
  waiting for transfers between devices  93.7 us (48%)
  blocking collectives  45.4 us (23%)
  between operations  13.7 us (7%)
  starting transfers between devices  13.3 us (7%)
  local copies, waits for them, and re-layouts  11.5 us (6%)
  matrix products  8.42 us (4%)
  other arithmetic  6.03 us (3%)
    all_gather x1, waiting for transfers between devices, per_device(): features = lax.all_gather(incoming, ('z', 'c'), axis=0, tiled=True)  58.7 us
    ppermute x3, waiting for transfers between devices, per_device(): pieces.append(lax.ppermute(piece, 'yl', [(i, i ^ m) for i in range(NYL)]))  28.5 us
    all_gather x1, blocking collectives, per_device(): held = lax.all_gather(payload, ('yh', 'yl'), axis=0, tiled=False)  20.8 us
    all_to_all x1, blocking collectives, per_device(): lax.all_to_all(mixed, ('yh', 'yl'), split_axis=0, concat_axis=0, tiled=True)  14.1 us
    all_to_all x1, blocking collectives, per_device(): lax.all_to_all(outgoing, 'x', split_axis=0, concat_axis=0, tiled=True)  10.5 us
    ppermute x3, starting transfers between devices, per_device(): pieces.append(lax.ppermute(piece, 'yl', [(i, i ^ m) for i in range(NYL)]))  9.27 us
    all_to_all x1, waiting for transfers between devices, per_device(): back = lax.all_to_all(out, 'x', split_axis=0, concat_axis=0, tiled=True)  6.45 us
    dot_general x1, matrix products, per_device(): lax.dot_general(both, features, (((0,), (0,)), ((), ())), preferred_eleme...  4.73 us
  transfers between devices with their start and end apart: 6, of which 4 were waited for; matrix products, arithmetic and copies ran while one was open for 4% of the time, Pallas kernels for 0%

profile of v1, /device:TPU:1, one launch (start us, length us, event | category | flops | bytes accessed | tf_op | source)
XLA Modules:
  0.0 192.1 jit_solution(11184248335502233781)
XLA Ops:
  6.5 0.7 convert_element_type.364
  7.2 0.8 fusion.35
  8.0 0.8 subtract_convert_fusion.1
  8.8 0.7 convert.8
  9.5 0.8 bitcast_convert_fusion
  10.3 20.8 %all-gather = bf16[896,128]{1,0:T(8,128)(2,1)S(1)} all-gather(bf16[112,128]{1,0:T(8,128)(2,1)S(1)} %concatenate.22), channel_id=2, replica_groups=mesh['x'=4,'yh'=2,'yl'=4,'z'=8,'c'=2] {'yh','yl'}, dimensions={0}, use_global_device_ids=true | all-gather | bytes 258048 | tf_op jit(solution)/shard_map/rows_over_y/all_gather | solution.py:59
  32.3 10.5 %all_to_all.15 = bf16[4,400,128]{2,1,0:T(8,128)(2,1)S(1)} all-to-all(bf16[4,400,128]{2,1,0:T(8,128)(2,1)S(1)} %bitcast.151), channel_id=1, replica_groups=mesh['x'=4,'yh'=2,'yl'=4,'z'=8,'c'=2] {'x'}, dimensions={0} | all-to-all | bytes 819200 | tf_op jit(solution)/shard_map/rows_over_x/all_to_all | solution.py:86
  42.8 0.8 copy_bitcast_fusion
  44.9 58.7 %all-gather.4.cloned.1.call-done = bf16[6400,512]{1,0:T(8,128)(2,1)} async-done(((bf16[400,512]{1,0:T(8,128)(2,1)}), bf16[6400,512]{1,0:T(8,128)(2,1)}) %all-gather.4.cloned.1.call-update) | async-done | bytes 6553616 | tf_op jit(solution)/shard_map/features_over_zc/all_gather | solution.py:94
  103.6 1.0 convert_reduce_fusion
  104.6 4.7 %fusion.50 = f32[256,512]{1,0:T(8,128)S(1)} fusion(bf16[6400,256]{1,0:T(8,128)(2,1)S(1)} %bitcast.147, bf16[6400,512]{1,0:T(8,128)(2,1)} %all-gather.4.cloned.1.call-done), kind=kOutput, calls=%fused_computation.110 | convolution fusion | flops 1677721600 | bytes 10354688 | tf_op jit(solution)/shard_map/dot_general | solution.py:116
  109.3 0.7 fusion.26
  110.1 2.9 %reshape.315 = bf16[96,4,2048]{2,1,0:T(4,128)(2,1)S(1)} reshape(bf16[96,8192]{1,0:T(8,128)(2,1)} %bitcast.154) | data formatting | bytes 3145728 | tf_op jit(solution)/shard_map/reshape | solution.py:96
  113.0 3.4 %constant_dynamic-slice_fusion.3 = (bf16[96,1,2048]{2,1,0:T(2,128)(2,1)S(1)}, bf16[96,1,2048]{2,1,0:T(2,128)(2,1)S(1)}, bf16[96,1,2048]{2,1,0:T(2,128)(2,1)S(1)}, bf16[96,1,2048]{2,1,0:T(2,128)(2,1)S(1)}) fusion(bf16[96,4,2048]{2,1,0:T(4,128)(2,1)S(1)} %reshape.315, s32[]{:T(128)S(6)} %select_n.41, s32[]{:T(128)S(6)} %select_n.44, s32[]{:T(128)S(6)} %select_n.43, ...), kind=kLoop, calls=%fused_computation.82 | loop fusion | bytes 3145744 | tf_op jit(solution)/shard_map/dynamic-slice
  116.7 5.0 %collective-permute-start.2 = (bf16[96,2048]{1,0:T(8,128)(2,1)S(1)}, bf16[96,2048]{1,0:T(8,128)(2,1)S(1)}, u32[]{:S(2)}, u32[]{:S(2)}) collective-permute-start(bf16[96,2048]{1,0:T(8,128)(2,1)S(1)} %bitcast.167), channel_id=1, source_target_pairs={{0,48},{16,32},{32,16},{48,0},{1,49},{17,33},{33,17},{49,1},{2,50}... | collective-permute-start | bytes 1179656 | tf_op jit(solution)/shard_map/down_over_y/ppermute | solution.py:101
  121.9 1.9 %collective-permute-start.1 = (bf16[96,2048]{1,0:T(8,128)(2,1)S(1)}, bf16[96,2048]{1,0:T(8,128)(2,1)S(1)}, u32[]{:S(2)}, u32[]{:S(2)}) collective-permute-start(bf16[96,2048]{1,0:T(8,128)(2,1)S(1)} %bitcast.168), channel_id=1, source_target_pairs={{0,32},{16,48},{32,0},{48,16},{1,33},{17,49},{33,1},{49,17},{2,34}... | collective-permute-start | bytes 1179656 | tf_op jit(solution)/shard_map/down_over_y/ppermute | solution.py:101
  124.1 2.4 %collective-permute-start = (bf16[96,2048]{1,0:T(8,128)(2,1)S(1)}, bf16[96,2048]{1,0:T(8,128)(2,1)S(1)}, u32[]{:S(2)}, u32[]{:S(2)}) collective-permute-start(bf16[96,2048]{1,0:T(8,128)(2,1)S(1)} %bitcast.169), channel_id=1, source_target_pairs={{0,16},{16,0},{32,48},{48,32},{1,17},{17,1},{33,49},{49,33},{2,18}... | collective-permute-start | bytes 1179656 | tf_op jit(solution)/shard_map/down_over_y/ppermute | solution.py:101
  126.7 4.2 %collective-permute-done.2 = bf16[96,2048]{1,0:T(8,128)(2,1)S(1)} collective-permute-done((bf16[96,2048]{1,0:T(8,128)(2,1)S(1)}, bf16[96,2048]{1,0:T(8,128)(2,1)S(1)}, u32[]{:S(2)}, u32[]{:S(2)}) %collective-permute-start.2) | collective-permute-done | bytes 393248 | tf_op jit(solution)/shard_map/down_over_y/ppermute | solution.py:101
  130.9 24.4 %collective-permute-done.1 = bf16[96,2048]{1,0:T(8,128)(2,1)S(1)} collective-permute-done((bf16[96,2048]{1,0:T(8,128)(2,1)S(1)}, bf16[96,2048]{1,0:T(8,128)(2,1)S(1)}, u32[]{:S(2)}, u32[]{:S(2)}) %collective-permute-start.1) | collective-permute-done | bytes 393248 | tf_op jit(solution)/shard_map/down_over_y/ppermute | solution.py:101
  155.7 2.6 %fusion.15 = bf16[48,4,8,128]{3,2,1,0:T(8,128)(2,1)S(1)} fusion(bf16[2048,512]{1,0:T(8,128)(2,1)} %all-gather.6.cloned.1.call-done, bf16[96,2048]{1,0:T(8,128)(2,1)S(1)} %get-tuple-element.14, bf16[96,2048]{1,0:T(8,128)(2,1)S(1)} %get-tuple-element.15, bf16[96,2048]{1,0:T(8,128)(2,1)S(1)} %get-tuple-element.16, bf16[96,2048]{1,0:T(8,128)(2,1)S(1)} %get-tuple-element.13), kind=kOutput, calls=%fused_computation.17 | convolution fusion | flops 811794432 | bytes 4063232 | tf_op jit(solution)/shard_map/dot_general | solution.py:122
  158.2 0.8 copy.50
  159.1 4.0 %all-to-all-start.1 = ((bf16[4,384,128]{2,1,0:T(8,128)(2,1)}), bf16[4,384,128]{2,1,0:T(8,128)(2,1)S(1)}, u32[]{:S(2)}, u32[]{:S(2)}) async-start(bf16[4,384,128]{2,1,0:T(8,128)(2,1)} %bitcast.140), calls=%async_computation.1 | async-start | bytes 786432 | tf_op jit(solution)/shard_map/out_over_x/all_to_all | solution.py:125
  163.0 6.4 %all-to-all-done.1 = bf16[4,384,128]{2,1,0:T(8,128)(2,1)S(1)} async-done(((bf16[4,384,128]{2,1,0:T(8,128)(2,1)}), bf16[4,384,128]{2,1,0:T(8,128)(2,1)S(1)}, u32[]{:S(2)}, u32[]{:S(2)}) %all-to-all-start.1) | async-done | bytes 393248 | tf_op jit(solution)/shard_map/out_over_x/all_to_all | solution.py:125
  170.5 14.1 %all_to_all.16 = bf16[8,96,128]{2,1,0:T(8,128)(2,1)S(1)} all-to-all(bf16[8,96,128]{2,1,0:T(8,128)(2,1)S(1)} %bitcast.161), channel_id=1, replica_groups=mesh['x'=4,'yh'=2,'yl'=4,'z'=8,'c'=2] {'yh','yl'}, dimensions={0} | all-to-all | bytes 393216 | tf_op jit(solution)/shard_map/out_over_y/all_to_all | solution.py:133
  (54 shorter events, 5.4 us)
Async XLA Ops:
  6.5 97.1 %all-gather.4.cloned.1.call-start = ((), (), s32[]{:S(2)}) async-start(), calls=%async_computation.3 | async-start | bytes 6963200 | tf_op jit(solution)/shard_map/features_over_zc/all_gather | solution.py:94
  31.4 12.2 %copy-start = (bf16[1,6144,128]{2,1,0:T(8,128)(2,1)S(1)}, bf16[1,6144,128]{2,1,0:T(8,128)(2,1)}, u32[]{:S(2)}) copy-start(bf16[1,6144,128]{2,1,0:T(8,128)(2,1)} %param.12) | copy-start | bytes 4718596
  42.8 1.6 copy-start.1
  43.6 112.0 %all-gather.6.cloned.1.call-start = ((), (), s32[]{:S(2)}) async-start(), calls=%async_computation.4 | async-start | bytes 2228224 | tf_op jit(solution)/shard_map/units_over_zc/all_gather | solution.py:121
  116.7 14.2 %collective-permute-start.2 = (bf16[96,2048]{1,0:T(8,128)(2,1)S(1)}, bf16[96,2048]{1,0:T(8,128)(2,1)S(1)}, u32[]{:S(2)}, u32[]{:S(2)}) collective-permute-start(bf16[96,2048]{1,0:T(8,128)(2,1)S(1)} %bitcast.167), channel_id=1, source_target_pairs={{0,48},{16,32},{32,16},{48,0},{1,49},{17,33},{33,17},{49,1},{2,50}... | collective-permute-start | bytes 1179656 | tf_op jit(solution)/shard_map/down_over_y/ppermute | solution.py:101
  121.9 33.3 %collective-permute-start.1 = (bf16[96,2048]{1,0:T(8,128)(2,1)S(1)}, bf16[96,2048]{1,0:T(8,128)(2,1)S(1)}, u32[]{:S(2)}, u32[]{:S(2)}) collective-permute-start(bf16[96,2048]{1,0:T(8,128)(2,1)S(1)} %bitcast.168), channel_id=1, source_target_pairs={{0,32},{16,48},{32,0},{48,16},{1,33},{17,49},{33,1},{49,17},{2,34}... | collective-permute-start | bytes 1179656 | tf_op jit(solution)/shard_map/down_over_y/ppermute | solution.py:101
  124.1 31.2 %collective-permute-start = (bf16[96,2048]{1,0:T(8,128)(2,1)S(1)}, bf16[96,2048]{1,0:T(8,128)(2,1)S(1)}, u32[]{:S(2)}, u32[]{:S(2)}) collective-permute-start(bf16[96,2048]{1,0:T(8,128)(2,1)S(1)} %bitcast.169), channel_id=1, source_target_pairs={{0,16},{16,0},{32,48},{48,32},{1,17},{17,1},{33,49},{49,33},{2,18}... | collective-permute-start | bytes 1179656 | tf_op jit(solution)/shard_map/down_over_y/ppermute | solution.py:101
  159.1 10.4 %all-to-all-start.1 = ((bf16[4,384,128]{2,1,0:T(8,128)(2,1)}), bf16[4,384,128]{2,1,0:T(8,128)(2,1)S(1)}, u32[]{:S(2)}, u32[]{:S(2)}) async-start(bf16[4,384,128]{2,1,0:T(8,128)(2,1)} %bitcast.140), calls=%async_computation.1 | async-start | bytes 786432 | tf_op jit(solution)/shard_map/out_over_x/all_to_all | solution.py:125
Sparse Core Ops, SparseCore 0:
  43.7 59.8 all-gather.3
  110.2 41.0 all-gather.5

commit v2 on v0

v2 whole, which is shorter than its diff:
```python
import functools

import jax
import jax.numpy as jnp
from jax import lax
from jax.experimental import pallas as pl
from jax.experimental.pallas import tpu as pltpu
from jax.sharding import Mesh, PartitionSpec as P

D = 6144
EXPERTS = 8
NX, NYH, NYL, NZ, NC = 4, 2, 4, 8, 2
NZC = NZ * NC
FEATS = 96
ROW_DEV = 128
CAP = 64
SLOTS = EXPERTS * CAP
EXTRA = 16
DEPTH = NYL * FEATS + EXTRA
KSTEPS = 5
BF = jnp.bfloat16
F32 = jnp.float32
I32 = jnp.int32
BIG = 3.0e38
NT = (((1,), (1,)), ((), ()))
TN = (((0,), (0,)), ((), ()))
VMEM_LIMIT = 40 * 1024 * 1024


def iota(shape, dim):
    return lax.broadcasted_iota(I32, shape, dim)


def one_hot(condition):
    return jnp.where(condition, 1.0, 0.0).astype(BF)


def dot(a, b, dims=(((1,), (0,)), ((), ()))):
    return lax.dot_general(a, b, dims, preferred_element_type=F32)


def call(body, out_shape, *args, flops=1_000_000, moved=1_000_000, scalars=0, **kw):
    specs = [pl.BlockSpec(memory_space=pltpu.SMEM)] * scalars
    specs += [pl.BlockSpec(memory_space=pltpu.VMEM)] * (len(args) - scalars)
    return pl.pallas_call(
        body,
        out_shape=out_shape,
        in_specs=specs,
        out_specs=jax.tree.map(lambda _: pl.BlockSpec(memory_space=pltpu.VMEM), out_shape),
        compiler_params=pltpu.CompilerParams(vmem_limit_bytes=VMEM_LIMIT),
        cost_estimate=pl.CostEstimate(flops=flops, bytes_accessed=moved, transcendentals=0),
        **kw,
    )(*args)


def dispatch_body(hidden_ref, gain_ref, routes_ref, out_ref, target_ref):
    diagonal = iota((FEATS, FEATS), 0) == iota((FEATS, FEATS), 1)
    gain = jnp.sum(jnp.where(diagonal, gain_ref[...].astype(F32), 0.0), axis=1, keepdims=True)
    values = hidden_ref[...].astype(F32)
    scaled = jnp.clip(values * gain, -BIG, BIG)
    squares = jnp.minimum(jnp.sum(values * values, axis=0, keepdims=True), BIG)
    hi = squares.astype(BF).astype(F32)
    mid = (squares - hi).astype(BF).astype(F32)
    low = squares - hi - mid
    row = iota((ROW_DEV - FEATS, ROW_DEV), 0)
    parts = jnp.where(row == 0, hi, jnp.where(row == 1, mid, jnp.where(row == 2, low, 0.0)))
    rows = jnp.concatenate([scaled, parts], axis=0).astype(BF)

    first, second = routes_ref[0:1, :], routes_ref[1:2, :]
    expert = iota((2 * EXPERTS, ROW_DEV), 0)
    named0, named1 = expert == first, expert == second
    earlier = one_hot(iota((ROW_DEV, ROW_DEV), 0) < iota((ROW_DEV, ROW_DEV), 1))
    before = dot(one_hot(named0 | named1), earlier)
    rank0 = jnp.sum(jnp.where(named0, before, 0.0), axis=0, keepdims=True).astype(I32)
    rank1 = jnp.sum(jnp.where(named1, before, 0.0), axis=0, keepdims=True).astype(I32)
    target0, target1 = first * CAP + rank0, second * CAP + rank1
    target_ref[...] = jnp.where(iota((8, ROW_DEV), 0) == 0, target0, target1)
    slot = iota((SLOTS, ROW_DEV), 0)
    place = one_hot((slot == target0) | (slot == target1))
    sent = dot(place, rows, NT).astype(BF).reshape(EXPERTS, CAP, ROW_DEV)
    for j in range(NYL):
        out_ref[:, j] = sent


def turn_body(in_ref, out_ref):
    eye = one_hot(iota((FEATS, ROW_DEV), 0) == iota((FEATS, ROW_DEV), 1))
    row, lane = iota((EXTRA, ROW_DEV), 0), iota((EXTRA, ROW_DEV), 1)
    extra = jnp.zeros((EXTRA, SLOTS), F32)
    for j in range(NYL):
        rows = in_ref[:, j].reshape(SLOTS, ROW_DEV)
        out_ref[j * FEATS : (j + 1) * FEATS, :] = dot(eye, rows, NT).astype(BF)
        pick = one_hot((row - 3 * j == lane - FEATS) & (row >= 3 * j) & (row < 3 * j + 3))
        extra += dot(pick, rows, NT)
    out_ref[NYL * FEATS :, :] = extra.astype(BF)


def act_body(w_ref, x_ref, *rest):
    out_ref, acc_ref = rest[-2:]
    step = pl.program_id(0)

    @pl.when(step == 0)
    def _():
        acc_ref[...] = jnp.zeros_like(acc_ref)

    acc_ref[...] += dot(w_ref[...], x_ref[...])

    @pl.when(step == KSTEPS - 1)
    def _():
        units = out_ref.shape[1]
        inv_rms = lax.rsqrt(acc_ref[2 * units : 2 * units + 1, :] / D + 1e-05)
        gate = acc_ref[:units, :] * inv_rms
        up = acc_ref[units : 2 * units, :] * inv_rms
        act = (gate / (1.0 + jnp.exp(-gate)) * up).astype(BF)
        for z in range(NZ):
            out_ref[z] = act


def act_call(w, x, after):
    units = (w.shape[0] - EXTRA) // 2
    chunk = x.shape[0] // KSTEPS
    return pl.pallas_call(
        act_body,
        out_shape=jax.ShapeDtypeStruct((NZ, units, SLOTS), BF),
        grid=(KSTEPS,),
        in_specs=[
            pl.BlockSpec((w.shape[0], chunk), lambda k: (0, k)),
            pl.BlockSpec((chunk, SLOTS), lambda k: (k, 0)),
        ]
        + [pl.BlockSpec(memory_space=pl.ANY)] * len(after),
        out_specs=pl.BlockSpec((NZ, units, SLOTS), lambda k: (0, 0, 0)),
        scratch_shapes=[pltpu.VMEM((w.shape[0], SLOTS), F32)],
        compiler_params=pltpu.CompilerParams(
            dimension_semantics=("arbitrary",), vmem_limit_bytes=60 * 1024 * 1024
        ),
        cost_estimate=pl.CostEstimate(
            flops=2 * w.shape[0] * x.shape[0] * SLOTS, bytes_accessed=10_000_000, transcendentals=0
        ),
    )(w, x, *after)


def own_half_body(w_ref, x_ref, out_ref):
    out_ref[...] = dot(w_ref[...], x_ref[...])


def other_half_body(w_ref, x_ref, part_ref, out_ref):
    half = FEATS // 2
    out = part_ref[...] + dot(w_ref[...], x_ref[...])
    low = iota((half, 2 * CAP), 1) < CAP
    for j in range(NYL):
        for t in range(EXPERTS // 2):
            cols = slice(t * 2 * CAP, (t + 1) * 2 * CAP)
            a = out[j * FEATS : j * FEATS + half, cols]
            b = out[j * FEATS + half : (j + 1) * FEATS, cols]
            out_ref[2 * t, j] = jnp.where(low, a, pltpu.roll(b, CAP, 1)).astype(BF)
            out_ref[2 * t + 1, j] = jnp.where(low, pltpu.roll(a, CAP, 1), b).astype(BF)


def combine_body(in_ref, target_ref, gates_ref, out_ref):
    half = FEATS // 2
    target = jnp.concatenate([target_ref[0:1, :], target_ref[1:2, :]], axis=1)
    slot = iota((2 * CAP, 2 * ROW_DEV), 0) % CAP
    low = iota((half, 2 * CAP), 1) < CAP
    picked = jnp.zeros((FEATS, 2 * ROW_DEV), F32)
    for e in range(EXPERTS):
        place = one_hot(target - e * CAP == slot)
        total = in_ref[e, 0].astype(F32)
        for j in range(1, NYL):
            total += in_ref[e, j].astype(F32)
        total = jnp.concatenate([jnp.where(low, total, 0.0), jnp.where(low, 0.0, total)], axis=0)
        hi = total.astype(BF)
        rest = (total - hi.astype(F32)).astype(BF)
        picked += dot(hi, place) + dot(rest, place)
    mixed = gates_ref[0:1, :] * picked[:, :ROW_DEV] + gates_ref[1:2, :] * picked[:, ROW_DEV:]
    out_ref[...] = mixed.astype(BF)


def cut_body(place_ref, in_ref, *out_refs):
    width = out_refs[0].shape[1]
    for m, out_ref in enumerate(out_refs):
        start = pl.multiple_of(place_ref[m] * width, width)
        out_ref[...] = in_ref[:, pl.ds(start, width)]


def join_body(place_ref, *refs):
    pieces, (own_ref, other_ref) = refs[:NYL], refs[NYL:]
    step = pieces[0].shape[1] // NZC
    core = place_ref[NYL]
    for m, piece in enumerate(pieces):
        rows = pl.ds(pl.multiple_of(place_ref[m] * FEATS, FEATS), FEATS)
        for z in range(NZ):
            own = pl.ds(pl.multiple_of((2 * z + core) * step, step), step)
            other = pl.ds(pl.multiple_of((2 * z + 1 - core) * step, step), step)
            own_ref[rows, z * step : (z + 1) * step] = piece[:, own]
            other_ref[rows, z * step : (z + 1) * step] = piece[:, other]


def per_device(hidden_state, norm_gain, routes, gates, w_gate, w_up, w_down):
    quarter = lax.axis_index("yl")
    core = lax.axis_index("c")
    owners = ("x", "yh", "yl")

    outgoing, targets = call(
        dispatch_body,
        (
            jax.ShapeDtypeStruct((EXPERTS, NYL, CAP, ROW_DEV), BF),
            jax.ShapeDtypeStruct((8, ROW_DEV), I32),
        ),
        hidden_state.T,
        norm_gain[None, :],
        routes.T,
    )
    with jax.named_scope("rows_over_xy"):
        incoming = lax.all_to_all(
            outgoing.reshape(EXPERTS * NYL, CAP, ROW_DEV), owners, split_axis=0, concat_axis=0, tiled=True
        )
    incoming = incoming.reshape(EXPERTS, NYL, CAP, ROW_DEV)
    block = call(turn_body, jax.ShapeDtypeStruct((DEPTH, SLOTS), BF), incoming)

    block, down, gate_cols, up_cols = lax.optimization_barrier(
        (block, w_down[0], w_gate[0], w_up[0])
    )
    with jax.named_scope("features_over_zc"):
        features = lax.all_gather(block, ("z", "c"), axis=0, tiled=True)
    units = down.shape[0] // NYL
    places = jnp.stack([quarter ^ m for m in range(NYL)] + [core]).astype(I32)
    piece = jax.ShapeDtypeStruct((FEATS, units), BF)
    pieces = list(call(cut_body, (piece,) * NYL, places, down.T, scalars=1))
    for m in range(1, NYL):
        with jax.named_scope("down_over_y"):
            pieces[m] = lax.ppermute(pieces[m], "yl", [(i, i ^ m) for i in range(NYL)])
    part = jax.ShapeDtypeStruct((NYL * FEATS, units // NC), BF)
    down_own, down_other = call(join_body, (part, part), places, *pieces, scalars=1)

    def in_order(cols):
        cols = cols.reshape(NYL, NZC, FEATS, cols.shape[1]).transpose(1, 0, 2, 3)
        cols = cols.reshape(NZC, NYL * FEATS, cols.shape[3])
        return jnp.pad(cols, ((0, 0), (0, EXTRA), (0, 0)))

    is_part = (jnp.arange(DEPTH) >= NYL * FEATS) & (jnp.arange(DEPTH) < NYL * FEATS + 3 * NYL)
    count = jnp.broadcast_to(is_part.astype(BF)[None, :, None], (NZC, DEPTH, EXTRA))
    both = jnp.concatenate([in_order(gate_cols), in_order(up_cols), count], axis=2)
    both = both.reshape(NZC * DEPTH, both.shape[2]).T
    acts = act_call(both, features, (down_own, down_other))

    with jax.named_scope("units_over_z"):
        acts = lax.all_to_all(acts, "z", split_axis=0, concat_axis=0, tiled=True)
    acts = acts.reshape(units // NC, SLOTS)
    with jax.named_scope("units_over_c"):
        acts_other = lax.ppermute(acts, "c", [(0, 1), (1, 0)])
    part = call(
        own_half_body,
        jax.ShapeDtypeStruct((NYL * FEATS, SLOTS), F32),
        down_own,
        acts,
        flops=2 * NYL * FEATS * SLOTS * units // NC,
        moved=3_000_000,
    )
    out = call(
        other_half_body,
        jax.ShapeDtypeStruct((EXPERTS, NYL, FEATS // 2, 2 * CAP), BF),
        down_other,
        acts_other,
        part,
    )
    with jax.named_scope("out_over_xy"):
        back = lax.all_to_all(
            out.reshape(EXPERTS * NYL, FEATS // 2, 2 * CAP), owners, split_axis=0, concat_axis=0, tiled=True
        )
    back = back.reshape(EXPERTS, NYL, FEATS // 2, 2 * CAP)
    return call(
        combine_body, jax.ShapeDtypeStruct((FEATS, ROW_DEV), BF), back, targets, gates.T
    ).T


def solution(mesh):
    fine = Mesh(mesh.devices.reshape(NX, NYH, NYL, NZ, NC), ("x", "yh", "yl", "z", "c"))
    exp, tp = ("x", "yh"), ("yl", "z", "c")
    in_specs = (
        P(exp, tp),
        P(tp),
        P(exp, None),
        P(exp, None),
        P(exp, None, tp),
        P(exp, None, tp),
        P(exp, None, tp),
    )
    return jax.shard_map(
        per_device, mesh=fine, in_specs=in_specs, out_specs=P(exp, tp), check_vma=False
    )
```

time: 466 us -> 167 us (0.36)
  the two profiles are of different devices: /device:TPU:1 before, /device:TPU:8 now
where the time goes in v2:
time: 167 us
  blocking collectives  85.9 us (51%)
  waiting for transfers between devices  26.3 us (16%)
  local copies, waits for them, and re-layouts  13.9 us (8%)
  between operations  13.5 us (8%)
  Pallas kernels  13 us (8%)
  starting transfers between devices  11.1 us (7%)
  other arithmetic  3.02 us (2%)
    all_to_all x1, blocking collectives, per_device(): acts = lax.all_to_all(acts, 'z', split_axis=0, concat_axis=0, tiled=True)  33.4 us
    all_to_all x1, blocking collectives, per_device(): lax.all_to_all(outgoing.reshape(EXPERTS * NYL, CAP, ROW_DEV), owners, spl...  27.6 us
    all_to_all x1, blocking collectives, per_device(): lax.all_to_all(out.reshape(EXPERTS * NYL, FEATS // 2, 2 * CAP), owners, s...  25 us
    ppermute x3, waiting for transfers between devices, per_device(): pieces[m] = lax.ppermute(pieces[m], 'yl', [(i, i ^ m) for i in range(NYL)])  18.4 us
    ppermute x3, starting transfers between devices, per_device(): pieces[m] = lax.ppermute(pieces[m], 'yl', [(i, i ^ m) for i in range(NYL)])  9.21 us
    pallas_call x1, Pallas kernels, act_call(): pl.pallas_call(act_body, out_shape=jax.ShapeDtypeStruct((NZ, units, SLOTS...  7.42 us
    reshape x1, local copies, waits for them, and re-layouts, per_device(): both = both.reshape(NZC * DEPTH, both.shape[2]).T  6.36 us
    all_gather x1, waiting for transfers between devices, per_device(): features = lax.all_gather(block, ('z', 'c'), axis=0, tiled=True)  5.84 us
  transfers between devices with their start and end apart: 5, of which 4 were waited for; matrix products, arithmetic and copies ran while one was open for 7% of the time, Pallas kernels for 1%

profile of v2, /device:TPU:8, one launch (start us, length us, event | category | flops | bytes accessed | tf_op | source)
XLA Modules:
  0.0 166.7 jit_solution(712304027862437241)
XLA Ops:
  6.5 0.7 copy-done.5
  7.3 0.7 copy-done.7
  8.0 0.7 copy-done.8
  8.9 27.6 %all_to_all.15 = bf16[32,64,128]{2,1,0:T(8,128)(2,1)S(1)} all-to-all(bf16[32,64,128]{2,1,0:T(8,128)(2,1)S(1)} %bitcast.35), channel_id=1, replica_groups=mesh['x'=4,'yh'=2,'yl'=4,'z'=8,'c'=2] {'x','yh','yl'}, dimensions={0} | all-to-all | bytes 1048576 | tf_op jit(solution)/shard_map/rows_over_xy/all_to_all | solution.py:213
  36.5 1.2 shard_map.74
  37.9 1.4 copy-done.4
  39.9 1.9 %collective-permute-start = (bf16[96,2048]{1,0:T(8,128)(2,1)S(1)}, bf16[96,2048]{1,0:T(8,128)(2,1)S(1)}, u32[]{:S(2)}, u32[]{:S(2)}) collective-permute-start(bf16[96,2048]{1,0:T(8,128)(2,1)S(1)} %get-tuple-element.20), channel_id=1, source_target_pairs={{0,16},{16,0},{32,48},{48,32},{1,17},{17,1},{33,49},{49,33},{2,18}... | collective-permute-start | bytes 1179656 | tf_op jit(solution)/shard_map/down_over_y/ppermute | solution.py:230
  41.8 3.8 %collective-permute-start.1 = (bf16[96,2048]{1,0:T(8,128)(2,1)S(1)}, bf16[96,2048]{1,0:T(8,128)(2,1)S(1)}, u32[]{:S(2)}, u32[]{:S(2)}) collective-permute-start(bf16[96,2048]{1,0:T(8,128)(2,1)S(1)} %get-tuple-element.21), channel_id=1, source_target_pairs={{0,32},{16,48},{32,0},{48,16},{1,33},{17,49},{33,1},{49,17},{2,34}... | collective-permute-start | bytes 1179656 | tf_op jit(solution)/shard_map/down_over_y/ppermute | solution.py:230
  45.7 3.5 %collective-permute-start.2 = (bf16[96,2048]{1,0:T(8,128)(2,1)S(1)}, bf16[96,2048]{1,0:T(8,128)(2,1)S(1)}, u32[]{:S(2)}, u32[]{:S(2)}) collective-permute-start(bf16[96,2048]{1,0:T(8,128)(2,1)S(1)} %get-tuple-element.22), channel_id=1, source_target_pairs={{0,48},{16,32},{32,16},{48,0},{1,49},{17,33},{33,17},{49,1},{2,50}... | collective-permute-start | bytes 1179656 | tf_op jit(solution)/shard_map/down_over_y/ppermute | solution.py:230
  49.2 1.6 copy.11
  51.2 3.0 %fusion.4 = bf16[16,400,272]{2,1,0:T(8,128)(2,1)} fusion(bf16[16,384,128]{2,1,0:T(8,128)(2,1)S(1)} %bitcast.43, bf16[16,384,128]{2,1,0:T(8,128)(2,1)S(1)} %bitcast.42, bf16[16,400,16]{2,1,0:T(8,128)(2,1)S(1)} %broadcast_in_dim.10), kind=kLoop, calls=%fused_computation.7 | loop fusion | flops 20889600 | bytes 6832128 | tf_op jit(solution)/shard_map/concatenate | solution.py:241
  54.2 6.4 %copy.14 = bf16[6400,272]{0,1:T(8,128)(2,1)} copy(bf16[6400,272]{1,0:T(8,128)(2,1)} %bitcast.40) | data formatting | bytes 6963200 | tf_op jit(solution)/shard_map/reshape | solution.py:242
  60.6 11.2 %collective-permute-done.1.refs_2_ = bf16[96,2048]{1,0:T(8,128)(2,1)S(1)} collective-permute-done((bf16[96,2048]{1,0:T(8,128)(2,1)S(1)}, bf16[96,2048]{1,0:T(8,128)(2,1)S(1)}, u32[]{:S(2)}, u32[]{:S(2)}) %collective-permute-start.1) | collective-permute-done | bytes 393248 | tf_op jit(solution)/shard_map/down_over_y/ppermute | solution.py:230
  71.8 7.2 %collective-permute-done.2.refs_3_ = bf16[96,2048]{1,0:T(8,128)(2,1)S(1)} collective-permute-done((bf16[96,2048]{1,0:T(8,128)(2,1)S(1)}, bf16[96,2048]{1,0:T(8,128)(2,1)S(1)}, u32[]{:S(2)}, u32[]{:S(2)}) %collective-permute-start.2) | collective-permute-done | bytes 393248 | tf_op jit(solution)/shard_map/down_over_y/ppermute | solution.py:230
  79.0 1.1 shard_map.76
  80.1 1.0 copy-done
  81.1 1.0 copy-done.2
  82.0 5.8 %all-gather.2.cloned.1.call-done.x_ref = bf16[6400,512]{1,0:T(8,128)(2,1)} async-done(((bf16[400,512]{1,0:T(8,128)(2,1)}), bf16[6400,512]{1,0:T(8,128)(2,1)}) %all-gather.2.cloned.1.call-update) | async-done | bytes 6553616 | tf_op jit(solution)/shard_map/features_over_zc/all_gather | solution.py:223
  87.9 7.4 %shard_map.77 = bf16[8,128,512]{2,1,0:T(8,128)(2,1)} custom-call(bf16[272,6400]{1,0:T(8,128)(2,1)} %bitcast.41, bf16[6400,512]{1,0:T(8,128)(2,1)} %all-gather.2.cloned.1.call-done.x_ref, bf16[384,1024]{1,0:T(8,128)(2,1)} %copy-done.2, bf16[384,1024]{1,0:T(8,128)(2,1)} %copy-done), custom_call_target="tpu_custom_call" | custom-call | flops 1782579200 | bytes 10000000 | tf_op jit(solution)/shard_map/pallas_call | solution.py:121
  95.3 33.4 %all_to_all.16 = bf16[8,128,512]{2,1,0:T(8,128)(2,1)S(1)} all-to-all(bf16[8,128,512]{2,1,0:T(8,128)(2,1)} %shard_map.77), channel_id=1, replica_groups=mesh['x'=4,'yh'=2,'yl'=4,'z'=8,'c'=2] {'z'}, dimensions={0} | all-to-all | bytes 2097152 | tf_op jit(solution)/shard_map/units_over_z/all_to_all | solution.py:246
  128.7 1.9 %collective-permute-start.3 = (bf16[1024,512]{1,0:T(8,128)(2,1)S(1)}, bf16[1024,512]{1,0:T(8,128)(2,1)S(1)}, u32[]{:S(2)}, u32[]{:S(2)}) collective-permute-start(bf16[1024,512]{1,0:T(8,128)(2,1)S(1)} %bitcast.29), channel_id=1, source_target_pairs={{0,1},{1,0},{2,3},{3,2},{4,5},{5,4},{6,7},{7,6},{8,9},{9,8},{10,11... | collective-permute-start | bytes 3145736 | tf_op jit(solution)/shard_map/units_over_c/ppermute | solution.py:249
  131.2 2.0 %collective-permute-done.3.x_ref = bf16[1024,512]{1,0:T(8,128)(2,1)S(1)} collective-permute-done((bf16[1024,512]{1,0:T(8,128)(2,1)S(1)}, bf16[1024,512]{1,0:T(8,128)(2,1)S(1)}, u32[]{:S(2)}, u32[]{:S(2)}) %collective-permute-start.3) | collective-permute-done | bytes 1048608 | tf_op jit(solution)/shard_map/units_over_c/ppermute | solution.py:249
  133.9 25.0 %all_to_all.17 = bf16[32,48,128]{2,1,0:T(8,128)(2,1)S(1)} all-to-all(bf16[32,48,128]{2,1,0:T(8,128)(2,1)S(1)} %bitcast.34), channel_id=1, replica_groups=mesh['x'=4,'yh'=2,'yl'=4,'z'=8,'c'=2] {'x','yh','yl'}, dimensions={0} | all-to-all | bytes 786432 | tf_op jit(solution)/shard_map/out_over_xy/all_to_all | solution.py:266
  158.8 1.0 shard_map.80
  (25 shorter events, 2.8 us)
Async XLA Ops:
  6.5 81.3 %all-gather.2.cloned.1.call-start = ((), (), s32[]{:S(2)}) async-start(), calls=%async_computation.3 | async-start | bytes 6963200 | tf_op jit(solution)/shard_map/features_over_zc/all_gather | solution.py:223
  6.5 0.7 copy-start.5
  7.3 0.7 copy-start.7
  8.0 0.7 copy-start.8
  37.9 1.4 copy-start.4
  39.3 11.5 %copy-start.9 = (bf16[1,6144,128]{2,1,0:T(8,128)(2,1)S(1)}, bf16[1,6144,128]{2,1,0:T(8,128)(2,1)}, u32[]{:S(2)}) copy-start(bf16[1,6144,128]{2,1,0:T(8,128)(2,1)} %param.12) | copy-start | bytes 4718596
  39.9 20.7 %collective-permute-start = (bf16[96,2048]{1,0:T(8,128)(2,1)S(1)}, bf16[96,2048]{1,0:T(8,128)(2,1)S(1)}, u32[]{:S(2)}, u32[]{:S(2)}) collective-permute-start(bf16[96,2048]{1,0:T(8,128)(2,1)S(1)} %get-tuple-element.20), channel_id=1, source_target_pairs={{0,16},{16,0},{32,48},{48,32},{1,17},{17,1},{33,49},{49,33},{2,18}... | collective-permute-start | bytes 1179656 | tf_op jit(solution)/shard_map/down_over_y/ppermute | solution.py:230
  41.8 29.9 %collective-permute-start.1 = (bf16[96,2048]{1,0:T(8,128)(2,1)S(1)}, bf16[96,2048]{1,0:T(8,128)(2,1)S(1)}, u32[]{:S(2)}, u32[]{:S(2)}) collective-permute-start(bf16[96,2048]{1,0:T(8,128)(2,1)S(1)} %get-tuple-element.21), channel_id=1, source_target_pairs={{0,32},{16,48},{32,0},{48,16},{1,33},{17,49},{33,1},{49,17},{2,34}... | collective-permute-start | bytes 1179656 | tf_op jit(solution)/shard_map/down_over_y/ppermute | solution.py:230
  45.7 33.3 %collective-permute-start.2 = (bf16[96,2048]{1,0:T(8,128)(2,1)S(1)}, bf16[96,2048]{1,0:T(8,128)(2,1)S(1)}, u32[]{:S(2)}, u32[]{:S(2)}) collective-permute-start(bf16[96,2048]{1,0:T(8,128)(2,1)S(1)} %get-tuple-element.22), channel_id=1, source_target_pairs={{0,48},{16,32},{32,16},{48,0},{1,49},{17,33},{33,17},{49,1},{2,50}... | collective-permute-start | bytes 1179656 | tf_op jit(solution)/shard_map/down_over_y/ppermute | solution.py:230
  80.1 1.0 copy-start
  81.1 1.0 copy-start.2
  87.9 42.7 %copy-start.3 = (bf16[384,1024]{1,0:T(8,128)(2,1)S(1)}, bf16[384,1024]{1,0:T(8,128)(2,1)}, u32[]{:S(2)}) copy-start(bf16[384,1024]{1,0:T(8,128)(2,1)} %copy-done.2) | copy-start | bytes 2359300
  95.3 37.9 %copy-start.1 = (bf16[384,1024]{1,0:T(8,128)(2,1)S(1)}, bf16[384,1024]{1,0:T(8,128)(2,1)}, u32[]{:S(2)}) copy-start(bf16[384,1024]{1,0:T(8,128)(2,1)} %copy-done) | copy-start | bytes 2359300
  95.3 63.5 %copy-start.6 = (f32[128,2]{0,1:T(2,128)S(1)}, f32[128,2]{0,1:T(2,128)}, u32[]{:S(2)}) copy-start(f32[128,2]{0,1:T(2,128)} %param.10) | copy-start | bytes 3076
  128.7 4.5 %collective-permute-start.3 = (bf16[1024,512]{1,0:T(8,128)(2,1)S(1)}, bf16[1024,512]{1,0:T(8,128)(2,1)S(1)}, u32[]{:S(2)}, u32[]{:S(2)}) collective-permute-start(bf16[1024,512]{1,0:T(8,128)(2,1)S(1)} %bitcast.29), channel_id=1, source_target_pairs={{0,1},{1,0},{2,3},{3,2},{4,5},{5,4},{6,7},{7,6},{8,9},{9,8},{10,11... | collective-permute-start | bytes 3145736 | tf_op jit(solution)/shard_map/units_over_c/ppermute | solution.py:249
Sparse Core Ops, SparseCore 0:
  37.9 49.9 all-gather.1

commit v3 on v2

v3 whole, which is shorter than its diff:
```python
import functools

import jax
import jax.numpy as jnp
from jax import lax
from jax.experimental import pallas as pl
from jax.experimental.pallas import tpu as pltpu
from jax.sharding import Mesh, PartitionSpec as P

D = 6144
EXPERTS = 8
NX, NYH, NYA, NYB, NZ, NC = 4, 2, 2, 2, 8, 2
NYL = NYA * NYB
NZC = NZ * NC
FEATS = 96
GROUP = NYA * NC
ROW_DEV = 128
CAP = 64
PIECE = CAP // NC
SLOTS = EXPERTS * PIECE
EXTRA = 16
TILES = GROUP * FEATS // 128
PARTS = SLOTS // 128 * EXTRA
DEPTH = TILES * SLOTS + PARTS
PACK = 128 // PIECE
BF = jnp.bfloat16
F32 = jnp.float32
I32 = jnp.int32
BIG = 3.0e38
NT = (((1,), (1,)), ((), ()))
VMEM_LIMIT = 40 * 1024 * 1024


def iota(shape, dim):
    return lax.broadcasted_iota(I32, shape, dim)


def one_hot(condition):
    return jnp.where(condition, 1.0, 0.0).astype(BF)


def dot(a, b, dims=(((1,), (0,)), ((), ()))):
    return lax.dot_general(a, b, dims, preferred_element_type=F32)


def call(body, out_shape, *args, flops=1_000_000, moved=1_000_000, scalars=0, after=(), **kw):
    specs = [pl.BlockSpec(memory_space=pltpu.SMEM)] * scalars
    specs += [pl.BlockSpec(memory_space=pltpu.VMEM)] * (len(args) - scalars)
    specs += [pl.BlockSpec(memory_space=pl.ANY)] * len(after)
    return pl.pallas_call(
        body,
        out_shape=out_shape,
        in_specs=specs,
        out_specs=jax.tree.map(lambda _: pl.BlockSpec(memory_space=pltpu.VMEM), out_shape),
        compiler_params=pltpu.CompilerParams(vmem_limit_bytes=VMEM_LIMIT),
        cost_estimate=pl.CostEstimate(flops=flops, bytes_accessed=moved, transcendentals=0),
        **kw,
    )(*args, *after)


def dispatch_body(hidden_ref, gain_ref, routes_ref, out_ref, target_ref):
    diagonal = iota((FEATS, FEATS), 0) == iota((FEATS, FEATS), 1)
    gain = jnp.sum(jnp.where(diagonal, gain_ref[...].astype(F32), 0.0), axis=1, keepdims=True)
    values = hidden_ref[...].astype(F32)
    scaled = jnp.clip(values * gain, -BIG, BIG)
    squares = jnp.minimum(jnp.sum(values * values, axis=0, keepdims=True), BIG)
    hi = squares.astype(BF).astype(F32)
    mid = (squares - hi).astype(BF).astype(F32)
    low = squares - hi - mid
    row = iota((ROW_DEV - FEATS, ROW_DEV), 0)
    parts = jnp.where(row == 0, hi, jnp.where(row == 1, mid, jnp.where(row == 2, low, 0.0)))
    rows = jnp.concatenate([scaled, parts], axis=0).astype(BF)

    first, second = routes_ref[0:1, :], routes_ref[1:2, :]
    expert = iota((2 * EXPERTS, ROW_DEV), 0)
    named0, named1 = expert == first, expert == second
    earlier = one_hot(iota((ROW_DEV, ROW_DEV), 0) < iota((ROW_DEV, ROW_DEV), 1))
    before = dot(one_hot(named0 | named1), earlier)
    rank0 = jnp.sum(jnp.where(named0, before, 0.0), axis=0, keepdims=True).astype(I32)
    rank1 = jnp.sum(jnp.where(named1, before, 0.0), axis=0, keepdims=True).astype(I32)
    target0, target1 = first * CAP + rank0, second * CAP + rank1
    target_ref[...] = jnp.where(iota((8, ROW_DEV), 0) == 0, target0, target1)
    slot = iota((EXPERTS * CAP, ROW_DEV), 0)
    place = one_hot((slot == target0) | (slot == target1))
    sent = dot(place, rows, NT).astype(BF).reshape(EXPERTS, NC, PIECE, ROW_DEV)
    for j in range(NYA):
        out_ref[:, j] = sent


def turn_body(in_ref, out_ref, turned_ref):
    row, lane = iota((EXTRA, ROW_DEV), 0), iota((EXTRA, ROW_DEV), 1)
    source, column = iota((ROW_DEV, ROW_DEV), 0), iota((ROW_DEV, ROW_DEV), 1)
    extra = jnp.zeros((EXTRA, SLOTS), F32)
    rows = [in_ref[:, j].reshape(SLOTS, ROW_DEV) for j in range(GROUP)]
    for t in range(TILES):
        tile = jnp.zeros((SLOTS, ROW_DEV), F32)
        for j in range(GROUP):
            shift = t * ROW_DEV - j * FEATS
            if -ROW_DEV < shift < FEATS:
                pick = one_hot((source - column == shift) & (source < FEATS))
                tile += dot(rows[j], pick)
        turned_ref[t * SLOTS : (t + 1) * SLOTS, :] = tile.astype(BF)
    for j in range(GROUP):
        pick = one_hot((row - 3 * j == lane - FEATS) & (row >= 3 * j) & (row < 3 * j + 3))
        extra += dot(pick, rows[j], NT)
    for t in range(SLOTS // 128):
        start = TILES * SLOTS + t * EXTRA
        turned_ref[start : start + EXTRA, :] = extra[:, t * 128 : (t + 1) * 128].astype(BF)
    for z in range(NZ):
        out_ref[z] = turned_ref[...]


def halves_body(place_ref, gate_ref, up_ref, own_ref, other_ref):
    parity = place_ref[NYL + 1]
    for i, ref in enumerate((gate_ref, up_ref)):
        for j in range(NYA):
            own_ref[i, j] = ref[j, parity]
            other_ref[i, j] = ref[j, 1 - parity]


def products(x_ref, weight_refs, acc_ref):
    for z in range(0, NZ, 2):
        tiles, columns = [], []
        for i in range(z, z + 2):
            tiles += [x_ref[i, t * SLOTS : (t + 1) * SLOTS, :] for t in range(TILES)]
            weights = [w[k, :, i].reshape(GROUP * FEATS, 128) for w in weight_refs for k in range(2)]
            columns.append(jnp.concatenate(weights, axis=1))
        total = dot(jnp.concatenate(tiles, axis=1), jnp.concatenate(columns, axis=0))
        if z == 0:
            acc_ref[...] = total
        else:
            acc_ref[...] += total


def sums_of_squares(x_ref):
    parts = jnp.zeros((PARTS, 128), F32)
    for z in range(NZ):
        parts += x_ref[z, TILES * SLOTS :, :].astype(F32)
    sums = [
        jnp.sum(parts[t * EXTRA : (t + 1) * EXTRA], axis=0, keepdims=True) for t in range(SLOTS // 128)
    ]
    return jnp.concatenate(sums, axis=1)


def neighbour_body(w_ref, w2_ref, x_ref, out_ref, acc_ref):
    products(x_ref, (w_ref, w2_ref), acc_ref)
    out_ref[:SLOTS, :] = acc_ref[...].astype(BF)
    squares = jnp.minimum(sums_of_squares(x_ref), BIG)
    hi = squares.astype(BF).astype(F32)
    mid = (squares - hi).astype(BF).astype(F32)
    row = iota((EXTRA, SLOTS), 0)
    parts = jnp.where(row == 0, hi, jnp.where(row == 1, mid, squares - hi - mid))
    parts = jnp.where(row < 3, parts, 0.0).astype(BF)
    out_ref[SLOTS:, :] = jnp.concatenate([parts, parts], axis=1)


def own_body(w_ref, w2_ref, x_ref, out_ref, squares_ref):
    products(x_ref, (w_ref, w2_ref), out_ref)
    squares_ref[...] = jnp.broadcast_to(sums_of_squares(x_ref), (8, SLOTS))


def act_body(own_ref, squares_ref, got_ref, out_ref):
    diagonal = iota((128, 128), 0) == iota((128, 128), 1)
    got = jnp.sum(got_ref[SLOTS:, :SLOTS].astype(F32), axis=0, keepdims=True)
    squares = squares_ref[0:1, :] + got
    for t in range(SLOTS // 128):
        rows = slice(t * 128, (t + 1) * 128)
        column = jnp.sum(jnp.where(diagonal, squares[:, rows], 0.0), axis=1, keepdims=True)
        inv_rms = lax.rsqrt(column / D + 1e-05)
        hidden = (own_ref[rows, :] + got_ref[rows, :].astype(F32)) * inv_rms
        for k in range(NC):
            gate = hidden[:, 256 * k : 256 * k + 128]
            up = hidden[:, 256 * k + 128 : 256 * k + 256]
            act = (gate / (1.0 + jnp.exp(-gate)) * up).astype(BF)
            for z in range(NZ):
                out_ref[z, rows, 128 * k : 128 * (k + 1)] = act


def down_body(place_ref, own_ref, other_ref, x_ref, out_ref):
    rows = FEATS // PACK
    group = iota((rows, 128), 1) // PIECE
    core = place_ref[NYL]
    for k, w_ref in enumerate((own_ref, other_ref)):
        out = jnp.zeros((w_ref.shape[0], SLOTS), F32)
        for z in range(NZ):
            units = x_ref[z]
            if k == 1:
                units = jnp.concatenate([units[:, 128:], units[:, :128]], axis=1)
            out += dot(w_ref[:, z * 256 : (z + 1) * 256], units, NT)
        to = core if k == 0 else 1 - core
        for j in range(NYL):
            for t in range(EXPERTS // PACK):
                tile = out[j * FEATS : (j + 1) * FEATS, t * 128 : (t + 1) * 128]
                for i in range(PACK):
                    packed = jnp.zeros((rows, 128), F32)
                    for q in range(PACK):
                        part = tile[q * rows : (q + 1) * rows, :]
                        shift = (q - i) % PACK * PIECE
                        part = pltpu.roll(part, shift, 1) if shift else part
                        packed = jnp.where(group == q, part, packed)
                    out_ref[t * PACK + i, j, to] = packed.astype(BF)


def combine_body(target_ref, gates_ref, in_ref, out_ref):
    rows = FEATS // PACK
    target = jnp.concatenate([target_ref[0:1, :], target_ref[1:2, :]], axis=1)
    slot = iota((128, 2 * ROW_DEV), 0) % PIECE
    group = iota((rows, 128), 1) // PIECE
    picked = jnp.zeros((FEATS, 2 * ROW_DEV), F32)
    for e in range(EXPERTS):
        for h in range(NC):
            place = one_hot(target - (e * CAP + h * PIECE) == slot)
            total = in_ref[e, 0, h].astype(F32)
            for j in range(1, NYL):
                total += in_ref[e, j, h].astype(F32)
            total = jnp.concatenate([jnp.where(group == q, total, 0.0) for q in range(PACK)], axis=0)
            hi = total.astype(BF)
            rest = (total - hi.astype(F32)).astype(BF)
            picked += dot(hi, place) + dot(rest, place)
    mixed = gates_ref[0:1, :] * picked[:, :ROW_DEV] + gates_ref[1:2, :] * picked[:, ROW_DEV:]
    out_ref[...] = mixed.astype(BF)


def cut_body(place_ref, in_ref, *out_refs):
    width = out_refs[0].shape[1]
    for m, out_ref in enumerate(out_refs):
        start = pl.multiple_of(place_ref[m] * width, width)
        out_ref[...] = in_ref[:, pl.ds(start, width)]


def join_body(place_ref, *refs):
    pieces, out_ref = refs[:NYL], refs[NYL]
    core = place_ref[NYL]
    for m, piece in enumerate(pieces):
        rows = pl.ds(pl.multiple_of(place_ref[m] * FEATS, FEATS), FEATS)
        for z in range(NZ):
            for k, at in enumerate((core, 1 - core)):
                cols = pl.ds(pl.multiple_of((2 * z + at) * 128, 128), 128)
                start = (2 * z + k) * 128
                out_ref[rows, start : start + 128] = piece[:, cols]


def per_device(hidden_state, norm_gain, routes, gates, w_gate, w_up, w_down):
    quarter = 2 * lax.axis_index("ya") + lax.axis_index("yb")
    core = lax.axis_index("c")
    swap = [(0, 1), (1, 0)]
    places = [quarter ^ m for m in range(NYL)] + [core, lax.axis_index("yb")]
    places = jnp.stack(places).astype(I32)

    outgoing, targets = call(
        dispatch_body,
        (
            jax.ShapeDtypeStruct((EXPERTS, NYA, NC, PIECE, ROW_DEV), BF),
            jax.ShapeDtypeStruct((8, ROW_DEV), I32),
        ),
        hidden_state.T,
        norm_gain[None, :],
        routes.T,
    )
    with jax.named_scope("rows_over_xyc"):
        incoming = lax.all_to_all(
            outgoing.reshape(EXPERTS * GROUP, PIECE, ROW_DEV),
            ("x", "yh", "ya", "c"),
            split_axis=0,
            concat_axis=0,
            tiled=True,
        )
    incoming = incoming.reshape(EXPERTS, GROUP, PIECE, ROW_DEV)
    block = call(
        turn_body,
        jax.ShapeDtypeStruct((NZ, DEPTH, 128), BF),
        incoming,
        scratch_shapes=[pltpu.VMEM((DEPTH, 128), BF)],
    )
    with jax.named_scope("features_over_z"):
        features = lax.all_to_all(block, "z", split_axis=0, concat_axis=0, tiled=True)

    split = (NYA, NYB, NZ, NC * FEATS, 128)
    half = jax.ShapeDtypeStruct((2, NYA, NZ, NC * FEATS, 128), BF)
    gate_cols, up_cols = w_gate[0].reshape(split), w_up[0].reshape(split)
    w_own, w_sent = call(halves_body, (half, half), places, gate_cols, up_cols, scalars=1)
    w_sent, _ = lax.optimization_barrier((w_sent, block))
    with jax.named_scope("gate_up_over_y"):
        w_next = lax.ppermute(w_sent, "yb", swap)
    down = w_down[0]
    units = down.shape[0] // NYL
    piece = jax.ShapeDtypeStruct((FEATS, units), BF)
    pieces = list(call(cut_body, (piece,) * NYL, places, down.T, scalars=1))

    def over_y(m, after):
        sent, _ = lax.optimization_barrier((pieces[m], after))
        with jax.named_scope("down_over_y"):
            return lax.ppermute(sent, ("ya", "yb"), [(i, i ^ m) for i in range(NYL)])

    pieces[2] = over_y(2, block)
    w_next, pieces[2] = lax.optimization_barrier((w_next, pieces[2]))
    pieces[1] = over_y(1, w_next)
    with jax.named_scope("gate_up_over_c"):
        w_core = lax.ppermute(w_own, "c", swap)
        w_next_core = lax.ppermute(w_next, "c", swap)

    flops = 2 * SLOTS * D // 2 * 512
    sent = call(
        neighbour_body,
        jax.ShapeDtypeStruct((SLOTS + EXTRA, 512), BF),
        w_next,
        w_next_core,
        features,
        flops=flops,
        moved=5_000_000,
        scratch_shapes=[pltpu.VMEM((SLOTS, 512), F32)],
    )
    with jax.named_scope("hidden_over_y"):
        got = lax.ppermute(sent, "yb", swap)
    own, squares = call(
        own_body,
        (jax.ShapeDtypeStruct((SLOTS, 512), F32), jax.ShapeDtypeStruct((8, SLOTS), F32)),
        w_own,
        w_core,
        features,
        flops=flops,
        moved=5_000_000,
    )
    acts = call(act_body, jax.ShapeDtypeStruct((NZ, SLOTS, 256), BF), own, squares, got)
    with jax.named_scope("units_over_z"):
        acts = lax.all_to_all(acts, "z", split_axis=0, concat_axis=0, tiled=True)

    pieces[3] = over_y(3, own)
    part = jax.ShapeDtypeStruct((NYL * FEATS, units), BF)
    down_own = call(join_body, part, places, *pieces, scalars=1)
    with jax.named_scope("down_over_c"):
        down_other = lax.ppermute(down_own, "c", swap)

    rows = FEATS // PACK
    out = call(
        down_body,
        jax.ShapeDtypeStruct((EXPERTS, NYL, NC, rows, 128), BF),
        places,
        down_own,
        down_other,
        acts,
        scalars=1,
        flops=2 * NC * NYL * FEATS * units * SLOTS,
        moved=5_000_000,
    )
    with jax.named_scope("out_over_xyc"):
        back = lax.all_to_all(
            out.reshape(EXPERTS * NYL * NC, rows, 128),
            ("x", "yh", "ya", "yb", "c"),
            split_axis=0,
            concat_axis=0,
            tiled=True,
        )
    back = back.reshape(EXPERTS, NYL, NC, rows, 128)
    return call(
        combine_body, jax.ShapeDtypeStruct((FEATS, ROW_DEV), BF), targets, gates.T, back
    ).T


def solution(mesh):
    fine = Mesh(
        mesh.devices.reshape(NX, NYH, NYA, NYB, NZ, NC), ("x", "yh", "ya", "yb", "z", "c")
    )
    exp, tp = ("x", "yh"), ("ya", "yb", "z", "c")
    in_specs = (
        P(exp, tp),
        P(tp),
        P(exp, None),
        P(exp, None),
        P(exp, None, tp),
        P(exp, None, tp),
        P(exp, None, tp),
    )
    return jax.shard_map(
        per_device, mesh=fine, in_specs=in_specs, out_specs=P(exp, tp), check_vma=False
    )
```

time: 167 us -> 161 us (0.964)
  the two profiles are of different devices: /device:TPU:8 before, /device:TPU:1 now
where the time goes in v3:
time: 161 us
  waiting for transfers between devices  56.2 us (35%)
  starting transfers between devices  54.5 us (34%)
  blocking collectives  20.1 us (12%)
  Pallas kernels  17.3 us (11%)
  local copies, waits for them, and re-layouts  12.3 us (8%)
    ppermute x3, waiting for transfers between devices, over_y(): return lax.ppermute(sent, ('ya', 'yb'), [(i, i ^ m) for i in range(NYL)])  29.6 us
    all_to_all x1, blocking collectives, per_device(): lax.all_to_all(out.reshape(EXPERTS * NYL * NC, rows, 128), ('x', 'yh', 'y...  20.1 us
    pallas_call x10, Pallas kernels, call(): pl.pallas_call(body, out_shape=out_shape, in_specs=specs, out_specs=jax.t...  17.3 us
    all_to_all x1, waiting for transfers between devices, per_device(): acts = lax.all_to_all(acts, 'z', split_axis=0, concat_axis=0, tiled=True)  13.2 us
    unnamed x32, local copies, waits for them, and re-layouts  12.2 us
    all_to_all x1, starting transfers between devices, per_device(): lax.all_to_all(outgoing.reshape(EXPERTS * GROUP, PIECE, ROW_DEV), ('x', '...  11.2 us
    all_to_all x1, starting transfers between devices, per_device(): lax.all_to_all(block, 'z', split_axis=0, concat_axis=0, tiled=True)  10 us
    all_to_all x1, starting transfers between devices, per_device(): acts = lax.all_to_all(acts, 'z', split_axis=0, concat_axis=0, tiled=True)  10 us
  transfers between devices with their start and end apart: 11, of which 8 were waited for; matrix products, arithmetic and copies ran while one was open for 0% of the time, Pallas kernels for 7%

profile of v3, /device:TPU:1, one launch (start us, length us, event | category | flops | bytes accessed | tf_op | source)
XLA Modules:
  0.0 160.7 jit_solution(6973369863595945203)
XLA Ops:
  3.1 11.2 %all-to-all-start = ((bf16[32,32,128]{2,1,0:T(8,128)(2,1)}), bf16[32,32,128]{2,1,0:T(8,128)(2,1)S(1)}, u32[]{:S(2)}, u32[]{:S(2)}) async-start(bf16[32,32,128]{2,1,0:T(8,128)(2,1)} %bitcast.14), calls=%async_computation | async-start | bytes 524288 | tf_op jit(solution)/shard_map/rows_over_xyc/all_to_all | solution.py:261
  17.2 1.9 %shard_map.75 = (bf16[2,2,8,192,128]{4,3,2,1,0:T(8,128)(2,1)}, bf16[2,2,8,192,128]{4,3,2,1,0:T(8,128)(2,1)S(1)}) custom-call(s32[6]{0:T(128)S(1)} %stack.27.place_ref, bf16[2,2,8,192,128]{4,3,2,1,0:T(8,128)(2,1)S(1)} %bitcast.23, bf16[2,2,8,192,128]{4,3,2,1,0:T(8,128)(2,1)S(1)} %bitcast.24), custom_call_target="tpu_custom_call" | custom-call | flops 1000000 | bytes 1000000 | tf_op jit(solution)/shard_map/pallas_call | solution.py:50
  19.1 8.3 %all-to-all-done = bf16[32,32,128]{2,1,0:T(8,128)(2,1)S(1)} async-done(((bf16[32,32,128]{2,1,0:T(8,128)(2,1)}), bf16[32,32,128]{2,1,0:T(8,128)(2,1)S(1)}, u32[]{:S(2)}, u32[]{:S(2)}) %all-to-all-start) | async-done | bytes 262176 | tf_op jit(solution)/shard_map/rows_over_xyc/all_to_all | solution.py:261
  27.4 1.7 %shard_map.76 = bf16[8,800,128]{2,1,0:T(8,128)(2,1)} custom-call(bf16[8,4,32,128]{3,2,1,0:T(8,128)(2,1)S(1)} %bitcast.25), custom_call_target="tpu_custom_call" | custom-call | flops 1000000 | bytes 1000000 | tf_op jit(solution)/shard_map/pallas_call | solution.py:50
  29.1 2.1 %collective-permute-start = (bf16[2,2,8,192,128]{4,3,2,1,0:T(8,128)(2,1)}, bf16[2,2,8,192,128]{4,3,2,1,0:T(8,128)(2,1)S(1)}, u32[]{:S(2)}, u32[]{:S(2)}) collective-permute-start(bf16[2,2,8,192,128]{4,3,2,1,0:T(8,128)(2,1)} %copy-done.15), channel_id=1, source_target_pairs={{0,16},{16,0},{1,17},{17,1},{2,18},{18,2},{3,19},{19,3},{4,20},{20... | collective-permute-start | bytes 4718600 | tf_op jit(solution)/shard_map/gate_up_over_y/ppermute | solution.py:284
  31.2 10.0 %all-to-all-start.1 = ((bf16[8,800,128]{2,1,0:T(8,128)(2,1)}), bf16[8,800,128]{2,1,0:T(8,128)(2,1)S(1)}, u32[]{:S(2)}, u32[]{:S(2)}) async-start(bf16[8,800,128]{2,1,0:T(8,128)(2,1)} %shard_map.76), calls=%async_computation.1 | async-start | bytes 3276800 | tf_op jit(solution)/shard_map/features_over_z/all_to_all | solution.py:276
  42.6 1.6 shard_map.74
  45.0 3.0 %collective-permute-start.1 = (bf16[96,2048]{1,0:T(8,128)(2,1)S(1)}, bf16[96,2048]{1,0:T(8,128)(2,1)S(1)}, u32[]{:S(2)}, u32[]{:S(2)}) collective-permute-start(bf16[96,2048]{1,0:T(8,128)(2,1)S(1)} %get-tuple-element.28), channel_id=1, source_target_pairs={{0,32},{16,48},{32,0},{48,16},{1,33},{17,49},{33,1},{49,17},{2,34}... | collective-permute-start | bytes 1179656 | tf_op jit(solution)/shard_map/down_over_y/ppermute | solution.py:293
  48.0 25.4 %collective-permute-done.1.refs_2_ = bf16[96,2048]{1,0:T(8,128)(2,1)S(1)} collective-permute-done((bf16[96,2048]{1,0:T(8,128)(2,1)S(1)}, bf16[96,2048]{1,0:T(8,128)(2,1)S(1)}, u32[]{:S(2)}, u32[]{:S(2)}) %collective-permute-start.1) | collective-permute-done | bytes 393248 | tf_op jit(solution)/shard_map/down_over_y/ppermute | solution.py:293
  75.2 3.1 %collective-permute-start.6 = (bf16[2,2,8,192,128]{4,3,2,1,0:T(8,128)(2,1)S(1)}, bf16[2,2,8,192,128]{4,3,2,1,0:T(8,128)(2,1)}, u32[]{:S(2)}, u32[]{:S(2)}) collective-permute-start(bf16[2,2,8,192,128]{4,3,2,1,0:T(8,128)(2,1)S(1)} %collective-permute-done.w_ref), channel_id=1, source_target_pairs={{0,1},{1,0},{2,3},{3,2},{4,5},{5,4},{6,7},{7,6},{8,9},{9,8},{10,11... | collective-permute-start | bytes 4718600 | tf_op jit(solution)/shard_map/gate_up_over_c/ppermute | solution.py:300
  78.3 1.9 %collective-permute-start.3 = (bf16[2,2,8,192,128]{4,3,2,1,0:T(8,128)(2,1)}, bf16[2,2,8,192,128]{4,3,2,1,0:T(8,128)(2,1)}, u32[]{:S(2)}, u32[]{:S(2)}) collective-permute-start(bf16[2,2,8,192,128]{4,3,2,1,0:T(8,128)(2,1)} %get-tuple-element.33.w_ref), channel_id=1, source_target_pairs={{0,1},{1,0},{2,3},{3,2},{4,5},{5,4},{6,7},{7,6},{8,9},{9,8},{10,11... | collective-permute-start | bytes 4718600 | tf_op jit(solution)/shard_map/gate_up_over_c/ppermute | solution.py:299
  81.4 2.4 %shard_map.79 = bf16[272,512]{1,0:T(8,128)(2,1)S(1)} custom-call(bf16[2,2,8,192,128]{4,3,2,1,0:T(8,128)(2,1)S(1)} %collective-permute-done.w_ref, bf16[2,2,8,192,128]{4,3,2,1,0:T(8,128)(2,1)} %collective-permute-done.6.w2_ref, bf16[8,800,128]{2,1,0:T(8,128)(2,1)S(1)} %all-to-all-done.1.x_ref), custom_call_target="tpu_custom_call" | custom-call | flops 805306368 | bytes 5000000 | tf_op jit(solution)/shard_map/pallas_call | solution.py:50
  83.8 4.0 %collective-permute-start.7 = (bf16[272,512]{1,0:T(8,128)(2,1)S(1)}, bf16[272,512]{1,0:T(8,128)(2,1)S(1)}, u32[]{:S(2)}, u32[]{:S(2)}) collective-permute-start(bf16[272,512]{1,0:T(8,128)(2,1)S(1)} %shard_map.79), channel_id=1, source_target_pairs={{0,16},{16,0},{1,17},{17,1},{2,18},{18,2},{3,19},{19,3},{4,20},{20... | collective-permute-start | bytes 835592 | tf_op jit(solution)/shard_map/hidden_over_y/ppermute | solution.py:314
  87.9 1.9 %collective-permute-start.2 = (bf16[96,2048]{1,0:T(8,128)(2,1)}, bf16[96,2048]{1,0:T(8,128)(2,1)}, u32[]{:S(2)}, u32[]{:S(2)}) collective-permute-start(bf16[96,2048]{1,0:T(8,128)(2,1)} %get-tuple-element.30), channel_id=1, source_target_pairs={{0,16},{16,0},{32,48},{48,32},{1,17},{17,1},{33,49},{49,33},{2,18}... | collective-permute-start | bytes 1179656 | tf_op jit(solution)/shard_map/down_over_y/ppermute | solution.py:293
  89.8 2.9 %shard_map.77 = (f32[256,512]{1,0:T(8,128)S(1)}, f32[8,256]{1,0:T(8,128)S(1)}) custom-call(bf16[2,2,8,192,128]{4,3,2,1,0:T(8,128)(2,1)} %get-tuple-element.33.w_ref, bf16[2,2,8,192,128]{4,3,2,1,0:T(8,128)(2,1)} %collective-permute-done.3.w2_ref, bf16[8,800,128]{2,1,0:T(8,128)(2,1)S(1)} %all-to-all-done.1.x_ref), custom_call_target="tpu_custom_call" | custom-call | flops 805306368 | bytes 5000000 | tf_op jit(solution)/shard_map/pallas_call | solution.py:50
  92.7 2.9 %collective-permute-start.4 = (bf16[96,2048]{1,0:T(8,128)(2,1)}, bf16[96,2048]{1,0:T(8,128)(2,1)S(1)}, u32[]{:S(2)}, u32[]{:S(2)}) collective-permute-start(bf16[96,2048]{1,0:T(8,128)(2,1)} %get-tuple-element.35), channel_id=1, source_target_pairs={{0,48},{16,32},{32,16},{48,0},{1,49},{17,33},{33,17},{49,1},{2,50}... | collective-permute-start | bytes 1179656 | tf_op jit(solution)/shard_map/down_over_y/ppermute | solution.py:293
  96.8 10.0 %all-to-all-start.2 = ((bf16[8,256,256]{2,1,0:T(8,128)(2,1)}), bf16[8,256,256]{2,1,0:T(8,128)(2,1)S(1)}, u32[]{:S(2)}, u32[]{:S(2)}) async-start(bf16[8,256,256]{2,1,0:T(8,128)(2,1)} %shard_map.80), calls=%async_computation.2 | async-start | bytes 2097152 | tf_op jit(solution)/shard_map/units_over_z/all_to_all | solution.py:326
  106.9 4.1 %collective-permute-done.4.refs_3_ = bf16[96,2048]{1,0:T(8,128)(2,1)S(1)} collective-permute-done((bf16[96,2048]{1,0:T(8,128)(2,1)}, bf16[96,2048]{1,0:T(8,128)(2,1)S(1)}, u32[]{:S(2)}, u32[]{:S(2)}) %collective-permute-start.4) | collective-permute-done | bytes 393248 | tf_op jit(solution)/shard_map/down_over_y/ppermute | solution.py:293
  112.8 1.6 %shard_map.78.own_ref = bf16[384,2048]{1,0:T(8,128)(2,1)S(1)} custom-call(s32[6]{0:T(128)S(1)} %stack.27.place_ref, bf16[96,2048]{1,0:T(8,128)(2,1)S(1)} %copy-done.6, bf16[96,2048]{1,0:T(8,128)(2,1)} %collective-permute-done.2.refs_1_, bf16[96,2048]{1,0:T(8,128)(2,1)S(1)} %copy-done.8, bf16[96,2048]{1,0:T(8,128)(2,1)S(1)} %copy-done.10), custom_call_target="tpu_custom_call" | custom-call | flops 1000000 | bytes 1000000 | tf_op jit(solution)/shard_map/pallas_call | solution.py:50
  114.4 4.3 %collective-permute-start.5 = (bf16[384,2048]{1,0:T(8,128)(2,1)S(1)}, bf16[384,2048]{1,0:T(8,128)(2,1)S(1)}, u32[]{:S(2)}, u32[]{:S(2)}) collective-permute-start(bf16[384,2048]{1,0:T(8,128)(2,1)S(1)} %shard_map.78.own_ref), channel_id=1, source_target_pairs={{0,1},{1,0},{2,3},{3,2},{4,5},{5,4},{6,7},{7,6},{8,9},{9,8},{10,11... | collective-permute-start | bytes 4718600 | tf_op jit(solution)/shard_map/down_over_c/ppermute | solution.py:332
  118.7 3.0 %collective-permute-done.5.other_ref = bf16[384,2048]{1,0:T(8,128)(2,1)S(1)} collective-permute-done((bf16[384,2048]{1,0:T(8,128)(2,1)S(1)}, bf16[384,2048]{1,0:T(8,128)(2,1)S(1)}, u32[]{:S(2)}, u32[]{:S(2)}) %collective-permute-start.5) | collective-permute-done | bytes 1572896 | tf_op jit(solution)/shard_map/down_over_c/ppermute | solution.py:332
  122.9 13.2 %all-to-all-done.2.x_ref = bf16[8,256,256]{2,1,0:T(8,128)(2,1)S(1)} async-done(((bf16[8,256,256]{2,1,0:T(8,128)(2,1)}), bf16[8,256,256]{2,1,0:T(8,128)(2,1)S(1)}, u32[]{:S(2)}, u32[]{:S(2)}) %all-to-all-start.2) | async-done | bytes 1048608 | tf_op jit(solution)/shard_map/units_over_z/all_to_all | solution.py:326
  137.5 1.8 %shard_map.81 = bf16[8,4,2,24,128]{4,3,2,1,0:T(8,128)(2,1)S(1)} custom-call(s32[6]{0:T(128)S(1)} %stack.27.place_ref, bf16[384,2048]{1,0:T(8,128)(2,1)S(1)} %shard_map.78.own_ref, bf16[384,2048]{1,0:T(8,128)(2,1)S(1)} %copy-done.2, bf16[8,256,256]{2,1,0:T(8,128)(2,1)S(1)} %all-to-all-done.2.x_ref), custom_call_target="tpu_custom_call" | custom-call | flops 805306368 | bytes 5000000 | tf_op jit(solution)/shard_map/pallas_call | solution.py:50
  139.3 20.1 %all_to_all.20 = bf16[64,24,128]{2,1,0:T(8,128)(2,1)S(1)} all-to-all(bf16[64,24,128]{2,1,0:T(8,128)(2,1)S(1)} %bitcast.21), channel_id=1, replica_groups=mesh['x'=4,'yh'=2,'ya'=2,'yb'=2,'z'=8,'c'=2] {'x','yh','ya','yb','c'}, dimensions={0} | all-to-all | bytes 786432 | tf_op jit(solution)/shard_map/out_over_xyc/all_to_all | solution.py:347
  (42 shorter events, 17.9 us)
Async XLA Ops:
  3.1 24.3 %all-to-all-start = ((bf16[32,32,128]{2,1,0:T(8,128)(2,1)}), bf16[32,32,128]{2,1,0:T(8,128)(2,1)S(1)}, u32[]{:S(2)}, u32[]{:S(2)}) async-start(bf16[32,32,128]{2,1,0:T(8,128)(2,1)} %bitcast.14), calls=%async_computation | async-start | bytes 524288 | tf_op jit(solution)/shard_map/rows_over_xyc/all_to_all | solution.py:261
  14.4 1.4 copy-start.3
  15.8 1.4 copy-start.4
  19.1 9.9 %copy-start.15 = (bf16[2,2,8,192,128]{4,3,2,1,0:T(8,128)(2,1)}, bf16[2,2,8,192,128]{4,3,2,1,0:T(8,128)(2,1)S(1)}, u32[]{:S(2)}) copy-start(bf16[2,2,8,192,128]{4,3,2,1,0:T(8,128)(2,1)S(1)} %get-tuple-element.26) | copy-start | bytes 4718596
  29.1 46.1 %collective-permute-start = (bf16[2,2,8,192,128]{4,3,2,1,0:T(8,128)(2,1)}, bf16[2,2,8,192,128]{4,3,2,1,0:T(8,128)(2,1)S(1)}, u32[]{:S(2)}, u32[]{:S(2)}) collective-permute-start(bf16[2,2,8,192,128]{4,3,2,1,0:T(8,128)(2,1)} %copy-done.15), channel_id=1, source_target_pairs={{0,16},{16,0},{1,17},{17,1},{2,18},{18,2},{3,19},{19,3},{4,20},{20... | collective-permute-start | bytes 4718600 | tf_op jit(solution)/shard_map/gate_up_over_y/ppermute | solution.py:284
  31.2 49.5 %all-to-all-start.1 = ((bf16[8,800,128]{2,1,0:T(8,128)(2,1)}), bf16[8,800,128]{2,1,0:T(8,128)(2,1)S(1)}, u32[]{:S(2)}, u32[]{:S(2)}) async-start(bf16[8,800,128]{2,1,0:T(8,128)(2,1)} %shard_map.76), calls=%async_computation.1 | async-start | bytes 3276800 | tf_op jit(solution)/shard_map/features_over_z/all_to_all | solution.py:276
  41.2 1.4 copy-start
  44.2 0.8 copy-start.5
  45.0 28.4 %collective-permute-start.1 = (bf16[96,2048]{1,0:T(8,128)(2,1)S(1)}, bf16[96,2048]{1,0:T(8,128)(2,1)S(1)}, u32[]{:S(2)}, u32[]{:S(2)}) collective-permute-start(bf16[96,2048]{1,0:T(8,128)(2,1)S(1)} %get-tuple-element.28), channel_id=1, source_target_pairs={{0,32},{16,48},{32,0},{48,16},{1,33},{17,49},{33,1},{49,17},{2,34}... | collective-permute-start | bytes 1179656 | tf_op jit(solution)/shard_map/down_over_y/ppermute | solution.py:293
  73.4 0.8 copy-start.7
  75.2 6.3 %collective-permute-start.6 = (bf16[2,2,8,192,128]{4,3,2,1,0:T(8,128)(2,1)S(1)}, bf16[2,2,8,192,128]{4,3,2,1,0:T(8,128)(2,1)}, u32[]{:S(2)}, u32[]{:S(2)}) collective-permute-start(bf16[2,2,8,192,128]{4,3,2,1,0:T(8,128)(2,1)S(1)} %collective-permute-done.w_ref), channel_id=1, source_target_pairs={{0,1},{1,0},{2,3},{3,2},{4,5},{5,4},{6,7},{7,6},{8,9},{9,8},{10,11... | collective-permute-start | bytes 4718600 | tf_op jit(solution)/shard_map/gate_up_over_c/ppermute | solution.py:300
  78.3 11.5 %collective-permute-start.3 = (bf16[2,2,8,192,128]{4,3,2,1,0:T(8,128)(2,1)}, bf16[2,2,8,192,128]{4,3,2,1,0:T(8,128)(2,1)}, u32[]{:S(2)}, u32[]{:S(2)}) collective-permute-start(bf16[2,2,8,192,128]{4,3,2,1,0:T(8,128)(2,1)} %get-tuple-element.33.w_ref), channel_id=1, source_target_pairs={{0,1},{1,0},{2,3},{3,2},{4,5},{5,4},{6,7},{7,6},{8,9},{9,8},{10,11... | collective-permute-start | bytes 4718600 | tf_op jit(solution)/shard_map/gate_up_over_c/ppermute | solution.py:299
  83.8 11.7 %collective-permute-start.7 = (bf16[272,512]{1,0:T(8,128)(2,1)S(1)}, bf16[272,512]{1,0:T(8,128)(2,1)S(1)}, u32[]{:S(2)}, u32[]{:S(2)}) collective-permute-start(bf16[272,512]{1,0:T(8,128)(2,1)S(1)} %shard_map.79), channel_id=1, source_target_pairs={{0,16},{16,0},{1,17},{17,1},{2,18},{18,2},{3,19},{19,3},{4,20},{20... | collective-permute-start | bytes 835592 | tf_op jit(solution)/shard_map/hidden_over_y/ppermute | solution.py:314
  87.9 19.0 %collective-permute-start.2 = (bf16[96,2048]{1,0:T(8,128)(2,1)}, bf16[96,2048]{1,0:T(8,128)(2,1)}, u32[]{:S(2)}, u32[]{:S(2)}) collective-permute-start(bf16[96,2048]{1,0:T(8,128)(2,1)} %get-tuple-element.30), channel_id=1, source_target_pairs={{0,16},{16,0},{32,48},{48,32},{1,17},{17,1},{33,49},{49,33},{2,18}... | collective-permute-start | bytes 1179656 | tf_op jit(solution)/shard_map/down_over_y/ppermute | solution.py:293
  92.7 18.3 %collective-permute-start.4 = (bf16[96,2048]{1,0:T(8,128)(2,1)}, bf16[96,2048]{1,0:T(8,128)(2,1)S(1)}, u32[]{:S(2)}, u32[]{:S(2)}) collective-permute-start(bf16[96,2048]{1,0:T(8,128)(2,1)} %get-tuple-element.35), channel_id=1, source_target_pairs={{0,48},{16,32},{32,16},{48,0},{1,49},{17,33},{33,17},{49,1},{2,50}... | collective-permute-start | bytes 1179656 | tf_op jit(solution)/shard_map/down_over_y/ppermute | solution.py:293
  95.5 16.2 %copy-start.6 = (bf16[96,2048]{1,0:T(8,128)(2,1)S(1)}, bf16[96,2048]{1,0:T(8,128)(2,1)}, u32[]{:S(2)}) copy-start(bf16[96,2048]{1,0:T(8,128)(2,1)} %copy-done.5) | copy-start | bytes 1179652
  95.6 16.2 %copy-start.8 = (bf16[96,2048]{1,0:T(8,128)(2,1)S(1)}, bf16[96,2048]{1,0:T(8,128)(2,1)}, u32[]{:S(2)}) copy-start(bf16[96,2048]{1,0:T(8,128)(2,1)} %copy-done.7) | copy-start | bytes 1179652
  96.8 39.2 %all-to-all-start.2 = ((bf16[8,256,256]{2,1,0:T(8,128)(2,1)}), bf16[8,256,256]{2,1,0:T(8,128)(2,1)S(1)}, u32[]{:S(2)}, u32[]{:S(2)}) async-start(bf16[8,256,256]{2,1,0:T(8,128)(2,1)} %shard_map.80), calls=%async_computation.2 | async-start | bytes 2097152 | tf_op jit(solution)/shard_map/units_over_z/all_to_all | solution.py:326
  111.0 0.8 copy-start.9
  111.8 1.0 copy-start.10
  112.8 46.7 %copy-start.12 = (f32[128,2]{0,1:T(2,128)S(1)}, f32[128,2]{0,1:T(2,128)}, u32[]{:S(2)}) copy-start(f32[128,2]{0,1:T(2,128)} %param.10) | copy-start | bytes 3076
  114.4 7.3 %collective-permute-start.5 = (bf16[384,2048]{1,0:T(8,128)(2,1)S(1)}, bf16[384,2048]{1,0:T(8,128)(2,1)S(1)}, u32[]{:S(2)}, u32[]{:S(2)}) collective-permute-start(bf16[384,2048]{1,0:T(8,128)(2,1)S(1)} %shard_map.78.own_ref), channel_id=1, source_target_pairs={{0,1},{1,0},{2,3},{3,2},{4,5},{5,4},{6,7},{7,6},{8,9},{9,8},{10,11... | collective-permute-start | bytes 4718600 | tf_op jit(solution)/shard_map/down_over_c/ppermute | solution.py:332
  121.7 1.2 copy-start.1
  136.0 1.4 copy-start.2
  (3 other events, 2.1 us)

commit v4 on v3

--- a/solution.py
+++ b/solution.py
@@ -20,7 +20,7 @@
 SLOTS = EXPERTS * PIECE
 EXTRA = 16
 TILES = GROUP * FEATS // 128
-PARTS = SLOTS // 128 * EXTRA
+PARTS = SLOTS // 128 * 8
 DEPTH = TILES * SLOTS + PARTS
 PACK = 128 // PIECE
 BF = jnp.bfloat16
@@ -58,7 +58,13 @@
     )(*args, *after)
 
 
-def dispatch_body(hidden_ref, gain_ref, routes_ref, out_ref, target_ref):
+def dispatch_body(hidden_hbm, gain_hbm, routes_hbm, out_ref, target_ref, hidden_ref, gain_ref, routes_ref, sem):
+    pairs = ((routes_hbm, routes_ref), (hidden_hbm, hidden_ref), (gain_hbm, gain_ref))
+    copies = [pltpu.make_async_copy(a, b, sem.at[i]) for i, (a, b) in enumerate(pairs)]
+    for copy in copies:
+        copy.start()
+    for copy in copies:
+        copy.wait()
     diagonal = iota((FEATS, FEATS), 0) == iota((FEATS, FEATS), 1)
     gain = jnp.sum(jnp.where(diagonal, gain_ref[...].astype(F32), 0.0), axis=1, keepdims=True)
     values = hidden_ref[...].astype(F32)
@@ -101,11 +107,16 @@
                 tile += dot(rows[j], pick)
         turned_ref[t * SLOTS : (t + 1) * SLOTS, :] = tile.astype(BF)
     for j in range(GROUP):
-        pick = one_hot((row - 3 * j == lane - FEATS) & (row >= 3 * j) & (row < 3 * j + 3))
+        pick = one_hot((row == lane - FEATS) & (row < 3))
         extra += dot(pick, rows[j], NT)
-    for t in range(SLOTS // 128):
-        start = TILES * SLOTS + t * EXTRA
-        turned_ref[start : start + EXTRA, :] = extra[:, t * 128 : (t + 1) * 128].astype(BF)
+    squares = jnp.minimum(jnp.sum(extra, axis=0, keepdims=True), BIG)
+    hi = squares.astype(BF).astype(F32)
+    mid = (squares - hi).astype(BF).astype(F32)
+    row = iota((8, SLOTS), 0)
+    extra = jnp.where(row == 0, hi, jnp.where(row == 1, mid, squares - hi - mid))
+    extra = jnp.where(row < 3, extra, 0.0)
+    tiles = [extra[:, t * 128 : (t + 1) * 128] for t in range(SLOTS // 128)]
+    turned_ref[TILES * SLOTS :, :] = jnp.concatenate(tiles, axis=0).astype(BF)
     for z in range(NZ):
         out_ref[z] = turned_ref[...]
 
@@ -137,12 +148,13 @@
     for z in range(NZ):
         parts += x_ref[z, TILES * SLOTS :, :].astype(F32)
     sums = [
-        jnp.sum(parts[t * EXTRA : (t + 1) * EXTRA], axis=0, keepdims=True) for t in range(SLOTS // 128)
+        jnp.sum(parts[t * 8 : (t + 1) * 8], axis=0, keepdims=True) for t in range(SLOTS // 128)
     ]
     return jnp.concatenate(sums, axis=1)
 
 
-def neighbour_body(w_ref, w2_ref, x_ref, out_ref, acc_ref):
+def neighbour_body(w_ref, w2_ref, x_ref, *rest):
+    out_ref, acc_ref = rest[-2:]
     products(x_ref, (w_ref, w2_ref), acc_ref)
     out_ref[:SLOTS, :] = acc_ref[...].astype(BF)
     squares = jnp.minimum(sums_of_squares(x_ref), BIG)
@@ -247,16 +259,24 @@
     places = [quarter ^ m for m in range(NYL)] + [core, lax.axis_index("yb")]
     places = jnp.stack(places).astype(I32)
 
-    outgoing, targets = call(
+    hbm, vmem = (pl.BlockSpec(memory_space=space) for space in (pltpu.HBM, pltpu.VMEM))
+    outgoing, targets = pl.pallas_call(
         dispatch_body,
-        (
+        out_shape=(
             jax.ShapeDtypeStruct((EXPERTS, NYA, NC, PIECE, ROW_DEV), BF),
             jax.ShapeDtypeStruct((8, ROW_DEV), I32),
         ),
-        hidden_state.T,
-        norm_gain[None, :],
-        routes.T,
-    )
+        in_specs=[hbm, hbm, hbm],
+        out_specs=(vmem, vmem),
+        scratch_shapes=[
+            pltpu.VMEM((FEATS, ROW_DEV), BF),
+            pltpu.VMEM((1, FEATS), BF),
+            pltpu.VMEM((2, ROW_DEV), I32),
+            pltpu.SemaphoreType.DMA((3,)),
+        ],
+        compiler_params=pltpu.CompilerParams(vmem_limit_bytes=62 * 1024 * 1024),
+        cost_estimate=pl.CostEstimate(flops=1_000_000, bytes_accessed=1_000_000, transcendentals=0),
+    )(hidden_state.T, norm_gain[None, :], routes.T)
     with jax.named_scope("rows_over_xyc"):
         incoming = lax.all_to_all(
             outgoing.reshape(EXPERTS * GROUP, PIECE, ROW_DEV),
@@ -279,7 +299,6 @@
     half = jax.ShapeDtypeStruct((2, NYA, NZ, NC * FEATS, 128), BF)
     gate_cols, up_cols = w_gate[0].reshape(split), w_up[0].reshape(split)
     w_own, w_sent = call(halves_body, (half, half), places, gate_cols, up_cols, scalars=1)
-    w_sent, _ = lax.optimization_barrier((w_sent, block))
     with jax.named_scope("gate_up_over_y"):
         w_next = lax.ppermute(w_sent, "yb", swap)
     down = w_down[0]
@@ -293,13 +312,24 @@
             return lax.ppermute(sent, ("ya", "yb"), [(i, i ^ m) for i in range(NYL)])
 
     pieces[2] = over_y(2, block)
-    w_next, pieces[2] = lax.optimization_barrier((w_next, pieces[2]))
+    w_own, _ = lax.optimization_barrier((w_own, block))
+    with jax.named_scope("gate_up_over_c"):
+        w_core = lax.ppermute(w_own, "c", swap)
+    w_next, pieces[2], w_core = lax.optimization_barrier((w_next, pieces[2], w_core))
     pieces[1] = over_y(1, w_next)
     with jax.named_scope("gate_up_over_c"):
-        w_core = lax.ppermute(w_own, "c", swap)
         w_next_core = lax.ppermute(w_next, "c", swap)
 
     flops = 2 * SLOTS * D // 2 * 512
+    own, squares = call(
+        own_body,
+        (jax.ShapeDtypeStruct((SLOTS, 512), F32), jax.ShapeDtypeStruct((8, SLOTS), F32)),
+        w_own,
+        w_core,
+        features,
+        flops=flops,
+        moved=5_000_000,
+    )
     sent = call(
         neighbour_body,
         jax.ShapeDtypeStruct((SLOTS + EXTRA, 512), BF),
@@ -308,19 +338,11 @@
         features,
         flops=flops,
         moved=5_000_000,
+        after=(squares,),
         scratch_shapes=[pltpu.VMEM((SLOTS, 512), F32)],
     )
     with jax.named_scope("hidden_over_y"):
         got = lax.ppermute(sent, "yb", swap)
-    own, squares = call(
-        own_body,
-        (jax.ShapeDtypeStruct((SLOTS, 512), F32), jax.ShapeDtypeStruct((8, SLOTS), F32)),
-        w_own,
-        w_core,
-        features,
-        flops=flops,
-        moved=5_000_000,
-    )
     acts = call(act_body, jax.ShapeDtypeStruct((NZ, SLOTS, 256), BF), own, squares, got)
     with jax.named_scope("units_over_z"):
         acts = lax.all_to_all(acts, "z", split_axis=0, concat_axis=0, tiled=True)

time: 161 us -> 155 us (0.963)
  starting transfers between devices: 54.5 us -> 47.3 us
    all_to_all x1, waiting for transfers between devices: 0.5 us -> 13.7 us  [per_device(): lax.all_to_all(block, 'z', split_axis=0, concat_axis=0, tiled=True)]
    all_to_all x1, waiting for transfers between devices: 13.2 us -> 4.61 us  [per_device(): acts = lax.all_to_all(acts, 'z', split_axis=0, concat_axis=0, tiled=True)]
    all_to_all x1, starting transfers between devices: 10 us -> 3.56 us  [per_device(): acts = lax.all_to_all(acts, 'z', split_axis=0, concat_axis=0, tiled=True)]
    all_to_all x1, waiting for transfers between devices: 8.27 us -> 5.46 us  [per_device(): lax.all_to_all(outgoing.reshape(EXPERTS * GROUP, PIECE, ROW_DEV), ('x', '...]
    ppermute x1, starting transfers between devices: 4.01 us -> 1.92 us  [per_device(): got = lax.ppermute(sent, 'yb', swap)]
    ppermute x3, starting transfers between devices: 7.82 us -> 9.77 us  [over_y(): return lax.ppermute(sent, ('ya', 'yb'), [(i, i ^ m) for i in range(NYL)])]
    pallas_call x0 -> x1, Pallas kernels: none -> 1.81 us  [per_device(): pl.pallas_call(dispatch_body, out_shape=(jax.ShapeDtypeStruct((EXPERTS, N...]
    pallas_call x10 -> x9, Pallas kernels: 17.3 us -> 16.3 us  [call(): pl.pallas_call(body, out_shape=out_shape, in_specs=specs, out_specs=jax.t...]
  transfers between devices with their start and end apart: 11 -> 11, of which waited for: 8 -> 9; matrix products, arithmetic and copies ran while one was open for 0% -> 0% of each run, Pallas kernels for 7% -> 7%
where the time goes in v4:
time: 155 us; the launch traced here: 154 us
  waiting for transfers between devices  57.1 us (37%)
  starting transfers between devices  47.3 us (31%)
  blocking collectives  19.5 us (13%)
  Pallas kernels  18.1 us (12%)
  local copies, waits for them, and re-layouts  11.9 us (8%)
    ppermute x3, waiting for transfers between devices, over_y(): return lax.ppermute(sent, ('ya', 'yb'), [(i, i ^ m) for i in range(NYL)])  28.4 us
    all_to_all x1, blocking collectives, per_device(): lax.all_to_all(out.reshape(EXPERTS * NYL * NC, rows, 128), ('x', 'yh', 'y...  19.5 us
    pallas_call x9, Pallas kernels, call(): pl.pallas_call(body, out_shape=out_shape, in_specs=specs, out_specs=jax.t...  16.3 us
    all_to_all x1, waiting for transfers between devices, per_device(): lax.all_to_all(block, 'z', split_axis=0, concat_axis=0, tiled=True)  13.7 us
    unnamed x30, local copies, waits for them, and re-layouts  11.8 us
    all_to_all x1, starting transfers between devices, per_device(): lax.all_to_all(outgoing.reshape(EXPERTS * GROUP, PIECE, ROW_DEV), ('x', '...  11.2 us
    all_to_all x1, starting transfers between devices, per_device(): lax.all_to_all(block, 'z', split_axis=0, concat_axis=0, tiled=True)  10.1 us
    ppermute x3, starting transfers between devices, over_y(): return lax.ppermute(sent, ('ya', 'yb'), [(i, i ^ m) for i in range(NYL)])  9.77 us
  transfers between devices with their start and end apart: 11, of which 9 were waited for; matrix products, arithmetic and copies ran while one was open for 0% of the time, Pallas kernels for 7%

profile of v4, /device:TPU:1, one launch (start us, length us, event | category | flops | bytes accessed | tf_op | source)
XLA Modules:
  0.0 154.1 jit_solution(6460530482983205418)
XLA Ops:
  0.0 1.8 %shard_map.73 = (bf16[8,2,2,32,128]{4,3,2,1,0:T(8,128)(2,1)}, s32[8,128]{1,0:T(8,128)}) custom-call(bf16[96,128]{1,0:T(8,128)(2,1)} %bitcast.28, bf16[1,96]{1,0:T(2,128)(2,1)} %bitcast.30, s32[2,128]{1,0:T(2,128)} %bitcast.29), custom_call_target="tpu_custom_call" | custom-call | flops 1000000 | bytes 1000000 | tf_op jit(solution)/shard_map/pallas_call | solution.py:263
  1.8 11.2 %all-to-all-start = ((bf16[32,32,128]{2,1,0:T(8,128)(2,1)}), bf16[32,32,128]{2,1,0:T(8,128)(2,1)S(1)}, u32[]{:S(2)}, u32[]{:S(2)}) async-start(bf16[32,32,128]{2,1,0:T(8,128)(2,1)} %bitcast.27), calls=%async_computation | async-start | bytes 524288 | tf_op jit(solution)/shard_map/rows_over_xyc/all_to_all | solution.py:281
  16.0 2.4 %shard_map.75 = (bf16[2,2,8,192,128]{4,3,2,1,0:T(8,128)(2,1)}, bf16[2,2,8,192,128]{4,3,2,1,0:T(8,128)(2,1)}) custom-call(s32[6]{0:T(128)S(1)} %stack.27.place_ref, bf16[2,2,8,192,128]{4,3,2,1,0:T(8,128)(2,1)S(1)} %bitcast.23, bf16[2,2,8,192,128]{4,3,2,1,0:T(8,128)(2,1)S(1)} %bitcast.24), custom_call_target="tpu_custom_call" | custom-call | flops 1000000 | bytes 1000000 | tf_op jit(solution)/shard_map/pallas_call | solution.py:50
  18.4 2.3 %collective-permute-start = (bf16[2,2,8,192,128]{4,3,2,1,0:T(8,128)(2,1)}, bf16[2,2,8,192,128]{4,3,2,1,0:T(8,128)(2,1)S(1)}, u32[]{:S(2)}, u32[]{:S(2)}) collective-permute-start(bf16[2,2,8,192,128]{4,3,2,1,0:T(8,128)(2,1)} %get-tuple-element.25), channel_id=1, source_target_pairs={{0,16},{16,0},{1,17},{17,1},{2,18},{18,2},{3,19},{19,3},{4,20},{20... | collective-permute-start | bytes 4718600 | tf_op jit(solution)/shard_map/gate_up_over_y/ppermute | solution.py:303
  20.7 5.5 %all-to-all-done = bf16[32,32,128]{2,1,0:T(8,128)(2,1)S(1)} async-done(((bf16[32,32,128]{2,1,0:T(8,128)(2,1)}), bf16[32,32,128]{2,1,0:T(8,128)(2,1)S(1)}, u32[]{:S(2)}, u32[]{:S(2)}) %all-to-all-start) | async-done | bytes 262176 | tf_op jit(solution)/shard_map/rows_over_xyc/all_to_all | solution.py:281
  27.8 2.3 %collective-permute-start.2 = (bf16[2,2,8,192,128]{4,3,2,1,0:T(8,128)(2,1)}, bf16[2,2,8,192,128]{4,3,2,1,0:T(8,128)(2,1)}, u32[]{:S(2)}, u32[]{:S(2)}) collective-permute-start(bf16[2,2,8,192,128]{4,3,2,1,0:T(8,128)(2,1)} %get-tuple-element.30.w_ref), channel_id=1, source_target_pairs={{0,1},{1,0},{2,3},{3,2},{4,5},{5,4},{6,7},{7,6},{8,9},{9,8},{10,11... | collective-permute-start | bytes 4718600 | tf_op jit(solution)/shard_map/gate_up_over_c/ppermute | solution.py:317
  30.1 10.1 %all-to-all-start.1 = ((bf16[8,784,128]{2,1,0:T(8,128)(2,1)}), bf16[8,784,128]{2,1,0:T(8,128)(2,1)S(1)}, u32[]{:S(2)}, u32[]{:S(2)}) async-start(bf16[8,784,128]{2,1,0:T(8,128)(2,1)} %shard_map.76), calls=%async_computation.1 | async-start | bytes 3211264 | tf_op jit(solution)/shard_map/features_over_z/all_to_all | solution.py:296
  43.9 3.3 %collective-permute-start.1 = (bf16[96,2048]{1,0:T(8,128)(2,1)S(1)}, bf16[96,2048]{1,0:T(8,128)(2,1)S(1)}, u32[]{:S(2)}, u32[]{:S(2)}) collective-permute-start(bf16[96,2048]{1,0:T(8,128)(2,1)S(1)} %get-tuple-element.28), channel_id=1, source_target_pairs={{0,32},{16,48},{32,0},{48,16},{1,33},{17,49},{33,1},{49,17},{2,34}... | collective-permute-start | bytes 1179656 | tf_op jit(solution)/shard_map/down_over_y/ppermute | solution.py:312
  47.1 16.1 %collective-permute-done.1.refs_2_ = bf16[96,2048]{1,0:T(8,128)(2,1)S(1)} collective-permute-done((bf16[96,2048]{1,0:T(8,128)(2,1)S(1)}, bf16[96,2048]{1,0:T(8,128)(2,1)S(1)}, u32[]{:S(2)}, u32[]{:S(2)}) %collective-permute-start.1) | collective-permute-done | bytes 393248 | tf_op jit(solution)/shard_map/down_over_y/ppermute | solution.py:312
  64.7 2.9 %collective-permute-start.6 = (bf16[2,2,8,192,128]{4,3,2,1,0:T(8,128)(2,1)S(1)}, bf16[2,2,8,192,128]{4,3,2,1,0:T(8,128)(2,1)}, u32[]{:S(2)}, u32[]{:S(2)}) collective-permute-start(bf16[2,2,8,192,128]{4,3,2,1,0:T(8,128)(2,1)S(1)} %collective-permute-done.w_ref), channel_id=1, source_target_pairs={{0,1},{1,0},{2,3},{3,2},{4,5},{5,4},{6,7},{7,6},{8,9},{9,8},{10,11... | collective-permute-start | bytes 4718600 | tf_op jit(solution)/shard_map/gate_up_over_c/ppermute | solution.py:321
  67.6 13.7 %all-to-all-done.1.x_ref = bf16[8,784,128]{2,1,0:T(8,128)(2,1)S(1)} async-done(((bf16[8,784,128]{2,1,0:T(8,128)(2,1)}), bf16[8,784,128]{2,1,0:T(8,128)(2,1)S(1)}, u32[]{:S(2)}, u32[]{:S(2)}) %all-to-all-start.1) | async-done | bytes 1605664 | tf_op jit(solution)/shard_map/features_over_z/all_to_all | solution.py:296
  81.3 2.9 %shard_map.77 = (f32[256,512]{1,0:T(8,128)S(1)}, f32[8,256]{1,0:T(8,128)S(1)}) custom-call(bf16[2,2,8,192,128]{4,3,2,1,0:T(8,128)(2,1)} %get-tuple-element.30.w_ref, bf16[2,2,8,192,128]{4,3,2,1,0:T(8,128)(2,1)} %collective-permute-done.2.w2_ref, bf16[8,784,128]{2,1,0:T(8,128)(2,1)S(1)} %all-to-all-done.1.x_ref), custom_call_target="tpu_custom_call" | custom-call | flops 805306368 | bytes 5000000 | tf_op jit(solution)/shard_map/pallas_call | solution.py:50
  84.2 2.4 %shard_map.79 = bf16[272,512]{1,0:T(8,128)(2,1)S(1)} custom-call(bf16[2,2,8,192,128]{4,3,2,1,0:T(8,128)(2,1)S(1)} %collective-permute-done.w_ref, bf16[2,2,8,192,128]{4,3,2,1,0:T(8,128)(2,1)} %collective-permute-done.6.w2_ref, bf16[8,784,128]{2,1,0:T(8,128)(2,1)S(1)} %all-to-all-done.1.x_ref, f32[8,256]{1,0:T(8,128)S(1)} %get-tuple-element.38.rest_0_.squares_ref), custom_call_target="tpu_custom_call" | custom-call | flops 805306368 | bytes 5000000 | tf_op jit(solution)/shard_map/pallas_call | solution.py:50
  86.6 1.9 %collective-permute-start.7 = (bf16[272,512]{1,0:T(8,128)(2,1)S(1)}, bf16[272,512]{1,0:T(8,128)(2,1)S(1)}, u32[]{:S(2)}, u32[]{:S(2)}) collective-permute-start(bf16[272,512]{1,0:T(8,128)(2,1)S(1)} %shard_map.79), channel_id=1, source_target_pairs={{0,16},{16,0},{1,17},{17,1},{2,18},{18,2},{3,19},{19,3},{4,20},{20... | collective-permute-start | bytes 835592 | tf_op jit(solution)/shard_map/hidden_over_y/ppermute | solution.py:345
  88.5 3.4 %collective-permute-start.3 = (bf16[96,2048]{1,0:T(8,128)(2,1)}, bf16[96,2048]{1,0:T(8,128)(2,1)S(1)}, u32[]{:S(2)}, u32[]{:S(2)}) collective-permute-start(bf16[96,2048]{1,0:T(8,128)(2,1)} %get-tuple-element.32), channel_id=1, source_target_pairs={{0,16},{16,0},{32,48},{48,32},{1,17},{17,1},{33,49},{49,33},{2,18}... | collective-permute-start | bytes 1179656 | tf_op jit(solution)/shard_map/down_over_y/ppermute | solution.py:312
  91.9 3.1 %collective-permute-start.4 = (bf16[96,2048]{1,0:T(8,128)(2,1)}, bf16[96,2048]{1,0:T(8,128)(2,1)S(1)}, u32[]{:S(2)}, u32[]{:S(2)}) collective-permute-start(bf16[96,2048]{1,0:T(8,128)(2,1)} %get-tuple-element.37), channel_id=1, source_target_pairs={{0,48},{16,32},{32,16},{48,0},{1,49},{17,33},{33,17},{49,1},{2,50}... | collective-permute-start | bytes 1179656 | tf_op jit(solution)/shard_map/down_over_y/ppermute | solution.py:312
  97.5 3.6 %all-to-all-start.2 = ((bf16[8,256,256]{2,1,0:T(8,128)(2,1)}), bf16[8,256,256]{2,1,0:T(8,128)(2,1)S(1)}, u32[]{:S(2)}, u32[]{:S(2)}) async-start(bf16[8,256,256]{2,1,0:T(8,128)(2,1)} %shard_map.80), calls=%async_computation.2 | async-start | bytes 2097152 | tf_op jit(solution)/shard_map/units_over_z/all_to_all | solution.py:348
  101.1 3.6 %collective-permute-done.3.refs_1_ = bf16[96,2048]{1,0:T(8,128)(2,1)S(1)} collective-permute-done((bf16[96,2048]{1,0:T(8,128)(2,1)}, bf16[96,2048]{1,0:T(8,128)(2,1)S(1)}, u32[]{:S(2)}, u32[]{:S(2)}) %collective-permute-start.3) | collective-permute-done | bytes 393248 | tf_op jit(solution)/shard_map/down_over_y/ppermute | solution.py:312
  105.4 8.8 %collective-permute-done.4.refs_3_ = bf16[96,2048]{1,0:T(8,128)(2,1)S(1)} collective-permute-done((bf16[96,2048]{1,0:T(8,128)(2,1)}, bf16[96,2048]{1,0:T(8,128)(2,1)S(1)}, u32[]{:S(2)}, u32[]{:S(2)}) %collective-permute-start.4) | collective-permute-done | bytes 393248 | tf_op jit(solution)/shard_map/down_over_y/ppermute | solution.py:312
  118.1 3.2 %collective-permute-start.5 = (bf16[384,2048]{1,0:T(8,128)(2,1)S(1)}, bf16[384,2048]{1,0:T(8,128)(2,1)S(1)}, u32[]{:S(2)}, u32[]{:S(2)}) collective-permute-start(bf16[384,2048]{1,0:T(8,128)(2,1)S(1)} %shard_map.78.own_ref), channel_id=1, source_target_pairs={{0,1},{1,0},{2,3},{3,2},{4,5},{5,4},{6,7},{7,6},{8,9},{9,8},{10,11... | collective-permute-start | bytes 4718600 | tf_op jit(solution)/shard_map/down_over_c/ppermute | solution.py:354
  121.3 3.0 %collective-permute-done.5.other_ref = bf16[384,2048]{1,0:T(8,128)(2,1)S(1)} collective-permute-done((bf16[384,2048]{1,0:T(8,128)(2,1)S(1)}, bf16[384,2048]{1,0:T(8,128)(2,1)S(1)}, u32[]{:S(2)}, u32[]{:S(2)}) %collective-permute-start.5) | collective-permute-done | bytes 1572896 | tf_op jit(solution)/shard_map/down_over_c/ppermute | solution.py:354
  125.5 4.6 %all-to-all-done.2.x_ref = bf16[8,256,256]{2,1,0:T(8,128)(2,1)S(1)} async-done(((bf16[8,256,256]{2,1,0:T(8,128)(2,1)}), bf16[8,256,256]{2,1,0:T(8,128)(2,1)S(1)}, u32[]{:S(2)}, u32[]{:S(2)}) %all-to-all-start.2) | async-done | bytes 1048608 | tf_op jit(solution)/shard_map/units_over_z/all_to_all | solution.py:348
  131.5 1.9 %shard_map.81 = bf16[8,4,2,24,128]{4,3,2,1,0:T(8,128)(2,1)S(1)} custom-call(s32[6]{0:T(128)S(1)} %stack.27.place_ref, bf16[384,2048]{1,0:T(8,128)(2,1)S(1)} %shard_map.78.own_ref, bf16[384,2048]{1,0:T(8,128)(2,1)S(1)} %copy-done.2, bf16[8,256,256]{2,1,0:T(8,128)(2,1)S(1)} %all-to-all-done.2.x_ref), custom_call_target="tpu_custom_call" | custom-call | flops 805306368 | bytes 5000000 | tf_op jit(solution)/shard_map/pallas_call | solution.py:50
  133.4 19.5 %all_to_all.20 = bf16[64,24,128]{2,1,0:T(8,128)(2,1)S(1)} all-to-all(bf16[64,24,128]{2,1,0:T(8,128)(2,1)S(1)} %bitcast.21), channel_id=1, replica_groups=mesh['x'=4,'yh'=2,'ya'=2,'yb'=2,'z'=8,'c'=2] {'x','yh','ya','yb','c'}, dimensions={0} | all-to-all | bytes 786432 | tf_op jit(solution)/shard_map/out_over_xyc/all_to_all | solution.py:369
  (40 shorter events, 20.6 us)
Async XLA Ops:
  1.8 24.3 %all-to-all-start = ((bf16[32,32,128]{2,1,0:T(8,128)(2,1)}), bf16[32,32,128]{2,1,0:T(8,128)(2,1)S(1)}, u32[]{:S(2)}, u32[]{:S(2)}) async-start(bf16[32,32,128]{2,1,0:T(8,128)(2,1)} %bitcast.27), calls=%async_computation | async-start | bytes 524288 | tf_op jit(solution)/shard_map/rows_over_xyc/all_to_all | solution.py:281
  13.1 1.4 copy-start.3
  14.6 1.4 copy-start.4
  18.4 46.3 %collective-permute-start = (bf16[2,2,8,192,128]{4,3,2,1,0:T(8,128)(2,1)}, bf16[2,2,8,192,128]{4,3,2,1,0:T(8,128)(2,1)S(1)}, u32[]{:S(2)}, u32[]{:S(2)}) collective-permute-start(bf16[2,2,8,192,128]{4,3,2,1,0:T(8,128)(2,1)} %get-tuple-element.25), channel_id=1, source_target_pairs={{0,16},{16,0},{1,17},{17,1},{2,18},{18,2},{3,19},{19,3},{4,20},{20... | collective-permute-start | bytes 4718600 | tf_op jit(solution)/shard_map/gate_up_over_y/ppermute | solution.py:303
  27.8 36.9 %collective-permute-start.2 = (bf16[2,2,8,192,128]{4,3,2,1,0:T(8,128)(2,1)}, bf16[2,2,8,192,128]{4,3,2,1,0:T(8,128)(2,1)}, u32[]{:S(2)}, u32[]{:S(2)}) collective-permute-start(bf16[2,2,8,192,128]{4,3,2,1,0:T(8,128)(2,1)} %get-tuple-element.30.w_ref), channel_id=1, source_target_pairs={{0,1},{1,0},{2,3},{3,2},{4,5},{5,4},{6,7},{7,6},{8,9},{9,8},{10,11... | collective-permute-start | bytes 4718600 | tf_op jit(solution)/shard_map/gate_up_over_c/ppermute | solution.py:317
  30.1 51.2 %all-to-all-start.1 = ((bf16[8,784,128]{2,1,0:T(8,128)(2,1)}), bf16[8,784,128]{2,1,0:T(8,128)(2,1)S(1)}, u32[]{:S(2)}, u32[]{:S(2)}) async-start(bf16[8,784,128]{2,1,0:T(8,128)(2,1)} %shard_map.76), calls=%async_computation.1 | async-start | bytes 3211264 | tf_op jit(solution)/shard_map/features_over_z/all_to_all | solution.py:296
  40.2 1.4 copy-start
  43.1 0.8 copy-start.5
  43.9 19.3 %collective-permute-start.1 = (bf16[96,2048]{1,0:T(8,128)(2,1)S(1)}, bf16[96,2048]{1,0:T(8,128)(2,1)S(1)}, u32[]{:S(2)}, u32[]{:S(2)}) collective-permute-start(bf16[96,2048]{1,0:T(8,128)(2,1)S(1)} %get-tuple-element.28), channel_id=1, source_target_pairs={{0,32},{16,48},{32,0},{48,16},{1,33},{17,49},{33,1},{49,17},{2,34}... | collective-permute-start | bytes 1179656 | tf_op jit(solution)/shard_map/down_over_y/ppermute | solution.py:312
  64.7 19.5 %collective-permute-start.6 = (bf16[2,2,8,192,128]{4,3,2,1,0:T(8,128)(2,1)S(1)}, bf16[2,2,8,192,128]{4,3,2,1,0:T(8,128)(2,1)}, u32[]{:S(2)}, u32[]{:S(2)}) collective-permute-start(bf16[2,2,8,192,128]{4,3,2,1,0:T(8,128)(2,1)S(1)} %collective-permute-done.w_ref), channel_id=1, source_target_pairs={{0,1},{1,0},{2,3},{3,2},{4,5},{5,4},{6,7},{7,6},{8,9},{9,8},{10,11... | collective-permute-start | bytes 4718600 | tf_op jit(solution)/shard_map/gate_up_over_c/ppermute | solution.py:321
  86.6 9.6 %collective-permute-start.7 = (bf16[272,512]{1,0:T(8,128)(2,1)S(1)}, bf16[272,512]{1,0:T(8,128)(2,1)S(1)}, u32[]{:S(2)}, u32[]{:S(2)}) collective-permute-start(bf16[272,512]{1,0:T(8,128)(2,1)S(1)} %shard_map.79), channel_id=1, source_target_pairs={{0,16},{16,0},{1,17},{17,1},{2,18},{18,2},{3,19},{19,3},{4,20},{20... | collective-permute-start | bytes 835592 | tf_op jit(solution)/shard_map/hidden_over_y/ppermute | solution.py:345
  88.5 16.1 %collective-permute-start.3 = (bf16[96,2048]{1,0:T(8,128)(2,1)}, bf16[96,2048]{1,0:T(8,128)(2,1)S(1)}, u32[]{:S(2)}, u32[]{:S(2)}) collective-permute-start(bf16[96,2048]{1,0:T(8,128)(2,1)} %get-tuple-element.32), channel_id=1, source_target_pairs={{0,16},{16,0},{32,48},{48,32},{1,17},{17,1},{33,49},{49,33},{2,18}... | collective-permute-start | bytes 1179656 | tf_op jit(solution)/shard_map/down_over_y/ppermute | solution.py:312
  91.9 23.1 %copy-start.6 = (bf16[96,2048]{1,0:T(8,128)(2,1)S(1)}, bf16[96,2048]{1,0:T(8,128)(2,1)}, u32[]{:S(2)}) copy-start(bf16[96,2048]{1,0:T(8,128)(2,1)} %copy-done.5) | copy-start | bytes 1179652
  91.9 23.1 %copy-start.8 = (bf16[96,2048]{1,0:T(8,128)(2,1)S(1)}, bf16[96,2048]{1,0:T(8,128)(2,1)}, u32[]{:S(2)}) copy-start(bf16[96,2048]{1,0:T(8,128)(2,1)} %copy-done.7) | copy-start | bytes 1179652
  91.9 22.3 %collective-permute-start.4 = (bf16[96,2048]{1,0:T(8,128)(2,1)}, bf16[96,2048]{1,0:T(8,128)(2,1)S(1)}, u32[]{:S(2)}, u32[]{:S(2)}) collective-permute-start(bf16[96,2048]{1,0:T(8,128)(2,1)} %get-tuple-element.37), channel_id=1, source_target_pairs={{0,48},{16,32},{32,16},{48,0},{1,49},{17,33},{33,17},{49,1},{2,50}... | collective-permute-start | bytes 1179656 | tf_op jit(solution)/shard_map/down_over_y/ppermute | solution.py:312
  97.5 32.6 %all-to-all-start.2 = ((bf16[8,256,256]{2,1,0:T(8,128)(2,1)}), bf16[8,256,256]{2,1,0:T(8,128)(2,1)S(1)}, u32[]{:S(2)}, u32[]{:S(2)}) async-start(bf16[8,256,256]{2,1,0:T(8,128)(2,1)} %shard_map.80), calls=%async_computation.2 | async-start | bytes 2097152 | tf_op jit(solution)/shard_map/units_over_z/all_to_all | solution.py:348
  114.2 0.8 copy-start.11
  114.9 1.0 copy-start.10
  115.9 1.0 copy-start.12
  116.9 36.0 %copy-start.13 = (s32[8,128]{1,0:T(8,128)S(1)}, s32[8,128]{1,0:T(8,128)}, u32[]{:S(2)}) copy-start(s32[8,128]{1,0:T(8,128)} %get-tuple-element.22.target_ref) | copy-start | bytes 12292
  116.9 36.0 %copy-start.14 = (f32[128,2]{0,1:T(2,128)S(1)}, f32[128,2]{0,1:T(2,128)}, u32[]{:S(2)}) copy-start(f32[128,2]{0,1:T(2,128)} %param.10) | copy-start | bytes 3076
  118.1 6.2 %collective-permute-start.5 = (bf16[384,2048]{1,0:T(8,128)(2,1)S(1)}, bf16[384,2048]{1,0:T(8,128)(2,1)S(1)}, u32[]{:S(2)}, u32[]{:S(2)}) collective-permute-start(bf16[384,2048]{1,0:T(8,128)(2,1)S(1)} %shard_map.78.own_ref), channel_id=1, source_target_pairs={{0,1},{1,0},{2,3},{3,2},{4,5},{5,4},{6,7},{7,6},{8,9},{9,8},{10,11... | collective-permute-start | bytes 4718600 | tf_op jit(solution)/shard_map/down_over_c/ppermute | solution.py:354
  124.3 1.2 copy-start.1
  130.1 1.4 copy-start.2
  (2 other events, 1.5 us)

commit v5 on v3

--- a/solution.py
+++ b/solution.py
@@ -20,7 +20,7 @@
 SLOTS = EXPERTS * PIECE
 EXTRA = 16
 TILES = GROUP * FEATS // 128
-PARTS = SLOTS // 128 * EXTRA
+PARTS = SLOTS // 128 * 8
 DEPTH = TILES * SLOTS + PARTS
 PACK = 128 // PIECE
 BF = jnp.bfloat16
@@ -28,6 +28,7 @@
 I32 = jnp.int32
 BIG = 3.0e38
 NT = (((1,), (1,)), ((), ()))
+WHOLE_VMEM = 62 * 1024 * 1024
 VMEM_LIMIT = 40 * 1024 * 1024
 
 
@@ -43,7 +44,7 @@
     return lax.dot_general(a, b, dims, preferred_element_type=F32)
 
 
-def call(body, out_shape, *args, flops=1_000_000, moved=1_000_000, scalars=0, after=(), **kw):
+def call(body, out_shape, *args, flops=1_000_000, moved=1_000_000, scalars=0, after=(), limit=VMEM_LIMIT, **kw):
     specs = [pl.BlockSpec(memory_space=pltpu.SMEM)] * scalars
     specs += [pl.BlockSpec(memory_space=pltpu.VMEM)] * (len(args) - scalars)
     specs += [pl.BlockSpec(memory_space=pl.ANY)] * len(after)
@@ -52,7 +53,7 @@
         out_shape=out_shape,
         in_specs=specs,
         out_specs=jax.tree.map(lambda _: pl.BlockSpec(memory_space=pltpu.VMEM), out_shape),
-        compiler_params=pltpu.CompilerParams(vmem_limit_bytes=VMEM_LIMIT),
+        compiler_params=pltpu.CompilerParams(vmem_limit_bytes=limit),
         cost_estimate=pl.CostEstimate(flops=flops, bytes_accessed=moved, transcendentals=0),
         **kw,
     )(*args, *after)
@@ -101,21 +102,33 @@
                 tile += dot(rows[j], pick)
         turned_ref[t * SLOTS : (t + 1) * SLOTS, :] = tile.astype(BF)
     for j in range(GROUP):
-        pick = one_hot((row - 3 * j == lane - FEATS) & (row >= 3 * j) & (row < 3 * j + 3))
+        pick = one_hot((row == lane - FEATS) & (row < 3))
         extra += dot(pick, rows[j], NT)
-    for t in range(SLOTS // 128):
-        start = TILES * SLOTS + t * EXTRA
-        turned_ref[start : start + EXTRA, :] = extra[:, t * 128 : (t + 1) * 128].astype(BF)
+    squares = jnp.minimum(jnp.sum(extra, axis=0, keepdims=True), BIG)
+    hi = squares.astype(BF).astype(F32)
+    mid = (squares - hi).astype(BF).astype(F32)
+    row = iota((8, SLOTS), 0)
+    extra = jnp.where(row == 0, hi, jnp.where(row == 1, mid, squares - hi - mid))
+    extra = jnp.where(row < 3, extra, 0.0)
+    tiles = [extra[:, t * 128 : (t + 1) * 128] for t in range(SLOTS // 128)]
+    turned_ref[TILES * SLOTS :, :] = jnp.concatenate(tiles, axis=0).astype(BF)
     for z in range(NZ):
         out_ref[z] = turned_ref[...]
 
 
-def halves_body(place_ref, gate_ref, up_ref, own_ref, other_ref):
-    parity = place_ref[NYL + 1]
-    for i, ref in enumerate((gate_ref, up_ref)):
-        for j in range(NYA):
-            own_ref[i, j] = ref[j, parity]
-            other_ref[i, j] = ref[j, 1 - parity]
+def half_body(own, place_ref, gate_ref, up_ref, out_ref, held_ref, sem):
+    parity = place_ref[NYL + 1] if own else 1 - place_ref[NYL + 1]
+    parts = [(i, j, ref) for i, ref in enumerate((gate_ref, up_ref)) for j in range(NYA)]
+    to_held, to_out = [], []
+    for k, (i, j, ref) in enumerate(parts):
+        to_held.append(pltpu.make_async_copy(ref.at[j, parity], held_ref.at[i, j], sem.at[k]))
+        to_out.append(pltpu.make_async_copy(held_ref.at[i, j], out_ref.at[i, j], sem.at[len(parts) + k]))
+        to_held[-1].start()
+    for first, second in zip(to_held, to_out):
+        first.wait()
+        second.start()
+    for second in to_out:
+        second.wait()
 
 
 def products(x_ref, weight_refs, acc_ref):
@@ -137,7 +150,7 @@
     for z in range(NZ):
         parts += x_ref[z, TILES * SLOTS :, :].astype(F32)
     sums = [
-        jnp.sum(parts[t * EXTRA : (t + 1) * EXTRA], axis=0, keepdims=True) for t in range(SLOTS // 128)
+        jnp.sum(parts[t * 8 : (t + 1) * 8], axis=0, keepdims=True) for t in range(SLOTS // 128)
     ]
     return jnp.concatenate(sums, axis=1)
 
@@ -256,6 +269,7 @@
         hidden_state.T,
         norm_gain[None, :],
         routes.T,
+        limit=WHOLE_VMEM,
     )
     with jax.named_scope("rows_over_xyc"):
         incoming = lax.all_to_all(
@@ -278,8 +292,20 @@
     split = (NYA, NYB, NZ, NC * FEATS, 128)
     half = jax.ShapeDtypeStruct((2, NYA, NZ, NC * FEATS, 128), BF)
     gate_cols, up_cols = w_gate[0].reshape(split), w_up[0].reshape(split)
-    w_own, w_sent = call(halves_body, (half, half), places, gate_cols, up_cols, scalars=1)
-    w_sent, _ = lax.optimization_barrier((w_sent, block))
+    hbm = pl.BlockSpec(memory_space=pltpu.HBM)
+
+    def half_of(own, gate_cols, up_cols):
+        return pl.pallas_call(
+            functools.partial(half_body, own),
+            out_shape=half,
+            in_specs=[pl.BlockSpec(memory_space=pltpu.SMEM), hbm, hbm],
+            out_specs=hbm,
+            scratch_shapes=[pltpu.VMEM(half.shape, BF), pltpu.SemaphoreType.DMA((4 * NYA,))],
+            compiler_params=pltpu.CompilerParams(vmem_limit_bytes=WHOLE_VMEM),
+            cost_estimate=pl.CostEstimate(flops=0, bytes_accessed=3_000_000, transcendentals=0),
+        )(places, gate_cols, up_cols)
+
+    w_sent = half_of(False, gate_cols, up_cols)
     with jax.named_scope("gate_up_over_y"):
         w_next = lax.ppermute(w_sent, "yb", swap)
     down = w_down[0]
@@ -293,10 +319,13 @@
             return lax.ppermute(sent, ("ya", "yb"), [(i, i ^ m) for i in range(NYL)])
 
     pieces[2] = over_y(2, block)
-    w_next, pieces[2] = lax.optimization_barrier((w_next, pieces[2]))
+    w_own = half_of(True, gate_cols, up_cols)
+    w_own, _ = lax.optimization_barrier((w_own, block))
+    with jax.named_scope("gate_up_over_c"):
+        w_core = lax.ppermute(w_own, "c", swap)
+    w_next, pieces[2], w_core = lax.optimization_barrier((w_next, pieces[2], w_core))
     pieces[1] = over_y(1, w_next)
     with jax.named_scope("gate_up_over_c"):
-        w_core = lax.ppermute(w_own, "c", swap)
         w_next_core = lax.ppermute(w_next, "c", swap)
 
     flops = 2 * SLOTS * D // 2 * 512

time: 161 us -> 155 us (0.963)
  starting transfers between devices: 54.5 us -> 47.4 us
  Pallas kernels: 17.3 us -> 22 us
  local copies, waits for them, and re-layouts: 12.3 us -> 7.96 us
  blocking collectives: 20.1 us -> 22.9 us
  waiting for transfers between devices: 56.2 us -> 53.7 us
    all_to_all x1, waiting for transfers between devices: 0.5 us -> 15.4 us  [per_device(): lax.all_to_all(block, 'z', split_axis=0, concat_axis=0, tiled=True)]
    all_to_all x1, waiting for transfers between devices: 13.2 us -> 3.96 us  [per_device(): acts = lax.all_to_all(acts, 'z', split_axis=0, concat_axis=0, tiled=True)]
    all_to_all x1, starting transfers between devices: 10 us -> 3.56 us  [per_device(): acts = lax.all_to_all(acts, 'z', split_axis=0, concat_axis=0, tiled=True)]
    pallas_call x0 -> x2, Pallas kernels: none -> 5.85 us  [half_of(): pl.pallas_call(functools.partial(half_body, own), out_shape=half, in_spec...]
    unnamed x32 -> x26, local copies, waits for them, and re-layouts: 12.2 us -> 7.27 us
    all_to_all x1, waiting for transfers between devices: 8.27 us -> 4.21 us  [per_device(): lax.all_to_all(outgoing.reshape(EXPERTS * GROUP, PIECE, ROW_DEV), ('x', '...]
    ppermute x3, waiting for transfers between devices: 29.6 us -> 26.7 us  [over_y(): return lax.ppermute(sent, ('ya', 'yb'), [(i, i ^ m) for i in range(NYL)])]
    all_to_all x1, blocking collectives: 20.1 us -> 22.9 us  [per_device(): lax.all_to_all(out.reshape(EXPERTS * NYL * NC, rows, 128), ('x', 'yh', 'y...]
  transfers between devices with their start and end apart: 11 -> 11, of which waited for: 8 -> 8; matrix products, arithmetic and copies ran while one was open for 0% -> 0% of each run, Pallas kernels for 7% -> 9%
where the time goes in v5:
time: 155 us; the launch traced here: 154 us
  waiting for transfers between devices  53.7 us (35%)
  starting transfers between devices  47.4 us (31%)
  blocking collectives  22.9 us (15%)
  Pallas kernels  22 us (14%)
  local copies, waits for them, and re-layouts  7.96 us (5%)
    ppermute x3, waiting for transfers between devices, over_y(): return lax.ppermute(sent, ('ya', 'yb'), [(i, i ^ m) for i in range(NYL)])  26.7 us
    all_to_all x1, blocking collectives, per_device(): lax.all_to_all(out.reshape(EXPERTS * NYL * NC, rows, 128), ('x', 'yh', 'y...  22.9 us
    pallas_call x9, Pallas kernels, call(): pl.pallas_call(body, out_shape=out_shape, in_specs=specs, out_specs=jax.t...  16.1 us
    all_to_all x1, waiting for transfers between devices, per_device(): lax.all_to_all(block, 'z', split_axis=0, concat_axis=0, tiled=True)  15.4 us
    all_to_all x1, starting transfers between devices, per_device(): lax.all_to_all(outgoing.reshape(EXPERTS * GROUP, PIECE, ROW_DEV), ('x', '...  11.2 us
    all_to_all x1, starting transfers between devices, per_device(): lax.all_to_all(block, 'z', split_axis=0, concat_axis=0, tiled=True)  10.1 us
    ppermute x3, starting transfers between devices, over_y(): return lax.ppermute(sent, ('ya', 'yb'), [(i, i ^ m) for i in range(NYL)])  9.68 us
    unnamed x26, local copies, waits for them, and re-layouts  7.27 us
  transfers between devices with their start and end apart: 11, of which 8 were waited for; matrix products, arithmetic and copies ran while one was open for 0% of the time, Pallas kernels for 9%

profile of v5, /device:TPU:1, one launch (start us, length us, event | category | flops | bytes accessed | tf_op | source)
XLA Modules:
  0.0 154.2 jit_solution(16676606170038099968)
XLA Ops:
  1.8 11.2 %all-to-all-start = ((bf16[32,32,128]{2,1,0:T(8,128)(2,1)}), bf16[32,32,128]{2,1,0:T(8,128)(2,1)S(1)}, u32[]{:S(2)}, u32[]{:S(2)}) async-start(bf16[32,32,128]{2,1,0:T(8,128)(2,1)} %bitcast.29), calls=%async_computation | async-start | bytes 524288 | tf_op jit(solution)/shard_map/rows_over_xyc/all_to_all | solution.py:275
  13.7 2.9 %shard_map.75 = bf16[2,2,8,192,128]{4,3,2,1,0:T(8,128)(2,1)} custom-call(s32[6]{0:T(128)} %stack.27.place_ref, bf16[2,2,8,192,128]{4,3,2,1,0:T(8,128)(2,1)} %bitcast.25, bf16[2,2,8,192,128]{4,3,2,1,0:T(8,128)(2,1)} %bitcast.27), custom_call_target="tpu_custom_call" | custom-call | bytes 3000000 | tf_op jit(solution)/shard_map/pallas_call | solution.py:298
  16.7 2.3 %collective-permute-start = (bf16[2,2,8,192,128]{4,3,2,1,0:T(8,128)(2,1)}, bf16[2,2,8,192,128]{4,3,2,1,0:T(8,128)(2,1)}, u32[]{:S(2)}, u32[]{:S(2)}) collective-permute-start(bf16[2,2,8,192,128]{4,3,2,1,0:T(8,128)(2,1)} %shard_map.75), channel_id=1, source_target_pairs={{0,16},{16,0},{1,17},{17,1},{2,18},{18,2},{3,19},{19,3},{4,20},{20... | collective-permute-start | bytes 4718600 | tf_op jit(solution)/shard_map/gate_up_over_y/ppermute | solution.py:310
  19.0 2.9 %shard_map.77.w_ref = bf16[2,2,8,192,128]{4,3,2,1,0:T(8,128)(2,1)} custom-call(s32[6]{0:T(128)} %stack.27.place_ref, bf16[2,2,8,192,128]{4,3,2,1,0:T(8,128)(2,1)} %bitcast.26, bf16[2,2,8,192,128]{4,3,2,1,0:T(8,128)(2,1)} %bitcast.28), custom_call_target="tpu_custom_call" | custom-call | bytes 3000000 | tf_op jit(solution)/shard_map/pallas_call | solution.py:298
  21.9 4.2 %all-to-all-done = bf16[32,32,128]{2,1,0:T(8,128)(2,1)S(1)} async-done(((bf16[32,32,128]{2,1,0:T(8,128)(2,1)}), bf16[32,32,128]{2,1,0:T(8,128)(2,1)S(1)}, u32[]{:S(2)}, u32[]{:S(2)}) %all-to-all-start) | async-done | bytes 262176 | tf_op jit(solution)/shard_map/rows_over_xyc/all_to_all | solution.py:275
  27.8 2.4 %collective-permute-start.2 = (bf16[2,2,8,192,128]{4,3,2,1,0:T(8,128)(2,1)S(1)}, bf16[2,2,8,192,128]{4,3,2,1,0:T(8,128)(2,1)}, u32[]{:S(2)}, u32[]{:S(2)}) collective-permute-start(bf16[2,2,8,192,128]{4,3,2,1,0:T(8,128)(2,1)S(1)} %copy-done), channel_id=1, source_target_pairs={{0,1},{1,0},{2,3},{3,2},{4,5},{5,4},{6,7},{7,6},{8,9},{9,8},{10,11... | collective-permute-start | bytes 4718600 | tf_op jit(solution)/shard_map/gate_up_over_c/ppermute | solution.py:325
  30.2 10.1 %all-to-all-start.1 = ((bf16[8,784,128]{2,1,0:T(8,128)(2,1)}), bf16[8,784,128]{2,1,0:T(8,128)(2,1)S(1)}, u32[]{:S(2)}, u32[]{:S(2)}) async-start(bf16[8,784,128]{2,1,0:T(8,128)(2,1)} %shard_map.76), calls=%async_computation.1 | async-start | bytes 3211264 | tf_op jit(solution)/shard_map/features_over_z/all_to_all | solution.py:290
  44.0 3.3 %collective-permute-start.1 = (bf16[96,2048]{1,0:T(8,128)(2,1)S(1)}, bf16[96,2048]{1,0:T(8,128)(2,1)S(1)}, u32[]{:S(2)}, u32[]{:S(2)}) collective-permute-start(bf16[96,2048]{1,0:T(8,128)(2,1)S(1)} %get-tuple-element.25), channel_id=1, source_target_pairs={{0,32},{16,48},{32,0},{48,16},{1,33},{17,49},{33,1},{49,17},{2,34}... | collective-permute-start | bytes 1179656 | tf_op jit(solution)/shard_map/down_over_y/ppermute | solution.py:319
  47.3 14.6 %collective-permute-done.1.refs_2_ = bf16[96,2048]{1,0:T(8,128)(2,1)S(1)} collective-permute-done((bf16[96,2048]{1,0:T(8,128)(2,1)S(1)}, bf16[96,2048]{1,0:T(8,128)(2,1)S(1)}, u32[]{:S(2)}, u32[]{:S(2)}) %collective-permute-start.1) | collective-permute-done | bytes 393248 | tf_op jit(solution)/shard_map/down_over_y/ppermute | solution.py:319
  63.1 2.9 %collective-permute-start.6 = (bf16[2,2,8,192,128]{4,3,2,1,0:T(8,128)(2,1)}, bf16[2,2,8,192,128]{4,3,2,1,0:T(8,128)(2,1)}, u32[]{:S(2)}, u32[]{:S(2)}) collective-permute-start(bf16[2,2,8,192,128]{4,3,2,1,0:T(8,128)(2,1)} %collective-permute-done.w_ref), channel_id=1, source_target_pairs={{0,1},{1,0},{2,3},{3,2},{4,5},{5,4},{6,7},{7,6},{8,9},{9,8},{10,11... | collective-permute-start | bytes 4718600 | tf_op jit(solution)/shard_map/gate_up_over_c/ppermute | solution.py:329
  66.0 15.4 %all-to-all-done.1.x_ref = bf16[8,784,128]{2,1,0:T(8,128)(2,1)S(1)} async-done(((bf16[8,784,128]{2,1,0:T(8,128)(2,1)}), bf16[8,784,128]{2,1,0:T(8,128)(2,1)S(1)}, u32[]{:S(2)}, u32[]{:S(2)}) %all-to-all-start.1) | async-done | bytes 1605664 | tf_op jit(solution)/shard_map/features_over_z/all_to_all | solution.py:290
  81.4 2.9 %shard_map.80 = bf16[272,512]{1,0:T(8,128)(2,1)S(1)} custom-call(bf16[2,2,8,192,128]{4,3,2,1,0:T(8,128)(2,1)} %collective-permute-done.w_ref, bf16[2,2,8,192,128]{4,3,2,1,0:T(8,128)(2,1)} %collective-permute-done.6.w2_ref, bf16[8,784,128]{2,1,0:T(8,128)(2,1)S(1)} %all-to-all-done.1.x_ref), custom_call_target="tpu_custom_call" | custom-call | flops 805306368 | bytes 5000000 | tf_op jit(solution)/shard_map/pallas_call | solution.py:51
  84.3 1.9 %collective-permute-start.7 = (bf16[272,512]{1,0:T(8,128)(2,1)S(1)}, bf16[272,512]{1,0:T(8,128)(2,1)S(1)}, u32[]{:S(2)}, u32[]{:S(2)}) collective-permute-start(bf16[272,512]{1,0:T(8,128)(2,1)S(1)} %shard_map.80), channel_id=1, source_target_pairs={{0,16},{16,0},{1,17},{17,1},{2,18},{18,2},{3,19},{19,3},{4,20},{20... | collective-permute-start | bytes 835592 | tf_op jit(solution)/shard_map/hidden_over_y/ppermute | solution.py:343
  86.2 3.4 %collective-permute-start.3 = (bf16[96,2048]{1,0:T(8,128)(2,1)}, bf16[96,2048]{1,0:T(8,128)(2,1)}, u32[]{:S(2)}, u32[]{:S(2)}) collective-permute-start(bf16[96,2048]{1,0:T(8,128)(2,1)} %get-tuple-element.28), channel_id=1, source_target_pairs={{0,16},{16,0},{32,48},{48,32},{1,17},{17,1},{33,49},{49,33},{2,18}... | collective-permute-start | bytes 1179656 | tf_op jit(solution)/shard_map/down_over_y/ppermute | solution.py:319
  89.6 2.4 %shard_map.78 = (f32[256,512]{1,0:T(8,128)S(1)}, f32[8,256]{1,0:T(8,128)S(1)}) custom-call(bf16[2,2,8,192,128]{4,3,2,1,0:T(8,128)(2,1)S(1)} %copy-done, bf16[2,2,8,192,128]{4,3,2,1,0:T(8,128)(2,1)} %collective-permute-done.2.w2_ref, bf16[8,784,128]{2,1,0:T(8,128)(2,1)S(1)} %all-to-all-done.1.x_ref), custom_call_target="tpu_custom_call" | custom-call | flops 805306368 | bytes 5000000 | tf_op jit(solution)/shard_map/pallas_call | solution.py:51
  92.0 3.0 %collective-permute-start.4 = (bf16[96,2048]{1,0:T(8,128)(2,1)}, bf16[96,2048]{1,0:T(8,128)(2,1)S(1)}, u32[]{:S(2)}, u32[]{:S(2)}) collective-permute-start(bf16[96,2048]{1,0:T(8,128)(2,1)} %get-tuple-element.33), channel_id=1, source_target_pairs={{0,48},{16,32},{32,16},{48,0},{1,49},{17,33},{33,17},{49,1},{2,50}... | collective-permute-start | bytes 1179656 | tf_op jit(solution)/shard_map/down_over_y/ppermute | solution.py:319
  96.3 3.6 %all-to-all-start.2 = ((bf16[8,256,256]{2,1,0:T(8,128)(2,1)}), bf16[8,256,256]{2,1,0:T(8,128)(2,1)S(1)}, u32[]{:S(2)}, u32[]{:S(2)}) async-start(bf16[8,256,256]{2,1,0:T(8,128)(2,1)} %shard_map.81), calls=%async_computation.2 | async-start | bytes 2097152 | tf_op jit(solution)/shard_map/units_over_z/all_to_all | solution.py:355
  99.9 2.6 %collective-permute-done.3.refs_1_ = bf16[96,2048]{1,0:T(8,128)(2,1)} collective-permute-done((bf16[96,2048]{1,0:T(8,128)(2,1)}, bf16[96,2048]{1,0:T(8,128)(2,1)}, u32[]{:S(2)}, u32[]{:S(2)}) %collective-permute-start.3) | collective-permute-done | bytes 393248 | tf_op jit(solution)/shard_map/down_over_y/ppermute | solution.py:319
  102.5 9.5 %collective-permute-done.4.refs_3_ = bf16[96,2048]{1,0:T(8,128)(2,1)S(1)} collective-permute-done((bf16[96,2048]{1,0:T(8,128)(2,1)}, bf16[96,2048]{1,0:T(8,128)(2,1)S(1)}, u32[]{:S(2)}, u32[]{:S(2)}) %collective-permute-start.4) | collective-permute-done | bytes 393248 | tf_op jit(solution)/shard_map/down_over_y/ppermute | solution.py:319
  115.4 3.3 %collective-permute-start.5 = (bf16[384,2048]{1,0:T(8,128)(2,1)S(1)}, bf16[384,2048]{1,0:T(8,128)(2,1)S(1)}, u32[]{:S(2)}, u32[]{:S(2)}) collective-permute-start(bf16[384,2048]{1,0:T(8,128)(2,1)S(1)} %shard_map.79.own_ref), channel_id=1, source_target_pairs={{0,1},{1,0},{2,3},{3,2},{4,5},{5,4},{6,7},{7,6},{8,9},{9,8},{10,11... | collective-permute-start | bytes 4718600 | tf_op jit(solution)/shard_map/down_over_c/ppermute | solution.py:361
  118.6 3.0 %collective-permute-done.5.other_ref = bf16[384,2048]{1,0:T(8,128)(2,1)S(1)} collective-permute-done((bf16[384,2048]{1,0:T(8,128)(2,1)S(1)}, bf16[384,2048]{1,0:T(8,128)(2,1)S(1)}, u32[]{:S(2)}, u32[]{:S(2)}) %collective-permute-start.5) | collective-permute-done | bytes 1572896 | tf_op jit(solution)/shard_map/down_over_c/ppermute | solution.py:361
  122.8 4.0 %all-to-all-done.2.x_ref = bf16[8,256,256]{2,1,0:T(8,128)(2,1)S(1)} async-done(((bf16[8,256,256]{2,1,0:T(8,128)(2,1)}), bf16[8,256,256]{2,1,0:T(8,128)(2,1)S(1)}, u32[]{:S(2)}, u32[]{:S(2)}) %all-to-all-start.2) | async-done | bytes 1048608 | tf_op jit(solution)/shard_map/units_over_z/all_to_all | solution.py:355
  128.2 1.8 %shard_map.82 = bf16[8,4,2,24,128]{4,3,2,1,0:T(8,128)(2,1)S(1)} custom-call(s32[6]{0:T(128)S(1)} %copy-done.10, bf16[384,2048]{1,0:T(8,128)(2,1)S(1)} %shard_map.79.own_ref, bf16[384,2048]{1,0:T(8,128)(2,1)S(1)} %copy-done.3, bf16[8,256,256]{2,1,0:T(8,128)(2,1)S(1)} %all-to-all-done.2.x_ref), custom_call_target="tpu_custom_call" | custom-call | flops 805306368 | bytes 5000000 | tf_op jit(solution)/shard_map/pallas_call | solution.py:51
  130.1 22.9 %all_to_all.20 = bf16[64,24,128]{2,1,0:T(8,128)(2,1)S(1)} all-to-all(bf16[64,24,128]{2,1,0:T(8,128)(2,1)S(1)} %bitcast.21), channel_id=1, replica_groups=mesh['x'=4,'yh'=2,'ya'=2,'yb'=2,'z'=8,'c'=2] {'x','yh','ya','yb','c'}, dimensions={0} | all-to-all | bytes 786432 | tf_op jit(solution)/shard_map/out_over_xyc/all_to_all | solution.py:376
  (37 shorter events, 17.4 us)
Async XLA Ops:
  1.8 24.3 %all-to-all-start = ((bf16[32,32,128]{2,1,0:T(8,128)(2,1)}), bf16[32,32,128]{2,1,0:T(8,128)(2,1)S(1)}, u32[]{:S(2)}, u32[]{:S(2)}) async-start(bf16[32,32,128]{2,1,0:T(8,128)(2,1)} %bitcast.29), calls=%async_computation | async-start | bytes 524288 | tf_op jit(solution)/shard_map/rows_over_xyc/all_to_all | solution.py:275
  16.7 46.4 %collective-permute-start = (bf16[2,2,8,192,128]{4,3,2,1,0:T(8,128)(2,1)}, bf16[2,2,8,192,128]{4,3,2,1,0:T(8,128)(2,1)}, u32[]{:S(2)}, u32[]{:S(2)}) collective-permute-start(bf16[2,2,8,192,128]{4,3,2,1,0:T(8,128)(2,1)} %shard_map.75), channel_id=1, source_target_pairs={{0,16},{16,0},{1,17},{17,1},{2,18},{18,2},{3,19},{19,3},{4,20},{20... | collective-permute-start | bytes 4718600 | tf_op jit(solution)/shard_map/gate_up_over_y/ppermute | solution.py:310
  21.9 5.9 %copy-start = (bf16[2,2,8,192,128]{4,3,2,1,0:T(8,128)(2,1)S(1)}, bf16[2,2,8,192,128]{4,3,2,1,0:T(8,128)(2,1)}, u32[]{:S(2)}) copy-start(bf16[2,2,8,192,128]{4,3,2,1,0:T(8,128)(2,1)} %shard_map.77.w_ref) | copy-start | bytes 4718596
  27.8 12.5 %copy-start.10 = (s32[6]{0:T(128)S(1)}, s32[6]{0:T(128)}, u32[]{:S(2)}) copy-start(s32[6]{0:T(128)} %stack.27.place_ref) | copy-start | bytes 76
  27.8 35.3 %collective-permute-start.2 = (bf16[2,2,8,192,128]{4,3,2,1,0:T(8,128)(2,1)S(1)}, bf16[2,2,8,192,128]{4,3,2,1,0:T(8,128)(2,1)}, u32[]{:S(2)}, u32[]{:S(2)}) collective-permute-start(bf16[2,2,8,192,128]{4,3,2,1,0:T(8,128)(2,1)S(1)} %copy-done), channel_id=1, source_target_pairs={{0,1},{1,0},{2,3},{3,2},{4,5},{5,4},{6,7},{7,6},{8,9},{9,8},{10,11... | collective-permute-start | bytes 4718600 | tf_op jit(solution)/shard_map/gate_up_over_c/ppermute | solution.py:325
  30.2 51.2 %all-to-all-start.1 = ((bf16[8,784,128]{2,1,0:T(8,128)(2,1)}), bf16[8,784,128]{2,1,0:T(8,128)(2,1)S(1)}, u32[]{:S(2)}, u32[]{:S(2)}) async-start(bf16[8,784,128]{2,1,0:T(8,128)(2,1)} %shard_map.76), calls=%async_computation.1 | async-start | bytes 3211264 | tf_op jit(solution)/shard_map/features_over_z/all_to_all | solution.py:290
  40.3 1.4 copy-start.1
  43.2 0.8 copy-start.4
  44.0 17.9 %collective-permute-start.1 = (bf16[96,2048]{1,0:T(8,128)(2,1)S(1)}, bf16[96,2048]{1,0:T(8,128)(2,1)S(1)}, u32[]{:S(2)}, u32[]{:S(2)}) collective-permute-start(bf16[96,2048]{1,0:T(8,128)(2,1)S(1)} %get-tuple-element.25), channel_id=1, source_target_pairs={{0,32},{16,48},{32,0},{48,16},{1,33},{17,49},{33,1},{49,17},{2,34}... | collective-permute-start | bytes 1179656 | tf_op jit(solution)/shard_map/down_over_y/ppermute | solution.py:319
  61.9 0.8 copy-start.6
  63.1 18.4 %collective-permute-start.6 = (bf16[2,2,8,192,128]{4,3,2,1,0:T(8,128)(2,1)}, bf16[2,2,8,192,128]{4,3,2,1,0:T(8,128)(2,1)}, u32[]{:S(2)}, u32[]{:S(2)}) collective-permute-start(bf16[2,2,8,192,128]{4,3,2,1,0:T(8,128)(2,1)} %collective-permute-done.w_ref), channel_id=1, source_target_pairs={{0,1},{1,0},{2,3},{3,2},{4,5},{5,4},{6,7},{7,6},{8,9},{9,8},{10,11... | collective-permute-start | bytes 4718600 | tf_op jit(solution)/shard_map/gate_up_over_c/ppermute | solution.py:329
  84.3 10.7 %collective-permute-start.7 = (bf16[272,512]{1,0:T(8,128)(2,1)S(1)}, bf16[272,512]{1,0:T(8,128)(2,1)S(1)}, u32[]{:S(2)}, u32[]{:S(2)}) collective-permute-start(bf16[272,512]{1,0:T(8,128)(2,1)S(1)} %shard_map.80), channel_id=1, source_target_pairs={{0,16},{16,0},{1,17},{17,1},{2,18},{18,2},{3,19},{19,3},{4,20},{20... | collective-permute-start | bytes 835592 | tf_op jit(solution)/shard_map/hidden_over_y/ppermute | solution.py:343
  86.2 16.3 %collective-permute-start.3 = (bf16[96,2048]{1,0:T(8,128)(2,1)}, bf16[96,2048]{1,0:T(8,128)(2,1)}, u32[]{:S(2)}, u32[]{:S(2)}) collective-permute-start(bf16[96,2048]{1,0:T(8,128)(2,1)} %get-tuple-element.28), channel_id=1, source_target_pairs={{0,16},{16,0},{32,48},{48,32},{1,17},{17,1},{33,49},{49,33},{2,18}... | collective-permute-start | bytes 1179656 | tf_op jit(solution)/shard_map/down_over_y/ppermute | solution.py:319
  92.0 20.0 %collective-permute-start.4 = (bf16[96,2048]{1,0:T(8,128)(2,1)}, bf16[96,2048]{1,0:T(8,128)(2,1)S(1)}, u32[]{:S(2)}, u32[]{:S(2)}) collective-permute-start(bf16[96,2048]{1,0:T(8,128)(2,1)} %get-tuple-element.33), channel_id=1, source_target_pairs={{0,48},{16,32},{32,16},{48,0},{1,49},{17,33},{33,17},{49,1},{2,50}... | collective-permute-start | bytes 1179656 | tf_op jit(solution)/shard_map/down_over_y/ppermute | solution.py:319
  95.0 17.7 %copy-start.5 = (bf16[96,2048]{1,0:T(8,128)(2,1)S(1)}, bf16[96,2048]{1,0:T(8,128)(2,1)}, u32[]{:S(2)}) copy-start(bf16[96,2048]{1,0:T(8,128)(2,1)} %copy-done.4) | copy-start | bytes 1179652
  95.0 17.7 %copy-start.7 = (bf16[96,2048]{1,0:T(8,128)(2,1)S(1)}, bf16[96,2048]{1,0:T(8,128)(2,1)}, u32[]{:S(2)}) copy-start(bf16[96,2048]{1,0:T(8,128)(2,1)} %copy-done.6) | copy-start | bytes 1179652
  96.3 30.5 %all-to-all-start.2 = ((bf16[8,256,256]{2,1,0:T(8,128)(2,1)}), bf16[8,256,256]{2,1,0:T(8,128)(2,1)S(1)}, u32[]{:S(2)}, u32[]{:S(2)}) async-start(bf16[8,256,256]{2,1,0:T(8,128)(2,1)} %shard_map.81), calls=%async_computation.2 | async-start | bytes 2097152 | tf_op jit(solution)/shard_map/units_over_z/all_to_all | solution.py:355
  112.0 0.8 copy-start.8
  112.7 1.0 copy-start.9
  113.7 39.2 %copy-start.11 = (s32[8,128]{1,0:T(8,128)S(1)}, s32[8,128]{1,0:T(8,128)}, u32[]{:S(2)}) copy-start(s32[8,128]{1,0:T(8,128)} %get-tuple-element.20.target_ref) | copy-start | bytes 12292
  113.7 39.2 %copy-start.12 = (f32[128,2]{0,1:T(2,128)S(1)}, f32[128,2]{0,1:T(2,128)}, u32[]{:S(2)}) copy-start(f32[128,2]{0,1:T(2,128)} %param.10) | copy-start | bytes 3076
  115.4 6.3 %collective-permute-start.5 = (bf16[384,2048]{1,0:T(8,128)(2,1)S(1)}, bf16[384,2048]{1,0:T(8,128)(2,1)S(1)}, u32[]{:S(2)}, u32[]{:S(2)}) collective-permute-start(bf16[384,2048]{1,0:T(8,128)(2,1)S(1)} %shard_map.79.own_ref), channel_id=1, source_target_pairs={{0,1},{1,0},{2,3},{3,2},{4,5},{5,4},{6,7},{7,6},{8,9},{9,8},{10,11... | collective-permute-start | bytes 4718600 | tf_op jit(solution)/shard_map/down_over_c/ppermute | solution.py:361
  121.7 1.2 copy-start.2
  126.8 1.4 copy-start.3

commit v6 on v5

--- a/solution.py
+++ b/solution.py
@@ -193,13 +193,16 @@
     rows = FEATS // PACK
     group = iota((rows, 128), 1) // PIECE
     core = place_ref[NYL]
-    for k, w_ref in enumerate((own_ref, other_ref)):
-        out = jnp.zeros((w_ref.shape[0], SLOTS), F32)
-        for z in range(NZ):
-            units = x_ref[z]
-            if k == 1:
-                units = jnp.concatenate([units[:, 128:], units[:, :128]], axis=1)
-            out += dot(w_ref[:, z * 256 : (z + 1) * 256], units, NT)
+    columns = own_ref.shape[0]
+    total = jnp.zeros((2 * columns, SLOTS), F32)
+    for z in range(NZ):
+        cols = slice(z * 256, (z + 1) * 256)
+        swapped = jnp.concatenate(
+            [other_ref[:, z * 256 + 128 : (z + 1) * 256], other_ref[:, z * 256 : z * 256 + 128]], axis=1
+        )
+        total += dot(jnp.concatenate([own_ref[:, cols], swapped], axis=0), x_ref[z], NT)
+    for k in range(NC):
+        out = total[k * columns : (k + 1) * columns]
         to = core if k == 0 else 1 - core
         for j in range(NYL):
             for t in range(EXPERTS // PACK):
@@ -221,15 +224,20 @@
     group = iota((rows, 128), 1) // PIECE
     picked = jnp.zeros((FEATS, 2 * ROW_DEV), F32)
     for e in range(EXPERTS):
+        places, totals = [], []
         for h in range(NC):
-            place = one_hot(target - (e * CAP + h * PIECE) == slot)
+            places.append(one_hot(target - (e * CAP + h * PIECE) == slot))
             total = in_ref[e, 0, h].astype(F32)
             for j in range(1, NYL):
                 total += in_ref[e, j, h].astype(F32)
-            total = jnp.concatenate([jnp.where(group == q, total, 0.0) for q in range(PACK)], axis=0)
-            hi = total.astype(BF)
-            rest = (total - hi.astype(F32)).astype(BF)
-            picked += dot(hi, place) + dot(rest, place)
+            totals.append(
+                jnp.concatenate([jnp.where(group == q, total, 0.0) for q in range(PACK)], axis=0)
+            )
+        total = jnp.concatenate(totals, axis=1)
+        hi = total.astype(BF)
+        rest = (total - hi.astype(F32)).astype(BF)
+        both = dot(jnp.concatenate([hi, rest], axis=0), jnp.concatenate(places, axis=0))
+        picked += both[:FEATS] + both[FEATS:]
     mixed = gates_ref[0:1, :] * picked[:, :ROW_DEV] + gates_ref[1:2, :] * picked[:, ROW_DEV:]
     out_ref[...] = mixed.astype(BF)
 

time: 155 us -> 155 us (level)
  no operation moved by 1% of the time
where the time goes in v6:
time: 155 us; the launch traced here: 154 us
  waiting for transfers between devices  53.7 us (35%)
  starting transfers between devices  47.4 us (31%)
  blocking collectives  22.9 us (15%)
  Pallas kernels  21.7 us (14%)
  local copies, waits for them, and re-layouts  7.96 us (5%)
    ppermute x3, waiting for transfers between devices, over_y(): return lax.ppermute(sent, ('ya', 'yb'), [(i, i ^ m) for i in range(NYL)])  26.7 us
    all_to_all x1, blocking collectives, per_device(): lax.all_to_all(out.reshape(EXPERTS * NYL * NC, rows, 128), ('x', 'yh', 'y...  22.9 us
    pallas_call x9, Pallas kernels, call(): pl.pallas_call(body, out_shape=out_shape, in_specs=specs, out_specs=jax.t...  15.9 us
    all_to_all x1, waiting for transfers between devices, per_device(): lax.all_to_all(block, 'z', split_axis=0, concat_axis=0, tiled=True)  15.4 us
    all_to_all x1, starting transfers between devices, per_device(): lax.all_to_all(outgoing.reshape(EXPERTS * GROUP, PIECE, ROW_DEV), ('x', '...  11.2 us
    all_to_all x1, starting transfers between devices, per_device(): lax.all_to_all(block, 'z', split_axis=0, concat_axis=0, tiled=True)  10.1 us
    ppermute x3, starting transfers between devices, over_y(): return lax.ppermute(sent, ('ya', 'yb'), [(i, i ^ m) for i in range(NYL)])  9.68 us
    unnamed x26, local copies, waits for them, and re-layouts  7.27 us
  transfers between devices with their start and end apart: 11, of which 8 were waited for; matrix products, arithmetic and copies ran while one was open for 0% of the time, Pallas kernels for 9%

profile of v6, /device:TPU:1, one launch (start us, length us, event | category | flops | bytes accessed | tf_op | source)
XLA Modules:
  0.0 153.9 jit_solution(7452973302593197732)
XLA Ops:
  0.0 1.8 %shard_map.73 = (bf16[8,2,2,32,128]{4,3,2,1,0:T(8,128)(2,1)}, s32[8,128]{1,0:T(8,128)}) custom-call(bf16[96,128]{1,0:T(8,128)(2,1)} %bitcast.30, bf16[1,96]{1,0:T(2,128)(2,1)} %bitcast.32, s32[2,128]{1,0:T(2,128)} %bitcast.31), custom_call_target="tpu_custom_call" | custom-call | flops 1000000 | bytes 1000000 | tf_op jit(solution)/shard_map/pallas_call | solution.py:51
  1.8 11.2 %all-to-all-start = ((bf16[32,32,128]{2,1,0:T(8,128)(2,1)}), bf16[32,32,128]{2,1,0:T(8,128)(2,1)S(1)}, u32[]{:S(2)}, u32[]{:S(2)}) async-start(bf16[32,32,128]{2,1,0:T(8,128)(2,1)} %bitcast.29), calls=%async_computation | async-start | bytes 524288 | tf_op jit(solution)/shard_map/rows_over_xyc/all_to_all | solution.py:283
  13.7 2.9 %shard_map.75 = bf16[2,2,8,192,128]{4,3,2,1,0:T(8,128)(2,1)} custom-call(s32[6]{0:T(128)} %stack.27.place_ref, bf16[2,2,8,192,128]{4,3,2,1,0:T(8,128)(2,1)} %bitcast.25, bf16[2,2,8,192,128]{4,3,2,1,0:T(8,128)(2,1)} %bitcast.27), custom_call_target="tpu_custom_call" | custom-call | bytes 3000000 | tf_op jit(solution)/shard_map/pallas_call | solution.py:306
  16.7 2.3 %collective-permute-start = (bf16[2,2,8,192,128]{4,3,2,1,0:T(8,128)(2,1)}, bf16[2,2,8,192,128]{4,3,2,1,0:T(8,128)(2,1)}, u32[]{:S(2)}, u32[]{:S(2)}) collective-permute-start(bf16[2,2,8,192,128]{4,3,2,1,0:T(8,128)(2,1)} %shard_map.75), channel_id=1, source_target_pairs={{0,16},{16,0},{1,17},{17,1},{2,18},{18,2},{3,19},{19,3},{4,20},{20... | collective-permute-start | bytes 4718600 | tf_op jit(solution)/shard_map/gate_up_over_y/ppermute | solution.py:318
  19.0 2.9 %shard_map.77.w_ref = bf16[2,2,8,192,128]{4,3,2,1,0:T(8,128)(2,1)} custom-call(s32[6]{0:T(128)} %stack.27.place_ref, bf16[2,2,8,192,128]{4,3,2,1,0:T(8,128)(2,1)} %bitcast.26, bf16[2,2,8,192,128]{4,3,2,1,0:T(8,128)(2,1)} %bitcast.28), custom_call_target="tpu_custom_call" | custom-call | bytes 3000000 | tf_op jit(solution)/shard_map/pallas_call | solution.py:306
  21.9 4.2 %all-to-all-done = bf16[32,32,128]{2,1,0:T(8,128)(2,1)S(1)} async-done(((bf16[32,32,128]{2,1,0:T(8,128)(2,1)}), bf16[32,32,128]{2,1,0:T(8,128)(2,1)S(1)}, u32[]{:S(2)}, u32[]{:S(2)}) %all-to-all-start) | async-done | bytes 262176 | tf_op jit(solution)/shard_map/rows_over_xyc/all_to_all | solution.py:283
  27.8 2.4 %collective-permute-start.2 = (bf16[2,2,8,192,128]{4,3,2,1,0:T(8,128)(2,1)S(1)}, bf16[2,2,8,192,128]{4,3,2,1,0:T(8,128)(2,1)}, u32[]{:S(2)}, u32[]{:S(2)}) collective-permute-start(bf16[2,2,8,192,128]{4,3,2,1,0:T(8,128)(2,1)S(1)} %copy-done), channel_id=1, source_target_pairs={{0,1},{1,0},{2,3},{3,2},{4,5},{5,4},{6,7},{7,6},{8,9},{9,8},{10,11... | collective-permute-start | bytes 4718600 | tf_op jit(solution)/shard_map/gate_up_over_c/ppermute | solution.py:333
  30.2 10.1 %all-to-all-start.1 = ((bf16[8,784,128]{2,1,0:T(8,128)(2,1)}), bf16[8,784,128]{2,1,0:T(8,128)(2,1)S(1)}, u32[]{:S(2)}, u32[]{:S(2)}) async-start(bf16[8,784,128]{2,1,0:T(8,128)(2,1)} %shard_map.76), calls=%async_computation.1 | async-start | bytes 3211264 | tf_op jit(solution)/shard_map/features_over_z/all_to_all | solution.py:298
  44.0 3.3 %collective-permute-start.1 = (bf16[96,2048]{1,0:T(8,128)(2,1)S(1)}, bf16[96,2048]{1,0:T(8,128)(2,1)S(1)}, u32[]{:S(2)}, u32[]{:S(2)}) collective-permute-start(bf16[96,2048]{1,0:T(8,128)(2,1)S(1)} %get-tuple-element.25), channel_id=1, source_target_pairs={{0,32},{16,48},{32,0},{48,16},{1,33},{17,49},{33,1},{49,17},{2,34}... | collective-permute-start | bytes 1179656 | tf_op jit(solution)/shard_map/down_over_y/ppermute | solution.py:327
  47.3 14.6 %collective-permute-done.1.refs_2_ = bf16[96,2048]{1,0:T(8,128)(2,1)S(1)} collective-permute-done((bf16[96,2048]{1,0:T(8,128)(2,1)S(1)}, bf16[96,2048]{1,0:T(8,128)(2,1)S(1)}, u32[]{:S(2)}, u32[]{:S(2)}) %collective-permute-start.1) | collective-permute-done | bytes 393248 | tf_op jit(solution)/shard_map/down_over_y/ppermute | solution.py:327
  63.1 2.9 %collective-permute-start.6 = (bf16[2,2,8,192,128]{4,3,2,1,0:T(8,128)(2,1)}, bf16[2,2,8,192,128]{4,3,2,1,0:T(8,128)(2,1)}, u32[]{:S(2)}, u32[]{:S(2)}) collective-permute-start(bf16[2,2,8,192,128]{4,3,2,1,0:T(8,128)(2,1)} %collective-permute-done.w_ref), channel_id=1, source_target_pairs={{0,1},{1,0},{2,3},{3,2},{4,5},{5,4},{6,7},{7,6},{8,9},{9,8},{10,11... | collective-permute-start | bytes 4718600 | tf_op jit(solution)/shard_map/gate_up_over_c/ppermute | solution.py:337
  66.0 15.4 %all-to-all-done.1.x_ref = bf16[8,784,128]{2,1,0:T(8,128)(2,1)S(1)} async-done(((bf16[8,784,128]{2,1,0:T(8,128)(2,1)}), bf16[8,784,128]{2,1,0:T(8,128)(2,1)S(1)}, u32[]{:S(2)}, u32[]{:S(2)}) %all-to-all-start.1) | async-done | bytes 1605664 | tf_op jit(solution)/shard_map/features_over_z/all_to_all | solution.py:298
  81.4 2.9 %shard_map.80 = bf16[272,512]{1,0:T(8,128)(2,1)S(1)} custom-call(bf16[2,2,8,192,128]{4,3,2,1,0:T(8,128)(2,1)} %collective-permute-done.w_ref, bf16[2,2,8,192,128]{4,3,2,1,0:T(8,128)(2,1)} %collective-permute-done.6.w2_ref, bf16[8,784,128]{2,1,0:T(8,128)(2,1)S(1)} %all-to-all-done.1.x_ref), custom_call_target="tpu_custom_call" | custom-call | flops 805306368 | bytes 5000000 | tf_op jit(solution)/shard_map/pallas_call | solution.py:51
  84.3 1.9 %collective-permute-start.7 = (bf16[272,512]{1,0:T(8,128)(2,1)S(1)}, bf16[272,512]{1,0:T(8,128)(2,1)S(1)}, u32[]{:S(2)}, u32[]{:S(2)}) collective-permute-start(bf16[272,512]{1,0:T(8,128)(2,1)S(1)} %shard_map.80), channel_id=1, source_target_pairs={{0,16},{16,0},{1,17},{17,1},{2,18},{18,2},{3,19},{19,3},{4,20},{20... | collective-permute-start | bytes 835592 | tf_op jit(solution)/shard_map/hidden_over_y/ppermute | solution.py:351
  86.2 3.4 %collective-permute-start.3 = (bf16[96,2048]{1,0:T(8,128)(2,1)}, bf16[96,2048]{1,0:T(8,128)(2,1)}, u32[]{:S(2)}, u32[]{:S(2)}) collective-permute-start(bf16[96,2048]{1,0:T(8,128)(2,1)} %get-tuple-element.28), channel_id=1, source_target_pairs={{0,16},{16,0},{32,48},{48,32},{1,17},{17,1},{33,49},{49,33},{2,18}... | collective-permute-start | bytes 1179656 | tf_op jit(solution)/shard_map/down_over_y/ppermute | solution.py:327
  89.6 2.4 %shard_map.78 = (f32[256,512]{1,0:T(8,128)S(1)}, f32[8,256]{1,0:T(8,128)S(1)}) custom-call(bf16[2,2,8,192,128]{4,3,2,1,0:T(8,128)(2,1)S(1)} %copy-done, bf16[2,2,8,192,128]{4,3,2,1,0:T(8,128)(2,1)} %collective-permute-done.2.w2_ref, bf16[8,784,128]{2,1,0:T(8,128)(2,1)S(1)} %all-to-all-done.1.x_ref), custom_call_target="tpu_custom_call" | custom-call | flops 805306368 | bytes 5000000 | tf_op jit(solution)/shard_map/pallas_call | solution.py:51
  92.0 3.0 %collective-permute-start.4 = (bf16[96,2048]{1,0:T(8,128)(2,1)}, bf16[96,2048]{1,0:T(8,128)(2,1)S(1)}, u32[]{:S(2)}, u32[]{:S(2)}) collective-permute-start(bf16[96,2048]{1,0:T(8,128)(2,1)} %get-tuple-element.33), channel_id=1, source_target_pairs={{0,48},{16,32},{32,16},{48,0},{1,49},{17,33},{33,17},{49,1},{2,50}... | collective-permute-start | bytes 1179656 | tf_op jit(solution)/shard_map/down_over_y/ppermute | solution.py:327
  96.3 3.6 %all-to-all-start.2 = ((bf16[8,256,256]{2,1,0:T(8,128)(2,1)}), bf16[8,256,256]{2,1,0:T(8,128)(2,1)S(1)}, u32[]{:S(2)}, u32[]{:S(2)}) async-start(bf16[8,256,256]{2,1,0:T(8,128)(2,1)} %shard_map.81), calls=%async_computation.2 | async-start | bytes 2097152 | tf_op jit(solution)/shard_map/units_over_z/all_to_all | solution.py:363
  99.9 2.6 %collective-permute-done.3.refs_1_ = bf16[96,2048]{1,0:T(8,128)(2,1)} collective-permute-done((bf16[96,2048]{1,0:T(8,128)(2,1)}, bf16[96,2048]{1,0:T(8,128)(2,1)}, u32[]{:S(2)}, u32[]{:S(2)}) %collective-permute-start.3) | collective-permute-done | bytes 393248 | tf_op jit(solution)/shard_map/down_over_y/ppermute | solution.py:327
  102.5 9.5 %collective-permute-done.4.refs_3_ = bf16[96,2048]{1,0:T(8,128)(2,1)S(1)} collective-permute-done((bf16[96,2048]{1,0:T(8,128)(2,1)}, bf16[96,2048]{1,0:T(8,128)(2,1)S(1)}, u32[]{:S(2)}, u32[]{:S(2)}) %collective-permute-start.4) | collective-permute-done | bytes 393248 | tf_op jit(solution)/shard_map/down_over_y/ppermute | solution.py:327
  115.4 3.3 %collective-permute-start.5 = (bf16[384,2048]{1,0:T(8,128)(2,1)S(1)}, bf16[384,2048]{1,0:T(8,128)(2,1)S(1)}, u32[]{:S(2)}, u32[]{:S(2)}) collective-permute-start(bf16[384,2048]{1,0:T(8,128)(2,1)S(1)} %shard_map.79.own_ref), channel_id=1, source_target_pairs={{0,1},{1,0},{2,3},{3,2},{4,5},{5,4},{6,7},{7,6},{8,9},{9,8},{10,11... | collective-permute-start | bytes 4718600 | tf_op jit(solution)/shard_map/down_over_c/ppermute | solution.py:369
  118.6 3.0 %collective-permute-done.5.other_ref = bf16[384,2048]{1,0:T(8,128)(2,1)S(1)} collective-permute-done((bf16[384,2048]{1,0:T(8,128)(2,1)S(1)}, bf16[384,2048]{1,0:T(8,128)(2,1)S(1)}, u32[]{:S(2)}, u32[]{:S(2)}) %collective-permute-start.5) | collective-permute-done | bytes 1572896 | tf_op jit(solution)/shard_map/down_over_c/ppermute | solution.py:369
  122.8 4.0 %all-to-all-done.2.x_ref = bf16[8,256,256]{2,1,0:T(8,128)(2,1)S(1)} async-done(((bf16[8,256,256]{2,1,0:T(8,128)(2,1)}), bf16[8,256,256]{2,1,0:T(8,128)(2,1)S(1)}, u32[]{:S(2)}, u32[]{:S(2)}) %all-to-all-start.2) | async-done | bytes 1048608 | tf_op jit(solution)/shard_map/units_over_z/all_to_all | solution.py:363
  130.0 22.9 %all_to_all.20 = bf16[64,24,128]{2,1,0:T(8,128)(2,1)S(1)} all-to-all(bf16[64,24,128]{2,1,0:T(8,128)(2,1)S(1)} %bitcast.21), channel_id=1, replica_groups=mesh['x'=4,'yh'=2,'ya'=2,'yb'=2,'z'=8,'c'=2] {'x','yh','ya','yb','c'}, dimensions={0} | all-to-all | bytes 786432 | tf_op jit(solution)/shard_map/out_over_xyc/all_to_all | solution.py:384
  (37 shorter events, 17.2 us)
Async XLA Ops:
  1.8 24.3 %all-to-all-start = ((bf16[32,32,128]{2,1,0:T(8,128)(2,1)}), bf16[32,32,128]{2,1,0:T(8,128)(2,1)S(1)}, u32[]{:S(2)}, u32[]{:S(2)}) async-start(bf16[32,32,128]{2,1,0:T(8,128)(2,1)} %bitcast.29), calls=%async_computation | async-start | bytes 524288 | tf_op jit(solution)/shard_map/rows_over_xyc/all_to_all | solution.py:283
  16.7 46.4 %collective-permute-start = (bf16[2,2,8,192,128]{4,3,2,1,0:T(8,128)(2,1)}, bf16[2,2,8,192,128]{4,3,2,1,0:T(8,128)(2,1)}, u32[]{:S(2)}, u32[]{:S(2)}) collective-permute-start(bf16[2,2,8,192,128]{4,3,2,1,0:T(8,128)(2,1)} %shard_map.75), channel_id=1, source_target_pairs={{0,16},{16,0},{1,17},{17,1},{2,18},{18,2},{3,19},{19,3},{4,20},{20... | collective-permute-start | bytes 4718600 | tf_op jit(solution)/shard_map/gate_up_over_y/ppermute | solution.py:318
  21.9 5.9 %copy-start = (bf16[2,2,8,192,128]{4,3,2,1,0:T(8,128)(2,1)S(1)}, bf16[2,2,8,192,128]{4,3,2,1,0:T(8,128)(2,1)}, u32[]{:S(2)}) copy-start(bf16[2,2,8,192,128]{4,3,2,1,0:T(8,128)(2,1)} %shard_map.77.w_ref) | copy-start | bytes 4718596
  27.8 12.5 %copy-start.10 = (s32[6]{0:T(128)S(1)}, s32[6]{0:T(128)}, u32[]{:S(2)}) copy-start(s32[6]{0:T(128)} %stack.27.place_ref) | copy-start | bytes 76
  27.8 35.3 %collective-permute-start.2 = (bf16[2,2,8,192,128]{4,3,2,1,0:T(8,128)(2,1)S(1)}, bf16[2,2,8,192,128]{4,3,2,1,0:T(8,128)(2,1)}, u32[]{:S(2)}, u32[]{:S(2)}) collective-permute-start(bf16[2,2,8,192,128]{4,3,2,1,0:T(8,128)(2,1)S(1)} %copy-done), channel_id=1, source_target_pairs={{0,1},{1,0},{2,3},{3,2},{4,5},{5,4},{6,7},{7,6},{8,9},{9,8},{10,11... | collective-permute-start | bytes 4718600 | tf_op jit(solution)/shard_map/gate_up_over_c/ppermute | solution.py:333
  30.2 51.2 %all-to-all-start.1 = ((bf16[8,784,128]{2,1,0:T(8,128)(2,1)}), bf16[8,784,128]{2,1,0:T(8,128)(2,1)S(1)}, u32[]{:S(2)}, u32[]{:S(2)}) async-start(bf16[8,784,128]{2,1,0:T(8,128)(2,1)} %shard_map.76), calls=%async_computation.1 | async-start | bytes 3211264 | tf_op jit(solution)/shard_map/features_over_z/all_to_all | solution.py:298
  40.3 1.4 copy-start.1
  43.2 0.8 copy-start.4
  44.0 17.9 %collective-permute-start.1 = (bf16[96,2048]{1,0:T(8,128)(2,1)S(1)}, bf16[96,2048]{1,0:T(8,128)(2,1)S(1)}, u32[]{:S(2)}, u32[]{:S(2)}) collective-permute-start(bf16[96,2048]{1,0:T(8,128)(2,1)S(1)} %get-tuple-element.25), channel_id=1, source_target_pairs={{0,32},{16,48},{32,0},{48,16},{1,33},{17,49},{33,1},{49,17},{2,34}... | collective-permute-start | bytes 1179656 | tf_op jit(solution)/shard_map/down_over_y/ppermute | solution.py:327
  61.9 0.8 copy-start.6
  63.1 18.4 %collective-permute-start.6 = (bf16[2,2,8,192,128]{4,3,2,1,0:T(8,128)(2,1)}, bf16[2,2,8,192,128]{4,3,2,1,0:T(8,128)(2,1)}, u32[]{:S(2)}, u32[]{:S(2)}) collective-permute-start(bf16[2,2,8,192,128]{4,3,2,1,0:T(8,128)(2,1)} %collective-permute-done.w_ref), channel_id=1, source_target_pairs={{0,1},{1,0},{2,3},{3,2},{4,5},{5,4},{6,7},{7,6},{8,9},{9,8},{10,11... | collective-permute-start | bytes 4718600 | tf_op jit(solution)/shard_map/gate_up_over_c/ppermute | solution.py:337
  84.3 10.7 %collective-permute-start.7 = (bf16[272,512]{1,0:T(8,128)(2,1)S(1)}, bf16[272,512]{1,0:T(8,128)(2,1)S(1)}, u32[]{:S(2)}, u32[]{:S(2)}) collective-permute-start(bf16[272,512]{1,0:T(8,128)(2,1)S(1)} %shard_map.80), channel_id=1, source_target_pairs={{0,16},{16,0},{1,17},{17,1},{2,18},{18,2},{3,19},{19,3},{4,20},{20... | collective-permute-start | bytes 835592 | tf_op jit(solution)/shard_map/hidden_over_y/ppermute | solution.py:351
  86.2 16.3 %collective-permute-start.3 = (bf16[96,2048]{1,0:T(8,128)(2,1)}, bf16[96,2048]{1,0:T(8,128)(2,1)}, u32[]{:S(2)}, u32[]{:S(2)}) collective-permute-start(bf16[96,2048]{1,0:T(8,128)(2,1)} %get-tuple-element.28), channel_id=1, source_target_pairs={{0,16},{16,0},{32,48},{48,32},{1,17},{17,1},{33,49},{49,33},{2,18}... | collective-permute-start | bytes 1179656 | tf_op jit(solution)/shard_map/down_over_y/ppermute | solution.py:327
  92.0 20.0 %collective-permute-start.4 = (bf16[96,2048]{1,0:T(8,128)(2,1)}, bf16[96,2048]{1,0:T(8,128)(2,1)S(1)}, u32[]{:S(2)}, u32[]{:S(2)}) collective-permute-start(bf16[96,2048]{1,0:T(8,128)(2,1)} %get-tuple-element.33), channel_id=1, source_target_pairs={{0,48},{16,32},{32,16},{48,0},{1,49},{17,33},{33,17},{49,1},{2,50}... | collective-permute-start | bytes 1179656 | tf_op jit(solution)/shard_map/down_over_y/ppermute | solution.py:327
  95.0 17.7 %copy-start.5 = (bf16[96,2048]{1,0:T(8,128)(2,1)S(1)}, bf16[96,2048]{1,0:T(8,128)(2,1)}, u32[]{:S(2)}) copy-start(bf16[96,2048]{1,0:T(8,128)(2,1)} %copy-done.4) | copy-start | bytes 1179652
  95.0 17.7 %copy-start.7 = (bf16[96,2048]{1,0:T(8,128)(2,1)S(1)}, bf16[96,2048]{1,0:T(8,128)(2,1)}, u32[]{:S(2)}) copy-start(bf16[96,2048]{1,0:T(8,128)(2,1)} %copy-done.6) | copy-start | bytes 1179652
  96.3 30.5 %all-to-all-start.2 = ((bf16[8,256,256]{2,1,0:T(8,128)(2,1)}), bf16[8,256,256]{2,1,0:T(8,128)(2,1)S(1)}, u32[]{:S(2)}, u32[]{:S(2)}) async-start(bf16[8,256,256]{2,1,0:T(8,128)(2,1)} %shard_map.81), calls=%async_computation.2 | async-start | bytes 2097152 | tf_op jit(solution)/shard_map/units_over_z/all_to_all | solution.py:363
  112.0 0.8 copy-start.8
  112.7 1.0 copy-start.9
  113.7 39.1 %copy-start.11 = (s32[8,128]{1,0:T(8,128)S(1)}, s32[8,128]{1,0:T(8,128)}, u32[]{:S(2)}) copy-start(s32[8,128]{1,0:T(8,128)} %get-tuple-element.20.target_ref) | copy-start | bytes 12292
  113.7 39.1 %copy-start.12 = (f32[128,2]{0,1:T(2,128)S(1)}, f32[128,2]{0,1:T(2,128)}, u32[]{:S(2)}) copy-start(f32[128,2]{0,1:T(2,128)} %param.10) | copy-start | bytes 3076
  115.4 6.3 %collective-permute-start.5 = (bf16[384,2048]{1,0:T(8,128)(2,1)S(1)}, bf16[384,2048]{1,0:T(8,128)(2,1)S(1)}, u32[]{:S(2)}, u32[]{:S(2)}) collective-permute-start(bf16[384,2048]{1,0:T(8,128)(2,1)S(1)} %shard_map.79.own_ref), channel_id=1, source_target_pairs={{0,1},{1,0},{2,3},{3,2},{4,5},{5,4},{6,7},{7,6},{8,9},{9,8},{10,11... | collective-permute-start | bytes 4718600 | tf_op jit(solution)/shard_map/down_over_c/ppermute | solution.py:369
  121.7 1.2 copy-start.2
  126.8 1.4 copy-start.3
